TPU v7x, 32 devices: a whole 2x2x4 slice. The times are simulated.
32 devices in a mesh: section: 2 (over core), seq: 4 (over z), head: 4 (over y, x).
Axes of the slice: x: 2, y: 2, z: 4, core: 2. Of those that a mesh axis runs over, the one named last changes fastest.
Arguments:
- inputs: bfloat16 [2, 1024, 1792], P(None, 'seq'), may hold values from -6 to 6
- out_grad: bfloat16 [2, 1024, 1792], P(None, 'seq'), may hold values from -6 to 6
- lengths: int32 [2, 2], replicated, may hold values from 0 to 1024, as said below
- norm_attn: float32 [2, 1792], P('section'), may hold values from 0.5 to 1.5
- norm_ffn: float32 [2, 1792], P('section'), may hold values from 0.5 to 1.5
- w_query: bfloat16 [2, 1792, 256], P('section', None, 'head'), may hold values from -0.125 to 0.125
- w_key: bfloat16 [2, 1792, 256], P('section', None, 'head'), may hold values from -0.125 to 0.125
- w_value: bfloat16 [2, 1792, 1792], P('section', None, 'head'), may hold values from -0.125 to 0.125
- w_output_gate: bfloat16 [2, 1792, 1792], P('section', None, 'head'), may hold values from -0.125 to 0.125
- conv_kernel: float32 [2, 3, 1792], P('section', None, 'head'), may hold values from -3.5 to 3.5
- w_out: bfloat16 [2, 1792, 1792], P('section', 'head'), may hold values from -1 to 1
- w_gate: bfloat16 [2, 1792, 4864], P('section', None, 'head'), may hold values from -0.125 to 0.125
- w_up: bfloat16 [2, 1792, 4864], P('section', None, 'head'), may hold values from -0.125 to 0.125
- w_down: bfloat16 [2, 4864, 1792], P('section', 'head'), may hold values from -0.078125 to 0.078125
Outputs:
- section_out: bfloat16 [2, 2, 1024, 1792], P('section', None, 'seq')
- input_grad: bfloat16 [2, 2, 1024, 1792], P('section', None, 'seq')
- grad_norm_attn: float32 [2, 1792], P('section')
- grad_norm_ffn: float32 [2, 1792], P('section')
- grad_w_query: float32 [2, 1792, 256], P('section', 'seq', 'head')
- grad_w_key: float32 [2, 1792, 256], P('section', 'seq', 'head')
- grad_w_value: float32 [2, 1792, 1792], P('section', 'seq', 'head')
- grad_w_output_gate: float32 [2, 1792, 1792], P('section', 'seq', 'head')
- grad_conv_kernel: float32 [2, 3, 1792], P('section', None, 'head')
- grad_w_out: float32 [2, 1792, 1792], P('section', 'head', 'seq')
- grad_w_gate: float32 [2, 1792, 4864], P('section', 'seq', 'head')
- grad_w_up: float32 [2, 1792, 4864], P('section', 'seq', 'head')
- grad_w_down: float32 [2, 4864, 1792], P('section', 'head', 'seq')
Inputs may be any that keep to these rules, and one draw needn't show every extreme that they name: In each micro-batch the two lengths sum to 1024 or less and to 896 or more; the first is at least the smaller of 1024 and that sum; slots after both sequences are padding. In one micro-batch the first sequence fills all 1024 slots.
All inputs are finite; a program needn't handle non-finite values.
Results may differ from a plain program's by a relative error of at most 0.029.
Values may be sent and summed in bfloat16 or wider, within the bound.
A program may use at most 256 MiB of HBM per device.

v0:
```python
import jax
import jax.numpy as jnp
from jax import lax
from jax.sharding import PartitionSpec as P

HD = 112
FEAT = 16
KW = 3


epsilon = 1e-05
highest = lax.Precision.HIGHEST


def from_behind(value, axis, steps):
    count = lax.axis_size(axis)
    initial, last = (max(0, -steps), min(count, count - steps))
    return lax.ppermute(value, axis, [(source, source + steps) for source in range(initial, last)])


def carried_in(array, axis, join, neutral):
    place = lax.axis_index(axis)
    gathered = jax.tree.map(
        lambda a, kind: lax.all_gather(a.astype(kind), axis),
        array,
        (jnp.bfloat16, jnp.bfloat16, jnp.bfloat16),
    )
    state = jax.tree.map(lambda a, e: jnp.zeros_like(a) + jnp.asarray(e, a.dtype), array, neutral)

    def one(hop, state):
        return join(
            state,
            jax.tree.map(
                lambda a, own: lax.dynamic_index_in_dim(a, hop, 0, False).astype(own.dtype),
                gathered,
                array,
            ),
        )

    return lax.fori_loop(0, place, one, state)


def prefix(array, axis, combine, identity):
    size, position = (lax.axis_size(axis), lax.axis_index(axis))
    everything = jax.tree.map(
        lambda part, kind: lax.all_gather(part.astype(kind), axis),
        array,
        jax.tree.map(lambda a: jnp.bfloat16 if a.dtype == jnp.float32 else a.dtype, array),
    )
    start = jax.tree.map(
        lambda part, zero: jnp.broadcast_to(jnp.asarray(zero, part.dtype), part.shape),
        array,
        identity,
    )

    def hop(k, before):
        at = size - 1 - k
        reached = at > position
        new = combine(
            before, jax.tree.map(lambda part, own: part[at].astype(own.dtype), everything, array)
        )
        return jax.tree.map(lambda a, b: jnp.where(reached, a, b), new, before)

    return lax.fori_loop(0, size, hop, start)


def project(left_arr, right_arr):
    return jnp.dot(left_arr, right_arr, preferred_element_type=jnp.float32)


def contract_rows(left_arr, right_arr):
    return lax.dot_general(
        left_arr, right_arr, (((0,), (0,)), ((), ())), preferred_element_type=jnp.float32
    )


def contract_cols(left_arr, right_arr):
    return lax.dot_general(
        left_arr, right_arr, (((1,), (1,)), ((), ())), preferred_element_type=jnp.float32
    )


def normalize(values, gain_vec):
    inverse = lax.rsqrt(jnp.mean(values * values, axis=-1, keepdims=True) + epsilon)
    return values * inverse * gain_vec


def silu_slope(values):
    sigmoid = jax.nn.sigmoid(values)
    return sigmoid * (1.0 + values * (1.0 - sigmoid))


def segment_of(position, first_len, second_len):
    inside = (position >= first_len).astype(jnp.int32) + (
        position >= first_len + second_len
    ).astype(jnp.int32)
    return jnp.where(position >= 0, inside, -1)


def segment_start(segment, first_len, second_len):
    return jnp.where(segment <= 0, 0, jnp.where(segment == 1, first_len, first_len + second_len))


def taylor(values):
    row_count, head_count, feat_dim = values.shape
    outer_prod = (values[:, :, :, None] * values[:, :, None, :]).reshape(
        row_count, head_count, feat_dim * feat_dim
    )
    unit_col = jnp.ones((row_count, head_count, 1), jnp.float32)
    return jnp.concatenate([unit_col, values, outer_prod * 0.5**0.5], axis=2)


def attend(queries, key_rows, value_rows, state_in, norm_in, segment, applies, score_exact):
    row_count = queries.shape[0]
    if score_exact:
        scores = jnp.einsum("ihf,jhf->hij", queries, key_rows, precision=highest)
    else:
        scores = jnp.einsum("ihf,jhf->hij", queries, key_rows, preferred_element_type=jnp.float32)
    kernel = 1.0 + scores + 0.5 * scores * scores
    order_ids = jnp.arange(row_count, dtype=jnp.int32)
    allowed = (order_ids[None, :] <= order_ids[:, None]) & (segment[None, :] == segment[:, None])
    kernel = jnp.where(allowed[None], kernel, 0.0)
    numerator = jnp.einsum("hij,jhe->ihe", kernel, value_rows, precision=highest)
    denominator = jnp.sum(kernel, axis=2).T
    lifted = taylor(queries) * applies[:, None, None]
    numerator = numerator + jnp.einsum("ihf,hfe->ihe", lifted, state_in, precision=highest)
    denominator = denominator + jnp.einsum("ihf,hf->ih", lifted, norm_in, precision=highest)
    return numerator / denominator[:, :, None]


def tail_state(key_rows, value_rows, tail_mask):
    lifted = taylor(key_rows) * tail_mask[:, None, None]
    return (
        jnp.einsum("ihf,ihe->hfe", lifted, value_rows, precision=highest),
        jnp.sum(lifted, axis=0),
    )


def carry_combine(earlier_item, later_item):
    carry_keep = 1.0 - later_item[2]
    return (
        later_item[0] + carry_keep * earlier_item[0],
        later_item[1] + carry_keep * earlier_item[1],
        jnp.maximum(earlier_item[2], later_item[2]),
    )


def short_conv(extended, kernel, seg_ext, segment):
    kernel_width = kernel.shape[0]
    row_count = segment.shape[0]
    summed = jnp.zeros((row_count, extended.shape[1]), jnp.float32)
    for lag_step in range(kernel_width):
        begin_row = kernel_width - 1 - lag_step
        shifted = extended[begin_row : begin_row + row_count]
        same_doc = (seg_ext[begin_row : begin_row + row_count] == segment)[:, None]
        summed = summed + jnp.where(same_doc, shifted * kernel[lag_step][None, :], 0.0)
    return summed


def row_layout(row_count, lengths_now):
    first_pos = lax.axis_index("seq") * row_count
    positions = first_pos + jnp.arange(row_count, dtype=jnp.int32)
    first_len = lengths_now[0]
    second_len = lengths_now[1]
    segment = segment_of(positions, first_len, second_len)
    valid_rows = (positions < first_len + second_len).astype(jnp.float32)
    edge_seg = segment_of(
        first_pos - (KW - 1) + jnp.arange(KW - 1, dtype=jnp.int32), first_len, second_len
    )
    seg_ext = jnp.concatenate([edge_seg, segment])
    prior_seg = segment_of(first_pos - 1, first_len, second_len)
    applies = (segment == prior_seg).astype(jnp.float32)
    last_seg = segment[row_count - 1]
    tail_mask = (segment == last_seg).astype(jnp.float32)
    reset_flag = (
        (segment_start(last_seg, first_len, second_len) >= first_pos).astype(jnp.float32).reshape(1)
    )
    return (segment, valid_rows, seg_ext, applies, tail_mask, reset_flag)


def run_layer(layer_in, lengths_now, params):
    (
        gain_attn,
        gain_ffn,
        query_w,
        key_w,
        value_w,
        outgate_w,
        conv_w,
        mixout_w,
        gate_w,
        upward_w,
        down_w,
    ) = params
    row_count = layer_in.shape[0]
    head_count = query_w.shape[1] // FEAT
    feat_scale = FEAT ** (-0.25)
    segment, valid_rows, seg_ext, applies, tail_mask, reset_flag = row_layout(
        row_count, lengths_now
    )
    input_full = layer_in.astype(jnp.float32)
    normed_one = normalize(input_full, gain_attn).astype(jnp.bfloat16)
    query_low = project(normed_one, query_w).astype(jnp.bfloat16)
    key_low = project(normed_one, key_w).astype(jnp.bfloat16)
    value_low = project(normed_one, value_w).astype(jnp.bfloat16)
    outgate = project(normed_one, outgate_w)
    edge_rows = from_behind(value_low[row_count - (KW - 1) :], "seq", 1)
    extended = jnp.concatenate([edge_rows, value_low]).astype(jnp.float32)
    mixed_values = short_conv(extended, conv_w, seg_ext, segment)
    queries = query_low.astype(jnp.float32).reshape(row_count, head_count, FEAT) * feat_scale
    key_rows = key_low.astype(jnp.float32).reshape(row_count, head_count, FEAT) * feat_scale
    value_rows = mixed_values.reshape(row_count, head_count, HD)
    state_tail, norm_tail = tail_state(key_rows, value_rows, tail_mask)
    state_in, norm_in, reset_seen = carried_in(
        (state_tail, norm_tail, reset_flag),
        "seq",
        carry_combine,
        (jnp.zeros_like(state_tail), jnp.zeros_like(norm_tail), jnp.zeros_like(reset_flag)),
    )
    attended_heads = attend(
        queries, key_rows, value_rows, state_in, norm_in, segment, applies, False
    )
    attended = attended_heads.reshape(row_count, head_count * HD)
    gated = (attended * jax.nn.silu(outgate)).astype(jnp.bfloat16)
    mixer = lax.psum(project(gated, mixout_w).astype(jnp.bfloat16), "head").astype(jnp.float32)
    hidden_one = input_full + mixer
    normed_two = normalize(hidden_one, gain_ffn).astype(jnp.bfloat16)
    gate_pre = project(normed_two, gate_w)
    up_pre = project(normed_two, upward_w)
    activated = (jax.nn.silu(gate_pre) * up_pre).astype(jnp.bfloat16)
    feed = lax.psum(project(activated, down_w).astype(jnp.bfloat16), "head").astype(jnp.float32)
    block_out = ((hidden_one + feed) * valid_rows[:, None]).astype(jnp.bfloat16)
    saved = {
        "input_full": input_full,
        "normed_one": normed_one,
        "outgate": outgate,
        "extended": extended,
        "queries": queries,
        "key_rows": key_rows,
        "value_rows": value_rows,
        "state_in": state_in,
        "norm_in": norm_in,
        "attended": attended,
        "gated": gated,
        "hidden_one": hidden_one,
        "normed_two": normed_two,
        "gate_pre": gate_pre,
        "up_pre": up_pre,
        "activated": activated,
    }
    return (block_out, saved)


def layer_grads(saved, grad_out, lengths_now, params):
    (
        gain_attn,
        gain_ffn,
        query_w,
        key_w,
        value_w,
        outgate_w,
        conv_w,
        mixout_w,
        gate_w,
        upward_w,
        down_w,
    ) = params
    row_count = grad_out.shape[0]
    head_count = query_w.shape[1] // FEAT
    feat_scale = FEAT ** (-0.25)
    segment, valid_rows, seg_ext, applies, tail_mask, reset_flag = row_layout(
        row_count, lengths_now
    )

    def conv_here(ext_rows, conv_taps):
        return short_conv(ext_rows, conv_taps, seg_ext, segment)

    def tail_here(key_part, value_part):
        return tail_state(key_part, value_part, tail_mask)

    def attend_here(query_part, key_part, value_part, state_part, norm_part):
        return attend(
            query_part, key_part, value_part, state_part, norm_part, segment, applies, True
        )

    unused_one, norm_one_pull = jax.vjp(normalize, saved["input_full"], gain_attn)
    unused_two, conv_pull = jax.vjp(conv_here, saved["extended"], conv_w)
    unused_three, tail_pull = jax.vjp(tail_here, saved["key_rows"], saved["value_rows"])
    unused_four, attend_pull = jax.vjp(
        attend_here,
        saved["queries"],
        saved["key_rows"],
        saved["value_rows"],
        saved["state_in"],
        saved["norm_in"],
    )
    unused_five, norm_two_pull = jax.vjp(normalize, saved["hidden_one"], gain_ffn)
    grad_total = grad_out.astype(jnp.float32) * valid_rows[:, None]
    grad_low = grad_total.astype(jnp.bfloat16)
    grad_down = contract_rows(saved["activated"], grad_low)
    grad_act = contract_cols(grad_low, down_w)
    gate_pre = saved["gate_pre"]
    grad_gate_pre = (grad_act * saved["up_pre"] * silu_slope(gate_pre)).astype(jnp.bfloat16)
    grad_up_pre = (grad_act * jax.nn.silu(gate_pre)).astype(jnp.bfloat16)
    grad_gate = contract_rows(saved["normed_two"], grad_gate_pre)
    grad_upward = contract_rows(saved["normed_two"], grad_up_pre)
    partial_two = contract_cols(grad_gate_pre, gate_w) + contract_cols(grad_up_pre, upward_w)
    grad_normed_two = lax.psum(partial_two.astype(jnp.bfloat16), "head").astype(jnp.float32)
    grad_hidden_norm, grad_gain_ffn = norm_two_pull(grad_normed_two)
    grad_hidden = grad_total + grad_hidden_norm
    grad_mix_low = grad_hidden.astype(jnp.bfloat16)
    grad_mixout = contract_rows(saved["gated"], grad_mix_low)
    grad_gated = contract_cols(grad_mix_low, mixout_w)
    outgate = saved["outgate"]
    grad_attended = grad_gated * jax.nn.silu(outgate)
    grad_outgate_pre = (grad_gated * saved["attended"] * silu_slope(outgate)).astype(jnp.bfloat16)
    grad_queries, grad_keys, grad_values, grad_state_in, grad_norm_in = attend_pull(
        grad_attended.reshape(row_count, head_count, HD)
    )
    grad_state_tail, grad_norm_tail, reset_seen = prefix(
        (grad_state_in, grad_norm_in, reset_flag),
        "seq",
        carry_combine,
        (jnp.zeros_like(grad_state_in), jnp.zeros_like(grad_norm_in), jnp.zeros_like(reset_flag)),
    )
    extra_keys, extra_values = tail_pull((grad_state_tail, grad_norm_tail))
    grad_query_low = (
        (grad_queries * feat_scale).reshape(row_count, head_count * FEAT).astype(jnp.bfloat16)
    )
    grad_key_low = (
        ((grad_keys + extra_keys) * feat_scale)
        .reshape(row_count, head_count * FEAT)
        .astype(jnp.bfloat16)
    )
    grad_mixed = (grad_values + extra_values).reshape(row_count, head_count * HD)
    grad_extended, grad_conv = conv_pull(grad_mixed)
    edge_grads = from_behind(grad_extended[: KW - 1], "seq", -1)
    own_grads = grad_extended[KW - 1 :]
    grad_value_low = jnp.concatenate(
        [own_grads[: row_count - (KW - 1)], own_grads[row_count - (KW - 1) :] + edge_grads]
    ).astype(jnp.bfloat16)
    normed_one = saved["normed_one"]
    grad_query = contract_rows(normed_one, grad_query_low)
    grad_key = contract_rows(normed_one, grad_key_low)
    grad_value = contract_rows(normed_one, grad_value_low)
    grad_outgate = contract_rows(normed_one, grad_outgate_pre)
    partial_one = (
        contract_cols(grad_query_low, query_w)
        + contract_cols(grad_key_low, key_w)
        + contract_cols(grad_value_low, value_w)
        + contract_cols(grad_outgate_pre, outgate_w)
    )
    grad_normed_one = lax.psum(partial_one.astype(jnp.bfloat16), "head").astype(jnp.float32)
    grad_input_norm, grad_gain_attn = norm_one_pull(grad_normed_one)
    grad_input = (grad_hidden + grad_input_norm).astype(jnp.bfloat16)
    grads = (
        grad_gain_attn,
        grad_gain_ffn,
        grad_query,
        grad_key,
        grad_value,
        grad_outgate,
        grad_conv,
        grad_mixout,
        grad_gate,
        grad_upward,
        grad_down,
    )
    return (grad_input, tuple((grad_item[None] for grad_item in grads)))


def reduce_grads(grads):
    (
        grad_gain_attn,
        grad_gain_ffn,
        grad_query,
        grad_key,
        grad_value,
        grad_outgate,
        grad_conv,
        grad_mixout,
        grad_gate,
        grad_upward,
        grad_down,
    ) = grads
    small_sums = lax.psum((grad_gain_attn, grad_gain_ffn, grad_conv), "seq")
    row_parts = (
        lax.psum_scatter(
            grad_query.astype(jnp.bfloat16), "seq", scatter_dimension=1, tiled=True
        ).astype(jnp.float32),
        lax.psum_scatter(
            grad_key.astype(jnp.bfloat16), "seq", scatter_dimension=1, tiled=True
        ).astype(jnp.float32),
        lax.psum_scatter(
            grad_value.astype(jnp.bfloat16), "seq", scatter_dimension=1, tiled=True
        ).astype(jnp.float32),
        lax.psum_scatter(
            grad_outgate.astype(jnp.bfloat16), "seq", scatter_dimension=1, tiled=True
        ).astype(jnp.float32),
        lax.psum_scatter(
            grad_gate.astype(jnp.bfloat16), "seq", scatter_dimension=1, tiled=True
        ).astype(jnp.float32),
        lax.psum_scatter(
            grad_upward.astype(jnp.bfloat16), "seq", scatter_dimension=1, tiled=True
        ).astype(jnp.float32),
    )
    col_parts = (
        lax.psum_scatter(
            grad_mixout.astype(jnp.bfloat16), "seq", scatter_dimension=2, tiled=True
        ).astype(jnp.float32),
        lax.psum_scatter(
            grad_down.astype(jnp.bfloat16), "seq", scatter_dimension=2, tiled=True
        ).astype(jnp.float32),
    )
    return (
        small_sums[0],
        small_sums[1],
        row_parts[0],
        row_parts[1],
        row_parts[2],
        row_parts[3],
        small_sums[2],
        col_parts[0],
        row_parts[4],
        row_parts[5],
        col_parts[1],
    )


def shards(
    inputs,
    out_grad,
    lengths,
    norm_attn,
    norm_ffn,
    w_query,
    w_key,
    w_value,
    w_output_gate,
    conv_kernel,
    w_out,
    w_gate,
    w_up,
    w_down,
):
    params = (
        norm_attn[0],
        norm_ffn[0],
        w_query[0],
        w_key[0],
        w_value[0],
        w_output_gate[0],
        conv_kernel[0],
        w_out[0],
        w_gate[0],
        w_up[0],
        w_down[0],
    )
    section_index = lax.axis_index("section")
    section_count = lax.axis_size("section")
    micro_count = inputs.shape[0]
    tick_count = micro_count + section_count - 1
    received = jnp.zeros(inputs.shape[1:], jnp.bfloat16)
    section_rows = jnp.zeros_like(inputs)
    saved_inputs = jnp.zeros_like(inputs)
    for tick_number in range(tick_count):
        micro_index = tick_number - section_index
        is_valid = (micro_index >= 0) & (micro_index < micro_count)
        clipped = jnp.clip(micro_index, 0, micro_count - 1)
        own_input = lax.dynamic_index_in_dim(inputs, clipped, 0, keepdims=False)
        layer_in = jnp.where(section_index == 0, own_input, received)
        lengths_now = lax.dynamic_index_in_dim(lengths, clipped, 0, keepdims=False)
        block_out, saved = run_layer(layer_in, lengths_now, params)
        section_rows = jnp.where(
            is_valid,
            lax.dynamic_update_index_in_dim(section_rows, block_out, clipped, 0),
            section_rows,
        )
        saved_inputs = jnp.where(
            is_valid,
            lax.dynamic_update_index_in_dim(saved_inputs, layer_in, clipped, 0),
            saved_inputs,
        )
        received = from_behind(block_out, "section", 1)
    grad_received = jnp.zeros(inputs.shape[1:], jnp.bfloat16)
    grad_inputs = jnp.zeros_like(inputs)
    totals = tuple((jnp.zeros((1,) + weight_item.shape, jnp.float32) for weight_item in params))
    reduced = None
    for tick_number in range(tick_count):
        micro_index = tick_number - (section_count - 1 - section_index)
        is_valid = (micro_index >= 0) & (micro_index < micro_count)
        clipped = jnp.clip(micro_index, 0, micro_count - 1)
        own_grad = lax.dynamic_index_in_dim(out_grad, clipped, 0, keepdims=False)
        grad_here = jnp.where(section_index == section_count - 1, own_grad, grad_received)
        lengths_now = lax.dynamic_index_in_dim(lengths, clipped, 0, keepdims=False)
        layer_in = lax.dynamic_index_in_dim(saved_inputs, clipped, 0, keepdims=False)
        block_again, saved = run_layer(layer_in, lengths_now, params)
        grad_input, grads = layer_grads(saved, grad_here, lengths_now, params)
        weight_flag = is_valid.astype(jnp.float32)
        grads = tuple((weight_flag * grad_item for grad_item in grads))
        grad_inputs = jnp.where(
            is_valid,
            lax.dynamic_update_index_in_dim(grad_inputs, grad_input, clipped, 0),
            grad_inputs,
        )
        totals = tuple((first_val + second_val for first_val, second_val in zip(totals, grads)))
        grad_received = from_behind(grad_input, "section", -1)
    reduced = reduce_grads(totals)
    return (section_rows[None], grad_inputs[None]) + reduced


def solution(mesh):
    return jax.shard_map(
        shards,
        mesh=mesh,
        in_specs=(
            P(None, "seq", None),
            P(None, "seq", None),
            P(),
            P("section", None),
            P("section", None),
            P("section", None, "head"),
            P("section", None, "head"),
            P("section", None, "head"),
            P("section", None, "head"),
            P("section", None, "head"),
            P("section", "head", None),
            P("section", None, "head"),
            P("section", None, "head"),
            P("section", "head", None),
        ),
        out_specs=(
            P("section", None, "seq", None),
            P("section", None, "seq", None),
            P("section", None),
            P("section", None),
            P("section", "seq", "head"),
            P("section", "seq", "head"),
            P("section", "seq", "head"),
            P("section", "seq", "head"),
            P("section", None, "head"),
            P("section", "head", "seq"),
            P("section", "seq", "head"),
            P("section", "seq", "head"),
            P("section", "head", "seq"),
        ),
        check_vma=False,
    )
```

profile of v0, /device:TPU:0, one launch (start us, length us, event | category | flops | bytes accessed | tf_op | source)
XLA Modules:
  0.0 1879.2 jit_solution(15633997423877292674)
XLA Ops:
  97.6 19.2 %all-gather = bf16[16,273,112]{2,1,0:T(8,128)(2,1)S(1)} all-gather(bf16[4,273,112]{2,1,0:T(8,128)(2,1)S(1)} %convolution_convert_fusion.14), channel_id=2, replica_groups=mesh['section'=2,'seq'=4,'head'=4] {'seq'}, dimensions={0}, use_global_device_ids=true | all-gather | bytes 1223040 | tf_op jit(solution)/shard_map/all_gather | solution.py:24
  124.4 56.5 %all-reduce.41.cloned.1.call-done = bf16[256,1792]{1,0:T(8,128)(2,1)} async-done(((bf16[256,1792]{1,0:T(8,128)(2,1)}), bf16[256,1792]{1,0:T(8,128)(2,1)}) %all-reduce.41.cloned.1.call-update) | async-done | bytes 917520 | tf_op jit(solution)/shard_map/psum | solution.py:225
  198.0 50.0 %all-reduce.43.cloned.1.call-done = bf16[256,1792]{1,0:T(8,128)(2,1)} async-done(((bf16[256,1792]{1,0:T(8,128)(2,1)}), bf16[256,1792]{1,0:T(8,128)(2,1)}) %all-reduce.43.cloned.1.call-update) | async-done | bytes 917520 | tf_op jit(solution)/shard_map/psum | solution.py:231
  267.0 13.7 all-gather.19
  282.7 21.8 %all-gather.2 = bf16[16,273,112]{2,1,0:T(8,128)(2,1)} all-gather(bf16[4,273,112]{2,1,0:T(8,128)(2,1)S(1)} %convolution_convert_fusion.13), channel_id=4, replica_groups=mesh['section'=2,'seq'=4,'head'=4] {'seq'}, dimensions={0}, use_global_device_ids=true | all-gather | bytes 1223040 | tf_op jit(solution)/shard_map/all_gather | solution.py:24
  314.8 62.9 %all-reduce.45.cloned.1.call-done = bf16[256,1792]{1,0:T(8,128)(2,1)} async-done(((bf16[256,1792]{1,0:T(8,128)(2,1)}), bf16[256,1792]{1,0:T(8,128)(2,1)}) %all-reduce.45.cloned.1.call-update) | async-done | bytes 917520 | tf_op jit(solution)/shard_map/psum | solution.py:225
  399.0 46.3 %all-reduce.47.cloned.1.call-done = bf16[256,1792]{1,0:T(8,128)(2,1)} async-done(((bf16[256,1792]{1,0:T(8,128)(2,1)}), bf16[256,1792]{1,0:T(8,128)(2,1)}) %all-reduce.47.cloned.1.call-update) | async-done | bytes 917520 | tf_op jit(solution)/shard_map/psum | solution.py:231
  485.9 21.3 %all-gather.6 = bf16[16,273,112]{2,1,0:T(8,128)(2,1)} all-gather(bf16[4,273,112]{2,1,0:T(8,128)(2,1)S(1)} %convolution_convert_fusion.11), channel_id=8, replica_groups=mesh['section'=2,'seq'=4,'head'=4] {'seq'}, dimensions={0}, use_global_device_ids=true | all-gather | bytes 1223040 | tf_op jit(solution)/shard_map/all_gather | solution.py:24
  524.6 59.1 %all-reduce.49.cloned.1.call-done = bf16[256,1792]{1,0:T(8,128)(2,1)} async-done(((bf16[256,1792]{1,0:T(8,128)(2,1)}), bf16[256,1792]{1,0:T(8,128)(2,1)}) %all-reduce.49.cloned.1.call-update) | async-done | bytes 917520 | tf_op jit(solution)/shard_map/psum | solution.py:225
  604.5 13.8 all-gather.25
  630.2 13.8 all-gather.23
  647.3 20.1 %all-gather.14 = bf16[16,273,112]{2,1,0:T(8,128)(2,1)} all-gather(bf16[4,273,112]{2,1,0:T(8,128)(2,1)S(1)} %convolution_convert_fusion.7), channel_id=16, replica_groups=mesh['section'=2,'seq'=4,'head'=4] {'seq'}, dimensions={0}, use_global_device_ids=true | all-gather | bytes 1223040 | tf_op jit(solution)/shard_map/all_gather | solution.py:24
  680.1 30.0 %all-gather.10 = bf16[16,273,112]{2,1,0:T(8,128)(2,1)} all-gather(bf16[4,273,112]{2,1,0:T(8,128)(2,1)S(1)} %convolution_convert_fusion.9), channel_id=12, replica_groups=mesh['section'=2,'seq'=4,'head'=4] {'seq'}, dimensions={0}, use_global_device_ids=true | all-gather | bytes 1223040 | tf_op jit(solution)/shard_map/all_gather | solution.py:24
  740.6 75.7 %all-reduce.61.cloned.1.call-done = (bf16[256,1792]{1,0:T(8,128)(2,1)}, bf16[256,1792]{1,0:T(8,128)(2,1)}, bf16[256,1792]{1,0:T(8,128)(2,1)}) async-done(((bf16[256,1792]{1,0:T(8,128)(2,1)}, bf16[256,1792]{1,0:T(8,128)(2,1)}, bf16[256,1792]{1,0:T(8,128)(2,1)}), (bf16[256,1792]{1,0:T(8,128)(2,1)}, bf16[256,1792]{1,0:T(8,128)(2,1)}, bf16[256,1792]{1,0:T(8,128)(2,1)})) %all-reduce.61.cloned.1.call-update) | async-done | bytes 2752528 | tf_op jit(solution)/shard_map/psum | solution.py:308
  850.1 22.3 %all-gather.8 = bf16[16,273,112]{2,1,0:T(8,128)(2,1)} all-gather(bf16[4,273,112]{2,1,0:T(8,128)(2,1)S(1)} %convolution_convert_fusion.10), channel_id=10, replica_groups=mesh['section'=2,'seq'=4,'head'=4] {'seq'}, dimensions={0}, use_global_device_ids=true | all-gather | bytes 1223040 | tf_op jit(solution)/shard_map/all_gather | solution.py:46
  872.4 18.2 while.144
  911.1 13.8 all-gather.20
  931.2 28.2 %all-reduce.51.cloned.1.call-done = bf16[256,1792]{1,0:T(8,128)(2,1)} async-done(((bf16[256,1792]{1,0:T(8,128)(2,1)}), bf16[256,1792]{1,0:T(8,128)(2,1)}) %all-reduce.51.cloned.1.call-update) | async-done | bytes 917520 | tf_op jit(solution)/shard_map/psum | solution.py:353
  964.6 24.1 %all-gather.4 = bf16[16,273,112]{2,1,0:T(8,128)(2,1)} all-gather(bf16[4,273,112]{2,1,0:T(8,128)(2,1)S(1)} %copy-done.175), channel_id=6, replica_groups=mesh['section'=2,'seq'=4,'head'=4] {'seq'}, dimensions={0}, use_global_device_ids=true | all-gather | bytes 1223040 | tf_op jit(solution)/shard_map/all_gather | solution.py:24
  1004.9 47.2 %all-reduce.53.cloned.1.call-done = bf16[256,1792]{1,0:T(8,128)(2,1)} async-done(((bf16[256,1792]{1,0:T(8,128)(2,1)}), bf16[256,1792]{1,0:T(8,128)(2,1)}) %all-reduce.53.cloned.1.call-update) | async-done | bytes 917520 | tf_op jit(solution)/shard_map/psum | solution.py:308
  1082.4 23.0 %all-gather.12 = bf16[16,273,112]{2,1,0:T(8,128)(2,1)} all-gather(bf16[4,273,112]{2,1,0:T(8,128)(2,1)S(1)} %convolution_convert_fusion.8), channel_id=14, replica_groups=mesh['section'=2,'seq'=4,'head'=4] {'seq'}, dimensions={0}, use_global_device_ids=true | all-gather | bytes 1223040 | tf_op jit(solution)/shard_map/all_gather | solution.py:46
  1105.4 21.1 %while.145 = (s32[]{:T(128)}, f32[4,273,112]{2,1,0:T(8,128)}, f32[4,273]{1,0:T(4,128)S(1)}, s32[]{:T(128)}, bf16[4,4,273,112]{3,2,1,0:T(8,128)(2,1)}, /*index=5*...) while((s32[]{:T(128)}, f32[4,273,112]{2,1,0:T(8,128)}, ...), condition=%wide.region_57.58_spmd.clone, body=%wide.region_56.57_spmd.clone.sunk | while | flops 616989 | bytes 1234163 | solution.py:64
  1150.1 44.0 %all-reduce.55.cloned.1.call-done = bf16[256,1792]{1,0:T(8,128)(2,1)} async-done(((bf16[256,1792]{1,0:T(8,128)(2,1)}), bf16[256,1792]{1,0:T(8,128)(2,1)}) %all-reduce.55.cloned.1.call-update) | async-done | bytes 917520 | tf_op jit(solution)/shard_map/psum | solution.py:353
  1223.9 58.2 %all-reduce.59.cloned.1.call-done = (bf16[256,1792]{1,0:T(8,128)(2,1)}, bf16[256,1792]{1,0:T(8,128)(2,1)}) async-done(((bf16[256,1792]{1,0:T(8,128)(2,1)}, bf16[256,1792]{1,0:T(8,128)(2,1)}), (bf16[256,1792]{1,0:T(8,128)(2,1)}, bf16[256,1792]{1,0:T(8,128)(2,1)})) %all-reduce.59.cloned.1.call-update) | async-done | bytes 1835024 | tf_op jit(solution)/shard_map/psum | solution.py:308
  1310.7 23.1 %all-gather.16 = bf16[16,273,112]{2,1,0:T(8,128)(2,1)} all-gather(bf16[4,273,112]{2,1,0:T(8,128)(2,1)S(1)} %convolution_convert_fusion.6), channel_id=18, replica_groups=mesh['section'=2,'seq'=4,'head'=4] {'seq'}, dimensions={0}, use_global_device_ids=true | all-gather | bytes 1223040 | tf_op jit(solution)/shard_map/all_gather | solution.py:46
  1461.2 19.0 %copy.132 = bf16[1,1216,1792]{1,0,2:T(2,128)(2,1)} copy(bf16[1,1216,1792]{2,1,0:T(8,128)(2,1)} %fusion.17) | data formatting | bytes 8716288
  1494.4 18.9 %copy.130 = bf16[1,1792,1216]{2,0,1:T(2,128)(2,1)} copy(bf16[1,1792,1216]{1,2,0:T(8,128)(2,1)} %fusion.15) | data formatting | bytes 8716288
  1527.6 19.0 %copy.128 = bf16[1,1792,1216]{2,0,1:T(2,128)(2,1)} copy(bf16[1,1792,1216]{1,2,0:T(8,128)(2,1)} %fusion.16) | data formatting | bytes 8716288
  1563.3 21.0 %all-reduce.24 = (f32[1,1792]{1,0:T(1,128)}, f32[1,1792]{1,0:T(1,128)}, f32[1,3,448]{2,0,1:T(1,128)}) all-reduce(f32[1,1792]{1,0:T(1,128)S(1)} %add.1516, f32[1,1792]{1,0:T(1,128)S(1)} %add.1519, f32[1,3,448]{2,0,1:T(1,128)S(1)} %add.1530), channel_id=1, replica_groups=mesh['section'=2,'seq'=4,'head'=4] {'seq'}, use_global_device_ids=true, to_apply=%region_84.85 | all-reduce | flops 4928 | bytes 39424 | tf_op jit(solution)/shard_map/psum | solution.py:386
  1608.6 80.9 %reduce-scatter.39.cloned.1.call-done = bf16[448,1216]{1,0:T(8,128)(2,1)} async-done(((bf16[1792,1216]{1,0:T(8,128)(2,1)}), bf16[448,1216]{1,0:T(8,128)(2,1)}) %reduce-scatter.39.cloned.1.call-update) | async-done | bytes 1089552
  1698.6 76.8 %reduce-scatter.37.cloned.1.call-done = bf16[448,1216]{1,0:T(8,128)(2,1)} async-done(((bf16[1792,1216]{1,0:T(8,128)(2,1)}), bf16[448,1216]{1,0:T(8,128)(2,1)}) %reduce-scatter.37.cloned.1.call-update) | async-done | bytes 1089552
  1784.4 77.0 %reduce-scatter.35.cloned.1.call-done = bf16[448,1216]{1,0:T(8,128)(2,1)} async-done(((bf16[1792,1216]{1,0:T(8,128)(2,1)}), bf16[448,1216]{1,0:T(8,128)(2,1)}) %reduce-scatter.35.cloned.1.call-update) | async-done | bytes 1089552
  (1320 shorter events, 748.4 us)
Async XLA Ops:
  7.2 173.7 %all-reduce.41.cloned.1.call-start = ((), (), s32[]{:S(2)}) async-start(), calls=%async_computation.8 | async-start | bytes 1835008 | tf_op jit(solution)/shard_map/psum | solution.py:225
  13.6 80.9 %collective-permute-start = (bf16[2,448]{0,1:T(8,128)(2,1)}, bf16[2,448]{0,1:T(8,128)(2,1)}, u32[]{:S(2)}, u32[]{:S(2)}) collective-permute-start(bf16[2,448]{0,1:T(8,128)(2,1)} %slice.339), channel_id=1, source_target_pairs={{0,4},{4,8},{8,12},{1,5},{5,9},{9,13},{2,6},{6,10},{10,14},{3,7},{... | collective-permute-start | bytes 5384 | tf_op jit(solution)/shard_map/ppermute | solution.py:18
  124.1 123.9 %all-reduce.43.cloned.1.call-start = ((), (), s32[]{:S(2)}) async-start(), calls=%async_computation.9 | async-start | bytes 1835008 | tf_op jit(solution)/shard_map/psum | solution.py:231
  197.3 180.4 %all-reduce.45.cloned.1.call-start = ((), (), s32[]{:S(2)}) async-start(), calls=%async_computation.10 | async-start | bytes 1835008 | tf_op jit(solution)/shard_map/psum | solution.py:225
  251.7 4.4 collective-permute-start.1
  260.0 20.7 %collective-permute-start.2 = (bf16[2,448]{0,1:T(8,128)(2,1)S(1)}, bf16[2,448]{0,1:T(8,128)(2,1)S(1)}, u32[]{:S(2)}, u32[]{:S(2)}) collective-permute-start(bf16[2,448]{0,1:T(8,128)(2,1)S(1)} %slice.343), channel_id=1, source_target_pairs={{0,4},{4,8},{8,12},{1,5},{5,9},{9,13},{2,6},{6,10},{10,14},{3,7},{... | collective-permute-start | bytes 5384 | tf_op jit(solution)/shard_map/ppermute | solution.py:18
  312.7 132.6 %all-reduce.47.cloned.1.call-start = ((), (), s32[]{:S(2)}) async-start(), calls=%async_computation.11 | async-start | bytes 1835008 | tf_op jit(solution)/shard_map/psum | solution.py:231
  394.6 189.1 %all-reduce.49.cloned.1.call-start = ((), (), s32[]{:S(2)}) async-start(), calls=%async_computation.12 | async-start | bytes 1835008 | tf_op jit(solution)/shard_map/psum | solution.py:225
  449.1 9.4 collective-permute-start.3
  464.3 19.6 %collective-permute-start.5 = (bf16[2,448]{0,1:T(8,128)(2,1)S(1)}, bf16[2,448]{0,1:T(8,128)(2,1)S(1)}, u32[]{:S(2)}, u32[]{:S(2)}) collective-permute-start(bf16[2,448]{0,1:T(8,128)(2,1)S(1)} %slice.351), channel_id=1, source_target_pairs={{0,4},{4,8},{8,12},{1,5},{5,9},{9,13},{2,6},{6,10},{10,14},{3,7},{... | collective-permute-start | bytes 5384 | tf_op jit(solution)/shard_map/ppermute | solution.py:18
  519.3 297.1 %all-reduce.61.cloned.1.call-start = ((), (), s32[]{:S(2)}) async-start(), calls=%async_computation.26 | async-start | bytes 5505024 | tf_op jit(solution)/shard_map/psum | solution.py:308
  595.9 48.1 %collective-permute-start.8 = (bf16[2,448]{0,1:T(8,128)(2,1)S(1)}, bf16[2,448]{0,1:T(8,128)(2,1)S(1)}, u32[]{:S(2)}, u32[]{:S(2)}) collective-permute-start(bf16[2,448]{0,1:T(8,128)(2,1)S(1)} %slice.358), channel_id=1, source_target_pairs={{0,4},{4,8},{8,12},{1,5},{5,9},{9,13},{2,6},{6,10},{10,14},{3,7},{... | collective-permute-start | bytes 5384 | tf_op jit(solution)/shard_map/ppermute | solution.py:18
  599.4 44.8 %collective-permute-start.11 = (bf16[2,448]{0,1:T(8,128)(2,1)S(1)}, bf16[2,448]{0,1:T(8,128)(2,1)S(1)}, u32[]{:S(2)}, u32[]{:S(2)}) collective-permute-start(bf16[2,448]{0,1:T(8,128)(2,1)S(1)} %slice.365), channel_id=1, source_target_pairs={{0,4},{4,8},{8,12},{1,5},{5,9},{9,13},{2,6},{6,10},{10,14},{3,7},{... | collective-permute-start | bytes 5384 | tf_op jit(solution)/shard_map/ppermute | solution.py:18
  722.3 237.1 %all-reduce.51.cloned.1.call-start = ((), (), s32[]{:S(2)}) async-start(), calls=%async_computation.13 | async-start | bytes 1835008 | tf_op jit(solution)/shard_map/psum | solution.py:353
  727.0 12.0 collective-permute-start.4
  896.7 8.2 collective-permute-start.6
  908.9 143.2 %all-reduce.53.cloned.1.call-start = ((), (), s32[]{:S(2)}) async-start(), calls=%async_computation.14 | async-start | bytes 1835008 | tf_op jit(solution)/shard_map/psum | solution.py:308
  963.0 30.9 %collective-permute-start.7 = (bf16[256,1792]{1,0:T(8,128)(2,1)S(1)}, bf16[256,1792]{1,0:T(8,128)(2,1)S(1)}, u32[]{:S(2)}, u32[]{:S(2)}) collective-permute-start(bf16[256,1792]{1,0:T(8,128)(2,1)S(1)} %get-tuple-element.1200), channel_id=1, source_target_pairs={{16,0},{17,1},{18,2},{19,3},{20,4},{21,5},{22,6},{23,7},{24,8},{25... | collective-permute-start | bytes 2752520 | tf_op jit(solution)/shard_map/ppermute | solution.py:18
  1001.1 193.0 %all-reduce.55.cloned.1.call-start = ((), (), s32[]{:S(2)}) async-start(), calls=%async_computation.15 | async-start | bytes 1835008 | tf_op jit(solution)/shard_map/psum | solution.py:353
  1131.5 8.2 collective-permute-start.9
  1143.6 138.5 %all-reduce.59.cloned.1.call-start = ((), (), s32[]{:S(2)}) async-start(), calls=%async_computation.25 | async-start | bytes 3670016 | tf_op jit(solution)/shard_map/psum | solution.py:308
  1200.2 8.2 collective-permute-start.10
  1215.7 342.0 %reduce-scatter.27.cloned.1.call-start = ((), (), s32[]{:S(2)}) async-start(), calls=%async_computation.17 | async-start | bytes 573440
  1352.2 39.1 %collective-permute-start.12 = (f32[2,448]{0,1:T(8,128)}, f32[2,448]{0,1:T(8,128)}, u32[]{:S(2)}, u32[]{:S(2)}) collective-permute-start(f32[2,448]{0,1:T(8,128)} %slice.371), channel_id=1, source_target_pairs={{4,0},{8,4},{12,8},{5,1},{9,5},{13,9},{6,2},{10,6},{14,10},{7,3},{... | collective-permute-start | bytes 10760 | tf_op jit(solution)/shard_map/ppermute | solution.py:18
  1359.3 200.2 %reduce-scatter.25.cloned.1.call-start = ((), (), s32[]{:S(2)}) async-start(), calls=%async_computation.16 | async-start | bytes 573440
  1391.3 170.0 %all-reduce.57.cloned.1.call-start = ((), (), s32[]{:S(2)}) async-start(), calls=%async_computation.24 | async-start | bytes 3670016 | tf_op jit(solution)/shard_map/psum | solution.py:231
  1397.0 192.5 %reduce-scatter.33.cloned.1.call-start = ((), (), s32[]{:S(2)}) async-start(), calls=%async_computation.20 | async-start | bytes 2293760
  1416.3 177.0 %reduce-scatter.31.cloned.1.call-start = ((), (), s32[]{:S(2)}) async-start(), calls=%async_computation.19 | async-start | bytes 2293760
  1433.5 171.2 %reduce-scatter.29.cloned.1.call-start = ((), (), s32[]{:S(2)}) async-start(), calls=%async_computation.18 | async-start | bytes 2293760
  1451.0 238.5 %reduce-scatter.39.cloned.1.call-start = ((), (), s32[]{:S(2)}) async-start(), calls=%async_computation.23 | async-start | bytes 5734400
  1486.7 288.7 %reduce-scatter.37.cloned.1.call-start = ((), (), s32[]{:S(2)}) async-start(), calls=%async_computation.22 | async-start | bytes 5734400
  1520.0 341.4 %reduce-scatter.35.cloned.1.call-start = ((), (), s32[]{:S(2)}) async-start(), calls=%async_computation.21 | async-start | bytes 5734400
  (395 other events, 4317.0 us)
Sparse Core Ops, SparseCore 0:
  124.2 56.6 all-reduce.40
  197.4 50.5 all-reduce.42
  312.8 64.8 all-reduce.44
  394.7 50.5 all-reduce.46
  519.4 64.2 all-reduce.48
  722.4 93.8 all-reduce.60
  909.0 50.3 all-reduce.50
  1001.2 50.8 all-reduce.52
  1143.8 50.2 all-reduce.54
  1215.8 66.2 all-reduce.58
  1359.4 21.3 reduce-scatter.26
  1391.4 21.3 reduce-scatter.24
  1416.8 63.8 all-reduce.56
  1482.8 39.4 reduce-scatter.32
  1524.4 38.5 reduce-scatter.30
  1565.8 38.8 reduce-scatter.28
  1606.9 82.6 reduce-scatter.38
  1691.7 83.6 reduce-scatter.36
  1777.7 83.6 reduce-scatter.34
where the time goes:
time: 1900 us; the launch traced here: 1880 us
  waiting for transfers between devices  771 us (41%)
  blocking collectives  358 us (19%)
  matrix products  288 us (15%)
  local copies, waits for them, and re-layouts  217 us (11%)
  other arithmetic  162 us (9%)
  between operations  43 us (2%)
  starting transfers between devices  40.3 us (2%)
    unnamed x27, waiting for transfers between devices  243 us
    all_gather x12, blocking collectives, carried_in(): lax.all_gather(a.astype(kind), axis)  218 us
    unnamed x842, local copies, waits for them, and re-layouts  202 us
    psum x3, waiting for transfers between devices, layer_grads(): lax.psum(partial_two.astype(jnp.bfloat16), 'head').astype(jnp.float32)  181 us
    psum x3, waiting for transfers between devices, run_layer(): lax.psum(project(gated, mixout_w).astype(jnp.bfloat16), 'head')  179 us
    all_gather x6, blocking collectives, prefix(): lax.all_gather(part.astype(kind), axis)  109 us
    psum x3, waiting for transfers between devices, run_layer(): lax.psum(project(activated, down_w).astype(jnp.bfloat16), 'head')  96.3 us
    dot_general x42, matrix products, project(): return jnp.dot(left_arr, right_arr, preferred_element_type=jnp.float32)  95 us
  transfers between devices with their start and end apart: 32, of which 14 were waited for; matrix products, arithmetic and copies ran while one was open for 19% of the time, Pallas kernels for 0%

commit v1 on v0

v1 whole, which is shorter than its diff:
```python
import functools

import jax
import jax.numpy as jnp
import numpy as np
from jax import lax
from jax.experimental import pallas as pl
from jax.experimental.pallas import tpu as pltpu
from jax.sharding import PartitionSpec as P

HD = 112
FEAT = 16
KW = 3
EPS = 1e-05
LANES = 128
PSI = 256
PSI_SENT = 160
MESH = pl.DeviceIdType.MESH
F32 = jnp.float32
BF16 = jnp.bfloat16
VMEM_LIMIT = 60 << 20


def dot_nn(a, b):
    return lax.dot_general(a, b, (((1,), (0,)), ((), ())), preferred_element_type=F32)


def dot_nt(a, b):
    return lax.dot_general(a, b, (((1,), (1,)), ((), ())), preferred_element_type=F32)


def dot_tn(a, b):
    return lax.dot_general(a, b, (((0,), (0,)), ((), ())), preferred_element_type=F32)


def chunks(total, step, body):
    whole = total // step
    if whole > 1:

        def one(i, carry):
            body(pl.multiple_of(i * step, step), step)
            return carry

        lax.fori_loop(0, whole, one, 0)
    elif whole == 1:
        body(0, step)
    if total % step:
        body(whole * step, total % step)


def lift_tables(heads):
    first = np.zeros((heads * FEAT, heads * PSI), np.float32)
    second = np.zeros_like(first)
    second_key = np.zeros_like(first)
    for head in range(heads):
        row, col = head * FEAT, head * PSI
        for i in range(FEAT):
            first[row + i, col + 1 + i] = 1.0
        at = 1 + FEAT
        for i in range(FEAT):
            for j in range(i, FEAT):
                first[row + i, col + at] = 1.0
                second[row + j, col + at] = 1.0
                second_key[row + j, col + at] = 0.5 if i == j else 1.0
                at += 1
    return np.stack([first, second, second_key])


class Place:
    def __init__(self, lens, nz, nh, rows):
        self.sec, self.s, self.h = (lax.axis_index(a) for a in ("section", "seq", "head"))
        self.nz, self.nh, self.rows = nz, nh, rows
        self.l0 = lens[self.sec, 0]
        self.tot = self.l0 + lens[self.sec, 1]
        self.first = self.s * rows
        self.part = rows // nh
        self.mine = pl.ds(pl.multiple_of(self.h * self.part, self.part), self.part)

    def seg(self, pos):
        inside = (pos >= self.l0).astype(jnp.int32) + (pos >= self.tot).astype(jnp.int32)
        return jnp.where(pos >= 0, inside, -1)

    def pos(self, shift=0):
        return self.first + shift + lax.broadcasted_iota(jnp.int32, (self.rows, 1), 0)

    def same(self, shift):
        other = self.pos(shift)
        inside = other < self.nz * self.rows
        return (self.seg(other) == self.seg(self.pos())) & inside

    def allowed(self):
        shape = (self.rows, self.rows)
        row = lax.broadcasted_iota(jnp.int32, shape, 0)
        col = lax.broadcasted_iota(jnp.int32, shape, 1)
        return (col <= row) & (self.seg(self.first + col) == self.seg(self.first + row))

    def last_seg(self, block):
        return self.seg(block * self.rows + self.rows - 1)

    def prior_seg(self, block):
        return self.seg(block * self.rows - 1)

    def applies(self):
        return self.seg(self.pos()) == self.prior_seg(self.s)

    def tail(self):
        return self.seg(self.pos()) == self.last_seg(self.s)

    def peers(self):
        core = [(1 - self.sec, self.s, self.h)]
        seq = [(self.sec, (self.s + k) % self.nz, self.h) for k in range(1, self.nz)]
        head = [(self.sec, self.s, self.h ^ m) for m in range(1, self.nh)]
        return core, seq, head

    def barrier(self, core, seq, head):
        groups = self.peers()
        told = [d for use, g in zip((core, seq, head), groups) if use for d in g]
        sem = pltpu.get_barrier_semaphore()
        for device in told:
            pl.semaphore_signal(sem, 1, device_id=device, device_id_type=MESH)
        pl.semaphore_wait(sem, len(told))


def remote(src, dst, send, recv, device):
    return pltpu.make_async_remote_copy(
        src_ref=src, dst_ref=dst, send_sem=send, recv_sem=recv, device_id=device, device_id_type=MESH
    )


def scatter_start(at, buf, got, send, recv):
    sent = []
    for m in sorted(range(1, at.nh), reverse=True):
        peer = at.h ^ m
        rows = pl.ds(pl.multiple_of(peer * at.part, at.part), at.part)
        copy = remote(buf.at[rows], got.at[m - 1], send.at[m - 1], recv.at[m - 1], (at.sec, at.s, peer))
        copy.start()
        sent.append(copy)
    return sent


def scatter_sum(at, buf, got, sent):
    total = buf[at.mine].astype(F32)
    for copy in sent:
        copy.wait_recv()
    for m in range(1, at.nh):
        total = total + got[m - 1].astype(F32)
    return total


def gather_start(at, buf, send, recv):
    sent = []
    for m in sorted(range(1, at.nh), reverse=True):
        copy = remote(
            buf.at[at.mine], buf.at[at.mine], send.at[m - 1], recv.at[m - 1], (at.sec, at.s, at.h ^ m)
        )
        copy.start()
        sent.append(copy)
    return sent


def wait_recv(copies):
    for copy in copies:
        copy.wait_recv()


def wait_send(copies):
    for copy in copies:
        copy.wait_send()


def norm_rows(x, gain):
    return x * lax.rsqrt(jnp.mean(x * x, axis=-1, keepdims=True) + EPS) * gain


def norm_rows_back(x, gain, grad):
    inverse = lax.rsqrt(jnp.mean(x * x, axis=-1, keepdims=True) + EPS)
    unit = x * inverse
    scaled = grad * gain
    back = inverse * (scaled - unit * jnp.mean(scaled * unit, axis=-1, keepdims=True))
    return back, jnp.sum(grad * unit, axis=0, keepdims=True)


def lift_parts(low, tables, second, head):
    cols = slice(head * PSI, (head + 1) * PSI)
    lane = lax.broadcasted_iota(jnp.int32, (1, PSI), 1)
    one = dot_nn(low, tables[0, :, cols]) + (lane == 0).astype(F32)
    two = dot_nn(low, tables[second, :, cols]) + (lane <= FEAT).astype(F32)
    return one, two


def head_only(low, head):
    lane = lax.broadcasted_iota(jnp.int32, low.shape, 1)
    return jnp.where((lane >= head * FEAT) & (lane < (head + 1) * FEAT), low, jnp.zeros_like(low))


def convolve(at, u_s, taps, c_s, cx_s, heads):
    rows, width = at.rows, heads * HD
    out = taps[0:1, :width] * u_s[8 : 8 + rows, :width]
    for j in range(1, KW):
        shifted = u_s[8 - j : 8 - j + rows, :width]
        out = out + jnp.where(at.same(-j), shifted * taps[j : j + 1, :width], 0.0)
    c_s[0:rows, :width] = out
    lane = lax.broadcasted_iota(jnp.int32, (rows, LANES), 1)
    for head in range(heads):
        one = c_s[0:rows, head * HD : head * HD + LANES]
        cx_s[head] = jnp.where(lane < HD, one, jnp.where(lane == HD, 1.0, 0.0)).astype(BF16)


class Weights:
    def __init__(self, at, layer, own, other, slots, sems):
        self.at, self.layer, self.own, self.other, self.slots, self.sems = at, layer, own, other, slots, sems

    def _copy(self, src, i):
        return pltpu.make_async_copy(src[i].at[0], self.slots[i], self.sems.at[i])

    def start(self, i):
        @pl.when(self.at.sec == self.layer)
        def _():
            self._copy(self.own, i).start()

        @pl.when(self.at.sec != self.layer)
        def _():
            self._copy(self.other, i).start()

    def wait(self, i):
        self._copy(self.own, i).wait()


W_NAMES = ("q", "k", "v", "o", "out", "gate", "up", "down")


def fwd_kernel(layer, dims, *refs):
    nz, nh, rows, heads = dims
    refs = list(refs)

    def take(n):
        out = refs[:n]
        del refs[:n]
        return out

    lens, x_in, small_own = take(3)
    small_other = None if layer == 0 else take(1)[0]
    (tables,) = take(1)
    own = take(8)
    other = None if layer == 0 else take(8)
    if layer == 0:
        small_other = take(1)[0]
        other = take(8)
    xo_o, n1_o, n2_o, q_o, k_o, u_o, o_o, yx_o, sin_o, g_o, h_o, f_o, v_o = take(13)
    slots = take(8)
    (x_s, n1_s, n2_s, u_s, o_s, c_s, cx_s, yx_s, ss, sr, g_s, gb_s, p1, r1, p2, r2, f_s, v_s, t_s, xo_s, h_s, sm_s) = take(22)
    w_sem, io_sem, x_send, x_recv, e_send, e_recv, st_send, st_recv, head_send, head_recv = take(10)
    at = Place(lens, nz, nh, rows)
    d = x_s.shape[1]
    width = heads * HD
    core = (1 - at.sec, at.s, at.h)

    x_copy = pltpu.make_async_copy(x_in.at[at.sec] if layer == 0 else x_in, x_s, io_sem.at[0])
    x_copy.start()
    weights = Weights(at, layer, own, other, slots, w_sem)
    at.barrier(layer == 0, True, True)
    swaps = []
    if layer == 0:
        small_swap = remote(small_own, small_other, x_send.at[8], x_recv.at[8], core)
        small_swap.start()
        for i in range(8):
            swap = remote(own[i], other[i], x_send.at[i], x_recv.at[i], core)
            swap.start()
            swaps.append(swap)
        small_swap.wait_recv()
    small_copy = pltpu.make_async_copy(small_other, sm_s, io_sem.at[1])
    small_copy.start()

    def load(i):
        if layer == 0:

            @pl.when(at.sec == 1)
            def _():
                swaps[i].wait_recv()

        weights.start(i)

    if layer == 1:
        for i in range(8):
            load(i)
    else:
        for i in range(5):
            load(i)
    small_copy.wait()
    small = jnp.where(at.sec == layer, small_own[...], sm_s[...])
    gain_attn, gain_ffn, taps = small[0:1], small[1:2], small[2 : 2 + KW]
    x_copy.wait()
    n1_s[...] = norm_rows(x_s[...].astype(F32), gain_attn).astype(BF16)

    weights.wait(2)
    u_s[8 : 8 + rows, :width] = dot_nn(n1_s[...], slots[2][...]).astype(BF16).astype(F32)
    edge = remote(
        u_s.at[pl.ds(rows, 8)], u_s.at[pl.ds(0, 8)], e_send, e_recv, (at.sec, (at.s + 1) % nz, at.h)
    )

    @pl.when(at.s + 1 < nz)
    def _():
        edge.start()

    weights.wait(0)
    q_o[...] = (dot_nn(n1_s[...], slots[0][...]).astype(BF16).astype(F32) * 0.5).astype(BF16)
    weights.wait(1)
    k_o[...] = (dot_nn(n1_s[...], slots[1][...]).astype(BF16).astype(F32) * 0.5).astype(BF16)
    weights.wait(3)
    o_s[:, :width] = dot_nn(n1_s[...], slots[3][...])

    @pl.when(at.s > 0)
    def _():
        edge.wait_recv()

    convolve(at, u_s, taps, c_s, cx_s, heads)
    outs = [pltpu.make_async_copy(a, b, io_sem.at[2 + i]) for i, (a, b) in enumerate(((n1_s, n1_o), (u_s, u_o), (o_s, o_o)))]
    for copy in outs:
        copy.start()

    a_low, b_low = q_o[...], k_o[...]
    tail = at.tail()
    for head in range(heads):
        one, two = lift_parts(b_low, tables, 2, head)
        psi = jnp.where(tail, one * two, 0.0).astype(BF16)
        ss[head] = dot_tn(psi, cx_s[head])[:PSI_SENT].astype(BF16)
    for k in range(1, nz):

        @pl.when(at.s + k < nz)
        def _(k=k):
            remote(ss, sr.at[at.s], st_send.at[k - 1], st_recv.at[at.s], (at.sec, (at.s + k) % nz, at.h)).start()

    allowed = at.allowed()
    for head in range(heads):
        e = dot_nt(a_low, head_only(b_low, head))
        kern = jnp.where(allowed, 1.0 + e + 0.5 * e * e, 0.0).astype(BF16)
        yx_s[head] = dot_nn(kern, cx_s[head])
    for j in range(nz - 1):

        @pl.when(j < at.s)
        def _(j=j):
            remote(ss, sr.at[j], st_send.at[0], st_recv.at[j], core).wait_recv()

    prior = at.prior_seg(at.s)
    applies = at.applies()
    lane = lax.broadcasted_iota(jnp.int32, (rows, LANES), 1)
    sin_o[...] = jnp.zeros_like(sin_o)
    for head in range(heads):
        state = jnp.zeros((PSI_SENT, LANES), F32)
        for j in range(nz - 1):
            counts = (j < at.s) & (at.last_seg(j) == prior)
            state = state + jnp.where(counts, sr[j, head].astype(F32), 0.0)
        sin_o[head, 0:PSI_SENT] = state.astype(BF16)
        one, two = lift_parts(a_low, tables, 1, head)
        psi = (one * two).astype(BF16)
        yx = yx_s[head] + jnp.where(applies, dot_nn(psi, sin_o[head]), 0.0)
        yx_s[head] = yx
        gate = o_s[:, head * HD : head * HD + LANES]
        y = yx / yx[:, HD : HD + 1]
        g_s[:, head * HD : head * HD + LANES] = y * (gate * jax.nn.sigmoid(gate))
    gb_s[...] = g_s[:, :width].astype(BF16)
    outs2 = [pltpu.make_async_copy(a, b, io_sem.at[5 + i]) for i, (a, b) in enumerate(((yx_s, yx_o), (gb_s, g_o)))]
    for copy in outs2:
        copy.start()

    weights.wait(4)

    def mix_chunk(at_col, size):
        p1[:, pl.ds(at_col, size)] = dot_nn(gb_s[...], slots[4][:, pl.ds(at_col, size)]).astype(BF16)

    chunks(d, 256, mix_chunk)
    s1 = scatter_start(at, p1, r1, head_send.at[0], head_recv.at[0])
    if layer == 0:
        for i in range(5, 8):
            load(i)
    hidden = x_s[at.mine].astype(F32) + scatter_sum(at, p1, r1, s1)
    h_s[...] = hidden
    n2_s[at.mine] = norm_rows(hidden, gain_ffn).astype(BF16)
    s2 = gather_start(at, n2_s, head_send.at[1], head_recv.at[1])
    wait_recv(s2)
    outs3 = [pltpu.make_async_copy(a, b, io_sem.at[7 + i]) for i, (a, b) in enumerate(((n2_s, n2_o), (h_s, h_o)))]
    for copy in outs3:
        copy.start()

    weights.wait(5)
    weights.wait(6)

    def up_chunk(at_col, size):
        cols = pl.ds(at_col, size)
        f = dot_nn(n2_s[...], slots[5][:, cols])
        v = dot_nn(n2_s[...], slots[6][:, cols])
        f_s[:, cols] = f
        v_s[:, cols] = v
        t_s[:, cols] = (f * jax.nn.sigmoid(f) * v).astype(BF16)

    chunks(t_s.shape[1], 256, up_chunk)
    outs4 = [pltpu.make_async_copy(a, b, io_sem.at[9 + i]) for i, (a, b) in enumerate(((f_s, f_o), (v_s, v_o)))]
    for copy in outs4:
        copy.start()
    weights.wait(7)

    def down_chunk(at_col, size):
        p2[:, pl.ds(at_col, size)] = dot_nn(t_s[...], slots[7][:, pl.ds(at_col, size)]).astype(BF16)

    chunks(d, 256, down_chunk)
    s3 = scatter_start(at, p2, r2, head_send.at[2], head_recv.at[2])
    feed = scatter_sum(at, p2, r2, s3)
    my_pos = at.first + at.h * at.part + lax.broadcasted_iota(jnp.int32, (at.part, 1), 0)
    valid = my_pos < at.tot
    xo_s[at.mine] = jnp.where(valid, h_s[...] + feed, 0.0).astype(BF16)
    s4 = gather_start(at, xo_s, head_send.at[3], head_recv.at[3])
    wait_recv(s4)
    last = pltpu.make_async_copy(xo_s, xo_o, io_sem.at[11])
    last.start()
    wait_send(s1 + s2 + s3 + s4)

    @pl.when(at.s + 1 < nz)
    def _():
        edge.wait_send()

    for k in range(1, nz):

        @pl.when(at.s + k < nz)
        def _(k=k):
            remote(ss, sr.at[at.s], st_send.at[k - 1], st_recv.at[at.s], core).wait_send()

    if layer == 0:
        small_swap.wait_send()
        for i in range(8):
            swaps[i].wait_send()

            @pl.when(at.sec == 0)
            def _(i=i):
                swaps[i].wait_recv()

    for copy in outs + outs2 + outs3 + outs4 + [last]:
        copy.wait()


def bwd_kernel(layer, dims, *refs):
    nz, nh, rows, heads = dims
    refs = list(refs)

    def take(n):
        out = refs[:n]
        del refs[:n]
        return out

    lens, x_in, g_in, small_own, small_other, tables = take(6)
    own = take(8)
    other = take(8)
    n1_i, q_i, k_i, u_i, o_i, yx_i, sin_i, gb_i, h_i, f_i, v_i = take(11)
    ig_o, gains_o, conv_o, acat_o, aout_o = take(5)
    slots = take(8)
    (x_s, grad_s, n1_s, u_s, o_s, yx_s, gb_s, h_s, f_s, v_s) = take(10)
    (df_s, dv_s, p1, r1, p2, r2, dm_s, dh_s, dg_s, do_s, c_s, cx_s, dyx_s, ss, sr, st_s, da_s, db_s, dc_s, dcat_s, ig_s, acat_s, aout_s) = take(23)
    w_sem, io_sem, e_send, e_recv, st_send, st_recv, head_send, head_recv = take(8)
    at = Place(lens, nz, nh, rows)
    d = x_s.shape[1]
    width = heads * HD
    qk = heads * FEAT
    core = (1 - at.sec, at.s, at.h)

    loads = [
        pltpu.make_async_copy(a, b, io_sem.at[i])
        for i, (a, b) in enumerate(
            (
                (g_in.at[at.sec] if layer == 1 else g_in, grad_s),
                (f_i, f_s),
                (v_i, v_s),
                (h_i, h_s),
                (u_i, u_s),
                (o_i, o_s),
                (yx_i, yx_s),
                (gb_i, gb_s),
                (n1_i, n1_s),
                (x_in.at[at.sec] if layer == 0 else x_in, x_s),
            )
        )
    ]
    weights = Weights(at, layer, own, other, slots, w_sem)
    loads[0].start()
    weights.start(7)
    loads[1].start()
    loads[2].start()
    for i in (5, 6, 4):
        weights.start(i)
    for copy in loads[3:]:
        copy.start()
    for i in (0, 1, 2, 3):
        weights.start(i)
    at.barrier(False, True, True)
    small = jnp.where(at.sec == layer, small_own[...], small_other[...])
    gain_attn, gain_ffn, taps = small[0:1], small[1:2], small[2 : 2 + KW]
    valid = at.pos() < at.tot
    loads[0].wait()
    grad_s[...] = jnp.where(valid, grad_s[...].astype(F32), 0.0).astype(BF16)

    weights.wait(7)
    loads[1].wait()
    loads[2].wait()

    def down_chunk(at_row, size):
        cols = pl.ds(at_row, size)
        dt = dot_nt(grad_s[...], slots[7][cols, :])
        f = f_s[:, cols]
        sig = jax.nn.sigmoid(f)
        df_s[:, cols] = (dt * v_s[:, cols] * sig * (1.0 + f * (1.0 - sig))).astype(BF16)
        dv_s[:, cols] = (dt * f * sig).astype(BF16)

    chunks(df_s.shape[1], 256, down_chunk)
    weights.wait(5)
    weights.wait(6)

    def up_chunk(at_row, size):
        cols = pl.ds(at_row, size)
        part = dot_nt(df_s[...], slots[5][cols, :]) + dot_nt(dv_s[...], slots[6][cols, :])
        p1[:, cols] = part.astype(BF16)

    chunks(d, 256, up_chunk)
    s1 = scatter_start(at, p1, r1, head_send.at[0], head_recv.at[0])
    loads[3].wait()
    dn2 = scatter_sum(at, p1, r1, s1)
    back, gain_grad = norm_rows_back(h_s[...], gain_ffn, dn2)
    gains_o[1:2, :] = gain_grad
    dh = grad_s[at.mine].astype(F32) + back
    dh_s[...] = dh
    dm_s[at.mine] = dh.astype(BF16)
    s2 = gather_start(at, dm_s, head_send.at[1], head_recv.at[1])
    for copy in loads[4:]:
        copy.wait()
    for i in (4, 0, 1, 2, 3):
        weights.wait(i)
    convolve(at, u_s, taps, c_s, cx_s, heads)
    wait_recv(s2)

    def out_chunk(at_row, size):
        cols = pl.ds(at_row, size)
        dg_s[:, cols] = dot_nt(dm_s[...], slots[4][cols, :])

    chunks(width, 256, out_chunk)
    lane = lax.broadcasted_iota(jnp.int32, (rows, LANES), 1)
    applies = at.applies()
    tail = at.tail()
    a_low, b_low = q_i[...], k_i[...]
    for head in range(heads):
        cols = slice(head * HD, head * HD + LANES)
        gate, dg, yx = o_s[:, cols], dg_s[:, cols], yx_s[head]
        sig = jax.nn.sigmoid(gate)
        inverse = 1.0 / yx[:, HD : HD + 1]
        y = yx * inverse
        do_s[:, cols] = dg * y * sig * (1.0 + gate * (1.0 - sig))
        dy = jnp.where(lane < HD, dg * gate * sig, 0.0)
        dden = -jnp.sum(dy * y, axis=1, keepdims=True) * inverse
        dyx_s[head] = jnp.where(lane == HD, dden, dy * inverse).astype(BF16)
        one, two = lift_parts(a_low, tables, 1, head)
        psi = jnp.where(applies, one * two, 0.0).astype(BF16)
        ss[head] = dot_tn(psi, dyx_s[head])[:PSI_SENT].astype(BF16)
    for k in range(1, nz):

        @pl.when(at.s - k >= 0)
        def _(k=k):
            remote(ss, sr.at[at.s], st_send.at[k - 1], st_recv.at[at.s], (at.sec, (at.s + nz - k) % nz, at.h)).start()

    allowed = at.allowed()
    da_s[...] = jnp.zeros_like(da_s)
    db_s[...] = jnp.zeros_like(db_s)
    for head in range(heads):
        a_own, b_own = head_only(a_low, head), head_only(b_low, head)
        e = dot_nt(a_low, b_own)
        kern = jnp.where(allowed, 1.0 + e + 0.5 * e * e, 0.0).astype(BF16)
        dkern = dot_nt(dyx_s[head], cx_s[head])
        de = jnp.where(allowed, dkern * (1.0 + e), 0.0).astype(BF16)
        one, two = lift_parts(a_low, tables, 1, head)
        dpsi = jnp.where(applies, dot_nt(dyx_s[head], sin_i[head]), 0.0)
        pcols = slice(head * PSI, (head + 1) * PSI)
        da_s[...] += (
            dot_nn(de, b_own)
            + dot_nt((dpsi * two).astype(BF16), tables[0, :, pcols])
            + dot_nt((dpsi * one).astype(BF16), tables[1, :, pcols])
        )
        db_s[...] += dot_tn(de, a_own)
        yx_s[head] = dot_tn(kern, dyx_s[head])
    for j in range(1, nz):

        @pl.when(j > at.s)
        def _(j=j):
            remote(ss, sr.at[j], st_send.at[0], st_recv.at[j], core).wait_recv()

    mine_last = at.last_seg(at.s)
    st_s[...] = jnp.zeros_like(st_s)
    for head in range(heads):
        state = jnp.zeros((PSI_SENT, LANES), F32)
        for j in range(1, nz):
            counts = (j > at.s) & (at.prior_seg(j) == mine_last)
            state = state + jnp.where(counts, sr[j, head].astype(F32), 0.0)
        st_s[head, 0:PSI_SENT] = state.astype(BF16)
        one, two = lift_parts(b_low, tables, 2, head)
        psi = (one * two).astype(BF16)
        dpsi = jnp.where(tail, dot_nt(cx_s[head], st_s[head]), 0.0)
        pcols = slice(head * PSI, (head + 1) * PSI)
        db_s[...] += dot_nt((dpsi * two).astype(BF16), tables[0, :, pcols]) + dot_nt(
            (dpsi * one).astype(BF16), tables[2, :, pcols]
        )
        dc = yx_s[head] + jnp.where(tail, dot_nn(psi, st_s[head]), 0.0)
        dc_s[0:rows, head * HD : head * HD + LANES] = dc
    edge = remote(
        dc_s.at[pl.ds(0, 8)], dc_s.at[pl.ds(rows, 8)], e_send, e_recv, (at.sec, (at.s + nz - 1) % nz, at.h)
    )

    @pl.when(at.s > 0)
    def _():
        edge.start()

    dcat_s[:, 0:qk] = (da_s[...] * 0.5).astype(BF16)
    dcat_s[:, qk : 2 * qk] = (db_s[...] * 0.5).astype(BF16)
    dcat_s[:, 2 * qk + width :] = do_s[:, :width].astype(BF16)
    conv_o[...] = jnp.zeros_like(conv_o)
    for j in range(KW):
        product = dc_s[0:rows, :width] * u_s[8 - j : 8 - j + rows, :width]
        conv_o[j : j + 1, :width] = jnp.sum(jnp.where(at.same(-j), product, 0.0), axis=0, keepdims=True)

    @pl.when(at.s + 1 < nz)
    def _():
        edge.wait_recv()

    du = taps[0:1, :width] * dc_s[0:rows, :width]
    for j in range(1, KW):
        du = du + jnp.where(at.same(j), dc_s[j : j + rows, :width] * taps[j : j + 1, :width], 0.0)
    dcat_s[:, 2 * qk : 2 * qk + width] = du.astype(BF16)

    def proj_chunk(at_row, size):
        cols = pl.ds(at_row, size)
        part = (
            dot_nt(dcat_s[:, 0:qk], slots[0][cols, :])
            + dot_nt(dcat_s[:, qk : 2 * qk], slots[1][cols, :])
            + dot_nt(dcat_s[:, 2 * qk : 2 * qk + width], slots[2][cols, :])
            + dot_nt(dcat_s[:, 2 * qk + width :], slots[3][cols, :])
        )
        p2[:, cols] = part.astype(BF16)

    chunks(d, 256, proj_chunk)
    s3 = scatter_start(at, p2, r2, head_send.at[2], head_recv.at[2])

    def in_chunk(at_row, size):
        cols = pl.ds(at_row, size)
        acat_s[cols, :] = dot_tn(n1_s[:, cols], dcat_s[...]).astype(BF16)
        aout_s[:, cols] = dot_tn(gb_s[...], dm_s[:, cols]).astype(BF16)

    chunks(d, 256, in_chunk)
    outs = [pltpu.make_async_copy(a, b, io_sem.at[10 + i]) for i, (a, b) in enumerate(((acat_s, acat_o), (aout_s, aout_o)))]
    for copy in outs:
        copy.start()
    dn1 = scatter_sum(at, p2, r2, s3)
    back, gain_grad = norm_rows_back(x_s[at.mine].astype(F32), gain_attn, dn1)
    gains_o[0:1, :] = gain_grad
    gains_o[2:8, :] = jnp.zeros((6, d), F32)
    ig_s[at.mine] = (dh_s[...] + back).astype(BF16)
    s4 = gather_start(at, ig_s, head_send.at[3], head_recv.at[3])
    wait_recv(s4)
    last = pltpu.make_async_copy(ig_s, ig_o, io_sem.at[12])
    last.start()
    wait_send(s1 + s2 + s3 + s4)

    @pl.when(at.s > 0)
    def _():
        edge.wait_send()

    for k in range(1, nz):

        @pl.when(at.s - k >= 0)
        def _(k=k):
            remote(ss, sr.at[at.s], st_send.at[k - 1], st_recv.at[at.s], core).wait_send()

    for copy in outs + [last]:
        copy.wait()


def ffn_grad_kernel(dims, lens, n2_0, n2_1, g_0, g_1, *refs):
    nz, nh, rows, heads = dims
    refs = list(refs)

    def take(n):
        out = refs[:n]
        del refs[:n]
        return out

    own = take(3)
    other = take(3)
    outs = take(3)
    slots = [take(3), take(3)]
    n2_s, g_s, n2c, gc, t_s, df_s, dv_s = take(7)
    acc = take(3)
    send = take(3)
    got = take(3)
    w_sem, io_sem, x_send, x_recv = take(4)
    at = Place(lens, nz, nh, rows)
    d = n2_s.shape[2]
    block = d // nz
    core = (1 - at.sec, at.s, at.h)
    at.barrier(True, False, False)
    for role, source in ((0, other), (1, own)):
        for i in range(3):
            pltpu.make_async_copy(source[i].at[0], slots[role][i], w_sem.at[role, i]).start()

    def fetch(role, j, slot, go):
        where = pl.ds(pl.multiple_of(j * rows, rows), rows)
        for layer, n2_ref, g_ref in ((0, n2_0, g_0), (1, n2_1, g_1)):
            @pl.when((at.sec == layer) if role == 1 else (at.sec != layer))
            def _(n2_ref=n2_ref, g_ref=g_ref):
                for i, (src, dst) in enumerate(((n2_ref, n2_s), (g_ref, g_s))):
                    copy = pltpu.make_async_copy(src.at[where], dst.at[slot], io_sem.at[slot, i])
                    if go:
                        copy.start()
                    else:
                        copy.wait()

    fetch(0, 0, 0, True)
    swaps = []
    for role in range(2):
        gate, up, down = slots[role]
        for i in range(3):
            acc[i][...] = jnp.zeros_like(acc[i])

        def one(j, carry, role=role, gate=gate, up=up, down=down):
            slot = lax.rem(j, 2)
            fetch(role, j, slot, False)

            @pl.when(j + 1 < nz)
            def _():
                fetch(role, j + 1, lax.rem(j + 1, 2), True)

            if role == 0:

                @pl.when(j + 1 == nz)
                def _():
                    fetch(1, 0, 0 if nz % 2 == 0 else 1, True)

            pos = j * rows + lax.broadcasted_iota(jnp.int32, (rows, 1), 0)
            g_s[slot] = jnp.where(pos < at.tot, g_s[slot].astype(F32), 0.0).astype(BF16)
            for piece in range(nz):

                @pl.when(at.s == piece)
                def _(piece=piece):
                    n2c[...] = n2_s[slot, :, piece * block : (piece + 1) * block]
                    gc[...] = g_s[slot, :, piece * block : (piece + 1) * block]

            def hidden(at_col, size):
                cols = pl.ds(at_col, size)
                n2 = n2_s[slot]
                f = dot_nn(n2, gate[:, cols])
                v = dot_nn(n2, up[:, cols])
                dt = dot_nt(g_s[slot], down[cols, :])
                sig = jax.nn.sigmoid(f)
                t = (f * sig * v).astype(BF16)
                df = (dt * v * sig * (1.0 + f * (1.0 - sig))).astype(BF16)
                dv = (dt * f * sig).astype(BF16)
                acc[0][:, cols] += dot_tn(n2c[...], df)
                acc[1][:, cols] += dot_tn(n2c[...], dv)
                acc[2][:, cols] += dot_tn(gc[...], t)

            chunks(gate.shape[1], 256, hidden)
            return carry

        for i in range(3):
            pltpu.make_async_copy(own[i].at[0], slots[role][i], w_sem.at[role, i]).wait()
        lax.fori_loop(0, nz, one, 0)
        if role == 0:
            for i in range(3):
                send[i][...] = acc[i][...].astype(BF16)
                swap = remote(send[i], got[i], x_send.at[i], x_recv.at[i], core)
                swap.start()
                swaps.append(swap)
    for i in range(3):
        swaps[i].wait_recv()
        outs[i][...] = acc[i][...] + got[i][...].astype(F32)
    wait_send(swaps)


def swap_kernel(dims, a0, a1, b0, b1, x0, x1, g0, g1, a_o, b_o, x_o, g_o, a_s, b_s, a_r, b_r, io_sem, x_send, x_recv):
    sec, s, h = (lax.axis_index(a) for a in ("section", "seq", "head"))
    core = (1 - sec, s, h)
    sem = pltpu.get_barrier_semaphore()
    pl.semaphore_signal(sem, 1, device_id=core, device_id_type=MESH)
    pl.semaphore_wait(sem, 1)

    def moves(mine, his):
        out = [
            remote(his[0], a_r, x_send.at[0], x_recv.at[0], core),
            remote(his[1], b_r, x_send.at[1], x_recv.at[1], core),
            remote(his[2], x_o.at[sec], x_send.at[2], x_recv.at[2], core),
            remote(his[3], g_o.at[sec], x_send.at[3], x_recv.at[3], core),
        ]
        local = [
            pltpu.make_async_copy(mine[0], a_s, io_sem.at[0]),
            pltpu.make_async_copy(mine[1], b_s, io_sem.at[1]),
            pltpu.make_async_copy(mine[2], x_o.at[sec], io_sem.at[2]),
            pltpu.make_async_copy(mine[3], g_o.at[sec], io_sem.at[3]),
        ]
        return out, local

    sides = (((a0, b0, x0, g0), (a1, b1, x1, g1)), ((a1, b1, x1, g1), (a0, b0, x0, g0)))
    for here in range(2):

        @pl.when(sec == here)
        def _(here=here):
            out, local = moves(*sides[here])
            for copy in out + local:
                copy.start()

    out, local = moves(*sides[0])
    local[0].wait()
    out[0].wait_recv()
    a_s[...] = (a_s[...].astype(F32) + a_r[...].astype(F32)).astype(BF16)
    done_a = pltpu.make_async_copy(a_s, a_o, io_sem.at[4])
    done_a.start()
    local[1].wait()
    out[1].wait_recv()
    b_s[...] = (b_s[...].astype(F32) + b_r[...].astype(F32)).astype(BF16)
    done_b = pltpu.make_async_copy(b_s, b_o, io_sem.at[5])
    done_b.start()
    for copy in local[2:]:
        copy.wait()
    for copy in out[2:]:
        copy.wait_recv()
    for copy in out:
        copy.wait_send()
    done_a.wait()
    done_b.wait()


def shape(dims, kind=BF16):
    return jax.ShapeDtypeStruct(tuple(dims), kind)


ANY = pl.BlockSpec(memory_space=pl.ANY)
VM = pl.BlockSpec(memory_space=pltpu.VMEM)
SM = pl.BlockSpec(memory_space=pltpu.SMEM)
DMA = pltpu.SemaphoreType.DMA


def params(number):
    return pltpu.CompilerParams(collective_id=number, has_side_effects=True, vmem_limit_bytes=VMEM_LIMIT)


def shards(nz, nh, inputs, out_grad, lengths, norm_attn, norm_ffn, w_query, w_key, w_value, w_output_gate, conv_kernel, w_out, w_gate, w_up, w_down):
    micro, rows, d = inputs.shape
    heads = w_query.shape[2] // FEAT
    width, qk, ff = w_value.shape[2], w_query.shape[2], w_gate.shape[2]
    part = rows // nh
    dims = (nz, nh, rows, heads)
    wide = -(-width // LANES) * LANES + (LANES if (heads - 1) * HD + LANES > -(-width // LANES) * LANES else 0)
    tables = jnp.asarray(lift_tables(heads), BF16)
    own = (w_query, w_key, w_value, w_output_gate, w_out, w_gate, w_up, w_down)
    small_own = jnp.concatenate(
        [norm_attn, norm_ffn, jnp.pad(conv_kernel[0], ((0, 0), (0, d - width))), jnp.zeros((3, d), F32)]
    )
    w_slots = [pltpu.VMEM(w.shape[1:], BF16) for w in own]
    act = pltpu.VMEM((rows, d), BF16)
    headsum = pltpu.VMEM((nh - 1, part, d), BF16)

    def forward(layer, x, other_small, other):
        outs = [
            shape((rows, d)),
            shape((rows, d)),
            shape((rows, d)),
            shape((rows, qk)),
            shape((rows, qk)),
            shape((rows + 8, wide), F32),
            shape((rows, wide), F32),
            shape((heads, rows, LANES), F32),
            shape((heads, PSI, LANES)),
            shape((rows, width)),
            shape((part, d), F32),
            shape((rows, ff), F32),
            shape((rows, ff), F32),
        ]
        specs = [ANY, ANY, ANY, VM, VM, ANY, ANY, ANY, VM, ANY, ANY, ANY, ANY]
        ins = [lengths, x, small_own]
        in_specs = [SM, ANY, VM]
        if layer == 0:
            outs = [shape((8, d), F32)] + [shape(w.shape) for w in own] + outs
            specs = [ANY] * 9 + specs
        else:
            ins += [other_small]
            in_specs += [ANY]
        ins += [tables, *own]
        in_specs += [VM] + [ANY] * 8
        if layer == 1:
            ins += list(other)
            in_specs += [ANY] * 8
        scratch = w_slots + [
            act,
            act,
            act,
            pltpu.VMEM((rows + 8, wide), F32),
            pltpu.VMEM((rows, wide), F32),
            pltpu.VMEM((rows, wide), F32),
            pltpu.VMEM((heads, rows, LANES), BF16),
            pltpu.VMEM((heads, rows, LANES), F32),
            pltpu.VMEM((heads, PSI_SENT, LANES), BF16),
            pltpu.VMEM((nz, heads, PSI_SENT, LANES), BF16),
            pltpu.VMEM((rows, wide), F32),
            pltpu.VMEM((rows, width), BF16),
            act,
            headsum,
            act,
            headsum,
            pltpu.VMEM((rows, ff), F32),
            pltpu.VMEM((rows, ff), F32),
            pltpu.VMEM((rows, ff), BF16),
            act,
            pltpu.VMEM((part, d), F32),
            pltpu.VMEM((8, d), F32),
            DMA((8,)),
            DMA((12,)),
            DMA((9,)),
            DMA((9,)),
            DMA,
            DMA,
            DMA((nz,)),
            DMA((nz,)),
            DMA((4, nh - 1)),
            DMA((4, nh - 1)),
        ]
        return pl.pallas_call(
            functools.partial(fwd_kernel, layer, dims),
            out_shape=outs,
            in_specs=in_specs,
            out_specs=specs,
            scratch_shapes=scratch,
            compiler_params=params(layer),
        )(*ins)

    def backward(layer, x, grad, other_small, other, kept):
        outs = [shape((rows, d)), shape((8, d), F32), shape((8, wide), F32), shape((d, 2 * qk + 2 * width)), shape((width, d))]
        specs = [ANY, VM, VM, ANY, ANY]
        ins = [lengths, x, grad, small_own, other_small, tables, *own, *other, *kept]
        in_specs = [SM, ANY, ANY, VM, VM, VM] + [ANY] * 16 + [ANY, VM, VM, ANY, ANY, ANY, VM, ANY, ANY, ANY, ANY]
        scratch = w_slots + [
            act,
            act,
            act,
            pltpu.VMEM((rows + 8, wide), F32),
            pltpu.VMEM((rows, wide), F32),
            pltpu.VMEM((heads, rows, LANES), F32),
            pltpu.VMEM((rows, width), BF16),
            pltpu.VMEM((part, d), F32),
            pltpu.VMEM((rows, ff), F32),
            pltpu.VMEM((rows, ff), F32),
            pltpu.VMEM((rows, ff), BF16),
            pltpu.VMEM((rows, ff), BF16),
            act,
            headsum,
            act,
            headsum,
            act,
            pltpu.VMEM((part, d), F32),
            pltpu.VMEM((rows, wide), F32),
            pltpu.VMEM((rows, wide), F32),
            pltpu.VMEM((rows, wide), F32),
            pltpu.VMEM((heads, rows, LANES), BF16),
            pltpu.VMEM((heads, rows, LANES), BF16),
            pltpu.VMEM((heads, PSI_SENT, LANES), BF16),
            pltpu.VMEM((nz, heads, PSI_SENT, LANES), BF16),
            pltpu.VMEM((heads, PSI, LANES), BF16),
            pltpu.VMEM((rows, qk), F32),
            pltpu.VMEM((rows, qk), F32),
            pltpu.VMEM((rows + 8, wide), F32),
            pltpu.VMEM((rows, 2 * qk + 2 * width), BF16),
            act,
            pltpu.VMEM((d, 2 * qk + 2 * width), BF16),
            pltpu.VMEM((width, d), BF16),
            DMA((8,)),
            DMA((13,)),
            DMA,
            DMA,
            DMA((nz,)),
            DMA((nz,)),
            DMA((4, nh - 1)),
            DMA((4, nh - 1)),
        ]
        return pl.pallas_call(
            functools.partial(bwd_kernel, layer, dims),
            out_shape=outs,
            in_specs=in_specs,
            out_specs=specs,
            scratch_shapes=scratch,
            compiler_params=params(2 + layer),
        )(*ins)

    first = forward(0, inputs, None, None)
    other_small, other, kept_0 = first[0], first[1:9], first[9:]
    x_1, n2_0 = kept_0[0], kept_0[2]
    kept_1 = forward(1, x_1, other_small, other)
    x_2, n2_1 = kept_1[0], kept_1[2]

    def keep(kept):
        return (kept[1],) + tuple(kept[3:])

    ig_1, gains_1, conv_1, a_1, b_1 = backward(1, x_1, out_grad, other_small, other, keep(kept_1))
    ig_0, gains_0, conv_0, a_0, b_0 = backward(0, inputs, ig_1, other_small, other, keep(kept_0))

    def all_slots(block):
        return lax.all_gather(block, "seq", axis=0, tiled=True)

    sec = lax.axis_index("section")
    out_grad_mine = lax.dynamic_index_in_dim(out_grad, sec, 0, keepdims=False)
    block = d // nz
    ffn = [pltpu.VMEM(w.shape[1:], BF16) for w in own[5:]]
    grid_shapes = [(block, ff)] * 3
    g_gate, g_up, g_down = pl.pallas_call(
        functools.partial(ffn_grad_kernel, dims),
        out_shape=[shape(s, F32) for s in grid_shapes],
        in_specs=[SM] + [ANY] * 10,
        out_specs=[VM] * 3,
        scratch_shapes=ffn
        + ffn
        + [
            pltpu.VMEM((2, rows, d), BF16),
            pltpu.VMEM((2, rows, d), BF16),
            pltpu.VMEM((rows, block), BF16),
            pltpu.VMEM((rows, block), BF16),
            pltpu.VMEM((rows, ff), BF16),
            pltpu.VMEM((rows, ff), BF16),
            pltpu.VMEM((rows, ff), BF16),
        ]
        + [pltpu.VMEM(s, F32) for s in grid_shapes]
        + [pltpu.VMEM(s, BF16) for s in grid_shapes] * 2
        + [DMA((2, 3)), DMA((2, 2)), DMA((3,)), DMA((3,))],
        compiler_params=params(4),
    )(lengths, all_slots(n2_0), all_slots(n2_1), all_slots(ig_1), all_slots(out_grad_mine), *own[5:], *other[5:])

    a_sum, b_sum, section_out, input_grad = pl.pallas_call(
        functools.partial(swap_kernel, dims),
        out_shape=[shape(a_0.shape), shape(b_0.shape), shape((micro, rows, d)), shape((micro, rows, d))],
        in_specs=[ANY] * 8,
        out_specs=[ANY] * 4,
        scratch_shapes=[pltpu.VMEM(a_0.shape, BF16), pltpu.VMEM(b_0.shape, BF16)] * 2
        + [DMA((6,)), DMA((4,)), DMA((4,))],
        compiler_params=params(5),
    )(a_0, a_1, b_0, b_1, x_1, x_2, ig_0, ig_1)
    a_sum = lax.psum_scatter(a_sum, "seq", scatter_dimension=0, tiled=True).astype(F32)
    b_sum = lax.psum_scatter(b_sum, "seq", scatter_dimension=1, tiled=True).astype(F32)
    gains = lax.psum(jnp.stack([gains_0[:2], gains_1[:2]]), ("section", "seq", "head"))
    convs = lax.psum(jnp.stack([conv_0[:KW, :width], conv_1[:KW, :width]]), ("section", "seq"))
    gains = lax.dynamic_index_in_dim(gains, sec, 0, keepdims=False)
    convs = lax.dynamic_index_in_dim(convs, sec, 0, keepdims=True)
    return (
        section_out[None],
        input_grad[None],
        gains[0:1],
        gains[1:2],
        a_sum[None, :, 0:qk],
        a_sum[None, :, qk : 2 * qk],
        a_sum[None, :, 2 * qk : 2 * qk + width],
        a_sum[None, :, 2 * qk + width :],
        convs,
        b_sum[None],
        g_gate[None],
        g_up[None],
        g_down.T[None],
    )


def solution(mesh):
    return jax.shard_map(
        functools.partial(shards, mesh.shape["seq"], mesh.shape["head"]),
        mesh=mesh,
        in_specs=(
            P(None, "seq", None),
            P(None, "seq", None),
            P(),
            P("section", None),
            P("section", None),
            P("section", None, "head"),
            P("section", None, "head"),
            P("section", None, "head"),
            P("section", None, "head"),
            P("section", None, "head"),
            P("section", "head", None),
            P("section", None, "head"),
            P("section", None, "head"),
            P("section", "head", None),
        ),
        out_specs=(
            P("section", None, "seq", None),
            P("section", None, "seq", None),
            P("section", None),
            P("section", None),
            P("section", "seq", "head"),
            P("section", "seq", "head"),
            P("section", "seq", "head"),
            P("section", "seq", "head"),
            P("section", None, "head"),
            P("section", "head", "seq"),
            P("section", "seq", "head"),
            P("section", "seq", "head"),
            P("section", "head", "seq"),
        ),
        check_vma=False,
    )
```

time: 1900 us -> 843 us (0.44)
  waiting for transfers between devices: 771 us -> 251 us
  Pallas kernels: 0 us -> 448 us
  matrix products: 288 us -> 0 us
  blocking collectives: 358 us -> 71 us
  local copies, waits for them, and re-layouts: 217 us -> 48.2 us
  other arithmetic: 162 us -> 3.14 us
  starting transfers between devices: 40.3 us -> 0.24 us
  between operations: 43 us -> 14.5 us
    psum x11 -> x0, waiting for transfers between devices: 528 us -> none  [the longest x3 181 us: layer_grads(): lax.psum(partial_two.astype(jnp.bfloat16), 'head').astype(jnp.float32)]
    pallas_call x0 -> x6, Pallas kernels: none -> 448 us  [the longest x2 177 us: backward(): pl.pallas_call(functools.partial(bwd_kernel, layer, dims), out_shape=outs...]
    all_gather x18 -> x0, blocking collectives: 327 us -> none  [the longest x12 218 us: carried_in(): lax.all_gather(a.astype(kind), axis)]
    dot_general x153 -> x0, matrix products: 288 us -> none  [the longest x42 95 us: project(): return jnp.dot(left_arr, right_arr, preferred_element_type=jnp.float32)]
    all_gather x0 -> x4, waiting for transfers between devices: none -> 249 us  [all_slots(): return lax.all_gather(block, 'seq', axis=0, tiled=True)]
    unnamed x27 -> x7, waiting for transfers between devices: 243 us -> 2.44 us
    unnamed x842 -> x39, local copies, waits for them, and re-layouts: 202 us -> 43.2 us
    select_n x41 -> x0, other arithmetic: 62.6 us -> none  [the longest x24 42.4 us: hop(): return jax.tree.map(lambda a, b: jnp.where(reached, a, b), new, before)]
  transfers between devices with their start and end apart: 32 -> 6, of which waited for: 14 -> 4; matrix products, arithmetic and copies ran while one was open for 19% -> 1% of each run, Pallas kernels for 0% -> 10%
where the time goes in v1:
time: 843 us; the launch traced here: 837 us
  Pallas kernels  448 us (53%)
  waiting for transfers between devices  251 us (30%)
  blocking collectives  71 us (8%)
  local copies, waits for them, and re-layouts  48.2 us (6%)
  between operations  14.5 us (2%)
    all_gather x4, waiting for transfers between devices, all_slots(): return lax.all_gather(block, 'seq', axis=0, tiled=True)  249 us
    pallas_call x2, Pallas kernels, backward(): pl.pallas_call(functools.partial(bwd_kernel, layer, dims), out_shape=outs...  177 us
    pallas_call x2, Pallas kernels, forward(): pl.pallas_call(functools.partial(fwd_kernel, layer, dims), out_shape=outs...  134 us
    pallas_call x1, Pallas kernels, shards(): pl.pallas_call(functools.partial(ffn_grad_kernel, dims), out_shape=[shape...  80.1 us
    pallas_call x1, Pallas kernels, shards(): pl.pallas_call(functools.partial(swap_kernel, dims), out_shape=[shape(a_0...  56.9 us
    unnamed x39, local copies, waits for them, and re-layouts  43.2 us
    psum x1, blocking collectives, shards(): lax.psum(jnp.stack([gains_0[:2], gains_1[:2]]), ('section', 'seq', 'head'))  41.8 us
    psum x1, blocking collectives, shards(): lax.psum(jnp.stack([conv_0[:KW, :width], conv_1[:KW, :width]]), ('section...  29.3 us
  transfers between devices with their start and end apart: 6, of which 4 were waited for; matrix products, arithmetic and copies ran while one was open for 1% of the time, Pallas kernels for 10%

profile of v1, /device:TPU:0, one launch (start us, length us, event | category | flops | bytes accessed | tf_op | source)
XLA Modules:
  0.0 836.7 jit_solution(2935298684357225590)
XLA Ops:
  7.9 1.9 copy.57.refs_4_.refs_5_.refs_6_
  9.8 1.9 copy.58.refs_5_.refs_6_.refs_7_
  11.8 3.8 copy.59.refs_6_.refs_7_.refs_8_
  15.6 2.3 copy.60.refs_7_.refs_8_.refs_9_
  17.9 7.2 copy.61.refs_9_.refs_10_.refs_11_.refs_0_
  25.0 7.2 copy.62.refs_10_.refs_11_.refs_12_.refs_1_
  33.1 63.8 %shard_map.246 = (f32[8,1792]{1,0:T(8,128)}, bf16[1,1792,64]{2,1,0:T(8,128)(2,1)}, bf16[1,1792,64]{2,1,0:T(8,128)(2,1)}, bf16[1,1792,448]{2,1,0:T(8,128)(2,1)}, ...) custom-call(s32[2,2]{1,0:T(2,128)} %lens.1, ...), custom_call_target="tpu_custom_call" | custom-call | tf_op jit(solution)/shard_map/pallas_call | solution.py:926
  96.9 70.1 %shard_map.247 = (bf16[256,1792]{1,0:T(8,128)(2,1)}, bf16[256,1792]{1,0:T(8,128)(2,1)}, bf16[256,1792]{1,0:T(8,128)(2,1)}, bf16[256,64]{1,0:T(8,128)(2,1)}, bf16...) custom-call(s32[2,2]{1,0:T(2,128)} %lens.1, ...), custom_call_target="tpu_custom_call" | custom-call | tf_op jit(solution)/shard_map/pallas_call | solution.py:926
  167.0 105.4 %shard_map.248 = (bf16[256,1792]{1,0:T(8,128)(2,1)}, f32[8,1792]{1,0:T(8,128)}, f32[8,512]{1,0:T(8,128)}, bf16[1792,1024]{1,0:T(8,128)(2,1)}, bf16[448,1792]{1,0:T(8,128)(2,1)}) custom-call(s32[2,2]{1,0:T(2,128)} %lens.1, bf16[256,1792]{1,0:T(8,128)(2,1)} %get-tuple-element.65.refs_1_.x0, bf16[2,256,1792]{2,1,0:T(8,128)(2,1)} %refs_2_.2, ...), custom_call_target="tpu_custom_call" | custom-call | tf_op jit(solution)/shard_map/pallas_call | solution.py:983
  272.4 72.0 %shard_map.249 = (bf16[256,1792]{1,0:T(8,128)(2,1)}, f32[8,1792]{1,0:T(8,128)}, f32[8,512]{1,0:T(8,128)}, bf16[1792,1024]{1,0:T(8,128)(2,1)}, bf16[448,1792]{1,0:T(8,128)(2,1)}) custom-call(s32[2,2]{1,0:T(2,128)} %lens.1, bf16[2,256,1792]{2,1,0:T(8,128)(2,1)} %refs_1_.4, bf16[256,1792]{1,0:T(8,128)(2,1)} %get-tuple-element.86.refs_2_.g1, ...), custom_call_target="tpu_custom_call" | custom-call | tf_op jit(solution)/shard_map/pallas_call | solution.py:983
  344.4 56.9 %shard_map.250 = (bf16[1792,1024]{1,0:T(8,128)(2,1)}, bf16[448,1792]{1,0:T(8,128)(2,1)}, bf16[2,256,1792]{2,1,0:T(8,128)(2,1)}, bf16[2,256,1792]{2,1,0:T(8,128)(2,1)}) custom-call(bf16[1792,1024]{1,0:T(8,128)(2,1)} %get-tuple-element.98.a0, bf16[1792,1024]{1,0:T(8,128)(2,1)} %get-tuple-element.99.a1, bf16[448,1792]{1,0:T(8,128)(2,1)} %get-tuple-element.100.b0, ...), custom_call_target="tpu_custom_call" | custom-call | tf_op jit(solution)/shard_map/pallas_call | solution.py:1034
  401.3 3.7 copy.86
  407.2 1.0 constant_dynamic-slice_fusion
  409.0 29.3 %psum.15 = f32[2,3,448]{2,1,0:T(4,128)S(1)} all-reduce(f32[2,3,448]{2,1,0:T(4,128)S(1)} %pad_maximum_fusion.1), channel_id=1, replica_groups=mesh['section'=2,'seq'=4,'head'=4] {'section','seq'}, use_global_device_ids=true, to_apply=%region_2.3 | all-reduce | flops 2688 | bytes 21504 | tf_op jit(solution)/shard_map/psum | solution.py:1046
  440.6 41.8 %psum.14 = f32[2,2,1792]{2,1,0:T(2,128)S(1)} all-reduce(f32[2,2,1792]{2,1,0:T(2,128)S(1)} %pad_maximum_fusion), channel_id=1, replica_groups=mesh['section'=2,'seq'=4,'head'=4] {'section','seq','head'}, use_global_device_ids=true, to_apply=%region_0.1 | all-reduce | flops 7168 | bytes 57344 | tf_op jit(solution)/shard_map/psum | solution.py:1045
  483.0 1.2 copy.87
  484.2 1.0 bitcast_convert_fusion
  485.2 31.7 %all-gather.6.cloned.1.call-done.n2_0 = bf16[1024,1792]{1,0:T(8,128)(2,1)} async-done(((bf16[256,1792]{1,0:T(8,128)(2,1)}), bf16[1024,1792]{1,0:T(8,128)(2,1)}) %all-gather.6.cloned.1.call-update) | async-done | bytes 3670032 | tf_op jit(solution)/shard_map/all_gather | solution.py:1005
  517.0 72.2 %all-gather.8.cloned.1.call-done.n2_1 = bf16[1024,1792]{1,0:T(8,128)(2,1)} async-done(((bf16[256,1792]{1,0:T(8,128)(2,1)}), bf16[1024,1792]{1,0:T(8,128)(2,1)}) %all-gather.8.cloned.1.call-update) | async-done | bytes 3670032 | tf_op jit(solution)/shard_map/all_gather | solution.py:1005
  589.2 72.2 %all-gather.10.cloned.1.call-done.g_0 = bf16[1024,1792]{1,0:T(8,128)(2,1)} async-done(((bf16[256,1792]{1,0:T(8,128)(2,1)}), bf16[1024,1792]{1,0:T(8,128)(2,1)}) %all-gather.10.cloned.1.call-update) | async-done | bytes 3670032 | tf_op jit(solution)/shard_map/all_gather | solution.py:1005
  661.3 72.7 %all-gather.12.cloned.1.call-done = bf16[1,1024,1792]{2,1,0:T(8,128)(2,1)} async-done(((bf16[1,256,1792]{2,1,0:T(8,128)(2,1)}), bf16[1,1024,1792]{2,1,0:T(8,128)(2,1)}) %all-gather.12.cloned.1.call-update) | async-done | bytes 3670032 | tf_op jit(solution)/shard_map/all_gather | solution.py:1005
  734.1 80.1 %shard_map.251 = (f32[448,1216]{1,0:T(8,128)}, f32[448,1216]{1,0:T(8,128)}, f32[448,1216]{1,0:T(8,128)}) custom-call(s32[2,2]{1,0:T(2,128)} %lens.1, bf16[1024,1792]{1,0:T(8,128)(2,1)} %all-gather.6.cloned.1.call-done.n2_0, bf16[1024,1792]{1,0:T(8,128)(2,1)} %all-gather.8.cloned.1.call-done.n2_1, bf16[1024,1792]{1,0:T(8,128)(2,1)} %all-gather.10.cloned.1.call-done.g_0, ...), custom_call_target="tpu_custom_call" | custom-call | tf_op jit(solution)/shard_map/pallas_call | solution.py:1012
  814.2 1.4 convert_element_type.6
  815.7 1.5 slice_bitcast_fusion
  818.8 1.2 copy.96
  821.0 1.2 copy.97
  822.2 1.1 copy-done.3
  823.3 1.4 copy.98
  824.7 1.1 copy-done.2
  825.8 1.4 copy.99
  827.2 1.1 copy-done.1
  828.3 1.4 copy.100
  (49 shorter events, 9.9 us)
Async XLA Ops:
  7.2 475.8 %reduce-scatter.7.cloned.1.call-start = ((), (), s32[]{:S(2)}) async-start(), calls=%async_computation.7 | async-start | bytes 2293760
  11.7 3.8 copy-start.6
  25.0 7.3 copy-start.7
  25.0 7.3 copy-start.8
  405.1 2.1 copy-start
  405.1 111.9 %all-gather.6.cloned.1.call-start = ((), (), s32[]{:S(2)}) async-start(), calls=%async_computation.3 | async-start | bytes 4587520 | tf_op jit(solution)/shard_map/all_gather | solution.py:1005
  405.9 183.3 %all-gather.8.cloned.1.call-start = ((), (), s32[]{:S(2)}) async-start(), calls=%async_computation.4 | async-start | bytes 4587520 | tf_op jit(solution)/shard_map/all_gather | solution.py:1005
  406.6 254.7 %all-gather.10.cloned.1.call-start = ((), (), s32[]{:S(2)}) async-start(), calls=%async_computation.5 | async-start | bytes 4587520 | tf_op jit(solution)/shard_map/all_gather | solution.py:1005
  407.2 326.9 %all-gather.12.cloned.1.call-start = ((), (), s32[]{:S(2)}) async-start(), calls=%async_computation.6 | async-start | bytes 4587520 | tf_op jit(solution)/shard_map/all_gather | solution.py:1005
  408.2 405.9 %reduce-scatter.5.cloned.1.call-start = ((), (), s32[]{:S(2)}) async-start(), calls=%async_computation.2 | async-start | bytes 4587520 | tf_op jit(solution)/shard_map/reduce_scatter | solution.py:1043
  408.3 0.7 copy-start.9
  408.3 0.7 copy-start.10
  815.7 3.1 copy-start.5
  818.8 2.2 copy-start.4
  821.0 2.3 copy-start.3
  823.3 2.5 copy-start.2
  825.8 2.5 copy-start.1
Sparse Core Ops, SparseCore 0:
  405.2 37.8 reduce-scatter.6
  444.7 72.2 all-gather.5
  518.6 70.5 all-gather.7
  590.6 70.7 all-gather.9
  663.3 70.7 all-gather.11
  736.2 67.0 reduce-scatter.4

commit v2 on v0

v2 whole, which is shorter than its diff:
```python
import functools

import jax
import jax.numpy as jnp
import numpy as np
from jax import lax
from jax.experimental import pallas as pl
from jax.experimental.pallas import tpu as pltpu
from jax.sharding import PartitionSpec as P

HD = 112
FEAT = 16
KW = 3
EPS = 1e-05
LANES = 128
PSI = 256
PSI_SENT = 160
MESH = pl.DeviceIdType.MESH
F32 = jnp.float32
BF16 = jnp.bfloat16
VMEM_LIMIT = 62 << 20


def dot_nn(a, b):
    return lax.dot_general(a, b, (((1,), (0,)), ((), ())), preferred_element_type=F32)


def dot_nt(a, b):
    return lax.dot_general(a, b, (((1,), (1,)), ((), ())), preferred_element_type=F32)


def dot_tn(a, b):
    return lax.dot_general(a, b, (((0,), (0,)), ((), ())), preferred_element_type=F32)


def chunks(total, step, body):
    whole = total // step
    if whole > 1:

        def one(i, carry):
            body(pl.multiple_of(i * step, step), step)
            return carry

        lax.fori_loop(0, whole, one, 0)
    elif whole == 1:
        body(0, step)
    if total % step:
        body(whole * step, total % step)


def lift_tables(heads):
    first = np.zeros((heads * FEAT, heads * PSI), np.float32)
    second = np.zeros_like(first)
    second_key = np.zeros_like(first)
    for head in range(heads):
        row, col = head * FEAT, head * PSI
        for i in range(FEAT):
            first[row + i, col + 1 + i] = 1.0
        at = 1 + FEAT
        for i in range(FEAT):
            for j in range(i, FEAT):
                first[row + i, col + at] = 1.0
                second[row + j, col + at] = 1.0
                second_key[row + j, col + at] = 0.5 if i == j else 1.0
                at += 1
    return np.stack([first, second, second_key])


class Place:
    def __init__(self, lens, nz, nh, rows):
        self.sec, self.s, self.h = (lax.axis_index(a) for a in ("section", "seq", "head"))
        self.nz, self.nh, self.rows = nz, nh, rows
        self.l0 = lens[self.sec, 0]
        self.tot = self.l0 + lens[self.sec, 1]
        self.first = self.s * rows
        self.part = rows // nh
        self.mine = pl.ds(pl.multiple_of(self.h * self.part, self.part), self.part)

    def seg(self, pos):
        inside = (pos >= self.l0).astype(jnp.int32) + (pos >= self.tot).astype(jnp.int32)
        return jnp.where(pos >= 0, inside, -1)

    def pos(self, shift=0):
        return self.first + shift + lax.broadcasted_iota(jnp.int32, (self.rows, 1), 0)

    def same(self, shift):
        other = self.pos(shift)
        inside = other < self.nz * self.rows
        return (self.seg(other) == self.seg(self.pos())) & inside

    def allowed(self):
        shape = (self.rows, self.rows)
        row = lax.broadcasted_iota(jnp.int32, shape, 0)
        col = lax.broadcasted_iota(jnp.int32, shape, 1)
        return (col <= row) & (self.seg(self.first + col) == self.seg(self.first + row))

    def last_seg(self, block):
        return self.seg(block * self.rows + self.rows - 1)

    def prior_seg(self, block):
        return self.seg(block * self.rows - 1)

    def applies(self):
        return self.seg(self.pos()) == self.prior_seg(self.s)

    def tail(self):
        return self.seg(self.pos()) == self.last_seg(self.s)

    def peers(self):
        core = [(1 - self.sec, self.s, self.h)]
        seq = [(self.sec, (self.s + k) % self.nz, self.h) for k in range(1, self.nz)]
        head = [(self.sec, self.s, self.h ^ m) for m in range(1, self.nh)]
        return core, seq, head

    def barrier(self, core, seq, head):
        groups = self.peers()
        told = [d for use, g in zip((core, seq, head), groups) if use for d in g]
        sem = pltpu.get_barrier_semaphore()
        for device in told:
            pl.semaphore_signal(sem, 1, device_id=device, device_id_type=MESH)
        pl.semaphore_wait(sem, len(told))


def remote(src, dst, send, recv, device):
    return pltpu.make_async_remote_copy(
        src_ref=src, dst_ref=dst, send_sem=send, recv_sem=recv, device_id=device, device_id_type=MESH
    )


def scatter_start(at, buf, got, send, recv):
    sent = []
    for m in sorted(range(1, at.nh), reverse=True):
        peer = at.h ^ m
        rows = pl.ds(pl.multiple_of(peer * at.part, at.part), at.part)
        copy = remote(buf.at[rows], got.at[m - 1], send.at[m - 1], recv.at[m - 1], (at.sec, at.s, peer))
        copy.start()
        sent.append(copy)
    return sent


def scatter_sum(at, buf, got, sent):
    total = buf[at.mine].astype(F32)
    for copy in sent:
        copy.wait_recv()
    for m in range(1, at.nh):
        total = total + got[m - 1].astype(F32)
    return total


def gather_start(at, buf, send, recv):
    sent = []
    for m in sorted(range(1, at.nh), reverse=True):
        copy = remote(
            buf.at[at.mine], buf.at[at.mine], send.at[m - 1], recv.at[m - 1], (at.sec, at.s, at.h ^ m)
        )
        copy.start()
        sent.append(copy)
    return sent


def wait_recv(copies):
    for copy in copies:
        copy.wait_recv()


def wait_send(copies):
    for copy in copies:
        copy.wait_send()


def norm_rows(x, gain):
    return x * lax.rsqrt(jnp.mean(x * x, axis=-1, keepdims=True) + EPS) * gain


def norm_rows_back(x, gain, grad):
    inverse = lax.rsqrt(jnp.mean(x * x, axis=-1, keepdims=True) + EPS)
    unit = x * inverse
    scaled = grad * gain
    back = inverse * (scaled - unit * jnp.mean(scaled * unit, axis=-1, keepdims=True))
    return back, jnp.sum(grad * unit, axis=0, keepdims=True)


def lift_parts(low, tables, second, head):
    cols = slice(head * PSI, (head + 1) * PSI)
    lane = lax.broadcasted_iota(jnp.int32, (1, PSI), 1)
    one = dot_nn(low, tables[0, :, cols]) + (lane == 0).astype(F32)
    two = dot_nn(low, tables[second, :, cols]) + (lane <= FEAT).astype(F32)
    return one, two


def head_only(low, head):
    lane = lax.broadcasted_iota(jnp.int32, low.shape, 1)
    return jnp.where((lane >= head * FEAT) & (lane < (head + 1) * FEAT), low, jnp.zeros_like(low))


def convolve(at, u_s, taps, c_s, cx_s, heads):
    rows, width = at.rows, heads * HD
    out = taps[0:1, :width] * u_s[8 : 8 + rows, :width]
    for j in range(1, KW):
        shifted = u_s[8 - j : 8 - j + rows, :width]
        out = out + jnp.where(at.same(-j), shifted * taps[j : j + 1, :width], 0.0)
    c_s[0:rows, :width] = out
    lane = lax.broadcasted_iota(jnp.int32, (rows, LANES), 1)
    for head in range(heads):
        one = c_s[0:rows, head * HD : head * HD + LANES]
        cx_s[head] = jnp.where(lane < HD, one, jnp.where(lane == HD, 1.0, 0.0)).astype(BF16)


def order(at, i):
    left, right = at.s, at.nz - 1 - at.s
    both = 2 * jnp.minimum(left, right)
    near = i <= both
    dist = jnp.where(near, (i + 1) // 2, i - both // 2)
    leftward = jnp.where(near, i % 2 == 1, left > right)
    return jnp.where(leftward, at.s - dist, at.s + dist)


class Ring:
    def __init__(self, at, src, dst, send, recv):
        self.at, self.src, self.dst, self.send, self.recv = at, src, dst, send, recv

    def _copy(self, way, k, block, first):
        at = self.at
        to = lax.rem(at.s + (1 if way == 0 else at.nz - 1), at.nz)
        src = self.src if first else self.dst.at[block]
        return remote(src, self.dst.at[block], self.send.at[way, k], self.recv.at[way, k], (at.sec, to, at.h))

    def step(self, k):
        at = self.at
        first = isinstance(k, int) and k == 0
        for way in range(2):
            block = at.s - k if way == 0 else at.s + k
            there = block >= 0 if way == 0 else block < at.nz
            onward = at.s + 1 < at.nz if way == 0 else at.s > 0
            if not first:

                @pl.when(there)
                def _(way=way, block=block):
                    self._copy(way, k - 1, block, False).wait_recv()

            if not isinstance(k, int) or k < at.nz - 1:

                @pl.when(there & onward & (k < at.nz - 1))
                def _(way=way, block=block):
                    self._copy(way, k, block, first).start()

    def drain(self):
        at = self.at
        for k in range(at.nz - 1):
            for way in range(2):
                block = at.s - k if way == 0 else at.s + k
                there = block >= 0 if way == 0 else block < at.nz
                onward = at.s + 1 < at.nz if way == 0 else at.s > 0

                @pl.when(there & onward)
                def _(way=way, k=k):
                    self._copy(way, k, at.s, True).wait_send()


class LineSum:
    def __init__(self, at, mine, peer, land, work, io, send, recv, peer_recv):
        self.at, self.mine, self.peer, self.land, self.work = at, mine, peer, land, work
        self.io, self.send, self.recv, self.peer_recv = io, send, recv, peer_recv

    def _hop(self, way, d):
        at = self.at
        to = lax.rem(at.s + (1 if way == 0 else at.nz - 1), at.nz)
        return remote(self.work.at[way], self.land.at[way, d], self.send.at[way, d], self.recv.at[way, d], (at.sec, to, at.h))

    def _load(self, src, slot):
        copy = pltpu.make_async_copy(src, self.work.at[slot], self.io)
        copy.start()
        copy.wait()

    def _add(self, slot, src):
        self._load(src, 2)
        self.work[slot] = (self.work[slot].astype(F32) + self.work[2].astype(F32)).astype(BF16)

    def _own(self, slot, d):
        at = self.at
        self._load(self.mine.at[d], slot)
        remote(self.mine.at[d], self.peer.at[d], self.peer_recv.at[d], self.peer_recv.at[d], (1 - at.sec, at.s, at.h)).wait_recv()
        self._add(slot, self.peer.at[d])

    def slot(self, i):
        at = self.at
        for way in range(2):
            begun = i - at.s if way == 0 else i - (at.nz - 1 - at.s)
            d = at.nz - 1 - begun if way == 0 else begun
            earlier = at.s > 0 if way == 0 else at.s < at.nz - 1

            @pl.when((begun >= 0) & (i < at.nz - 1))
            def _(way=way, d=d, begun=begun, earlier=earlier):
                @pl.when(begun > 0)
                def _():
                    self._hop(way, d + 1 if way == 0 else d - 1).wait_send()

                self._own(way, d)

                @pl.when(earlier)
                def _():
                    self._hop(way, d).wait_recv()
                    self._add(way, self.land.at[way, d])

                self._hop(way, d).start()

    def last(self):
        at = self.at

        @pl.when(at.s < at.nz - 1)
        def _():
            self._hop(0, at.s + 1).wait_send()

        @pl.when(at.s > 0)
        def _():
            self._hop(1, at.s - 1).wait_send()

        self._own(0, at.s)

        @pl.when(at.s > 0)
        def _():
            self._hop(0, at.s).wait_recv()
            self._add(0, self.land.at[0, at.s])

        @pl.when(at.s < at.nz - 1)
        def _():
            self._hop(1, at.s).wait_recv()
            self._add(0, self.land.at[1, at.s])


def taker(refs):
    refs = list(refs)

    def take(n):
        out = refs[:n]
        del refs[:n]
        return out

    return take


def weight_slots(cat, out, gate, up, down, qk, width):
    at_row, views = 0, []
    for size in (qk, qk, width, width):
        views.append(cat.at[pl.ds(at_row, size)])
        at_row += size
    return views + [out, gate, up, down]


SAVED = 11


def fwd_kernel(dims, *refs):
    nz, nh, rows, heads = dims
    take = taker(refs)
    lens, inputs, out_grad, small_own, tables = take(5)
    own = take(8)
    small_other = take(1)[0]
    other = take(8)
    saved = [take(SAVED), take(SAVED)]
    x_out, gath_g1, gath_n2, n2_out = take(4)
    mats = [take(5), take(5)]
    (x_s, n1_s, n2_s, qk_s, u_s, edge_s, o_s, c_s, cx_s, yx_s, ss, sr, sin_s, g_s, gb_s, part_s, got_s, f_s, v_s, t_s, xo_s, h_s, sm_s) = take(23)
    w_sem, io_sem, save_sem, x_send, x_recv, e_send, e_recv, st_send, st_recv, head_send, head_recv, r_send, r_recv = take(13)
    at = Place(lens, nz, nh, rows)
    d = x_s.shape[1]
    width, qk = heads * HD, heads * FEAT
    core = (1 - at.sec, at.s, at.h)
    slots = [weight_slots(*m, qk, width) for m in mats]

    x_copy = pltpu.make_async_copy(inputs.at[at.sec], x_s, io_sem.at[0])
    x_copy.start()

    def local(layer, i):
        return pltpu.make_async_copy(own[i].at[0], slots[layer][i], w_sem.at[i])

    def swap(layer, i):
        return remote(own[i].at[0], slots[layer][i], x_send.at[i], x_recv.at[i], core)

    def stash(layer, i):
        return pltpu.make_async_copy(slots[layer][i], other[i].at[0], w_sem.at[8 + i])

    for here in range(2):

        @pl.when(at.sec == here)
        def _(here=here):
            for i in (2, 0, 1, 3, 4, 5, 6, 7):
                local(here, i).start()

    at.barrier(True, True, True)
    small_swap = remote(small_own, small_other, x_send.at[8], x_recv.at[8], core)
    small_swap.start()
    for here in range(2):

        @pl.when(at.sec == here)
        def _(here=here):
            for i in (2, 0, 1, 3, 4, 5, 6, 7):
                swap(here, i).start()

    ring_g = Ring(at, out_grad.at[at.sec], gath_g1, r_send.at[0], r_recv.at[0])
    ring_n = Ring(at, gath_n2.at[at.s], gath_n2, r_send.at[1], r_recv.at[1])
    ring_g.step(0)
    small_swap.wait_recv()
    small_copy = pltpu.make_async_copy(small_other, sm_s, io_sem.at[1])
    small_copy.start()
    small_copy.wait()

    def wait_weight(layer, i):
        @pl.when(at.sec == layer)
        def _():
            local(layer, i).wait()

        @pl.when(at.sec != layer)
        def _():
            swap(layer, i).wait_recv()
            stash(layer, i).start()

    allowed = at.allowed()
    applies, tail, prior = at.applies(), at.tail(), at.prior_seg(at.s)
    my_pos = at.first + at.h * at.part + lax.broadcasted_iota(jnp.int32, (at.part, 1), 0)
    my_valid = my_pos < at.tot

    def layer_forward(layer, x_s, hooks):
        cat, w_out, w_gate, w_up, w_down = mats[layer]
        small = jnp.where(at.sec == layer, small_own[...], sm_s[...])
        gain_attn, gain_ffn, taps = small[0:1], small[1:2], small[2 : 2 + KW]
        keep = []

        def save(src, i):
            copy = pltpu.make_async_copy(src, saved[layer][i], save_sem.at[i])
            copy.start()
            keep.append(copy)

        n1_s[...] = norm_rows(x_s[...].astype(F32), gain_attn).astype(BF16)
        save(x_s.at[at.mine], 0)
        save(n1_s, 1)
        wait_weight(layer, 2)
        u_s[8 : 8 + rows, :width] = dot_nt(n1_s[...], cat[2 * qk : 2 * qk + width, :]).astype(BF16).astype(F32)
        edge = remote(
            u_s.at[pl.ds(rows, 8)], edge_s.at[layer], e_send.at[layer], e_recv.at[layer],
            (at.sec, lax.rem(at.s + 1, nz), at.h),
        )

        @pl.when(at.s + 1 < nz)
        def _():
            edge.start()

        wait_weight(layer, 0)
        wait_weight(layer, 1)
        low = dot_nt(n1_s[...], cat[0 : 2 * qk, :]).astype(BF16).astype(F32)
        qk_s[...] = (low * 0.5).astype(BF16)
        save(qk_s, 2)
        a_low, b_low = qk_s[:, 0:qk], qk_s[:, qk : 2 * qk]

        @pl.when(at.s > 0)
        def _():
            edge.wait_recv()

        u_s[0:8, :] = edge_s[layer]
        save(u_s, 3)
        convolve(at, u_s, taps, c_s, cx_s, heads)

        for head in range(heads):
            one, two = lift_parts(b_low, tables, 2, head)
            psi = jnp.where(tail, one * two, 0.0).astype(BF16)
            ss[layer, head] = dot_tn(psi, cx_s[head])[:PSI_SENT].astype(BF16)

        def state(k):
            return remote(
                ss.at[layer], sr.at[layer, at.s], st_send.at[layer, k - 1], st_recv.at[layer, at.s],
                (at.sec, lax.rem(at.s + k, nz), at.h),
            )

        for k in range(1, nz):

            @pl.when(at.s + k < nz)
            def _(k=k):
                state(k).start()

        wait_weight(layer, 3)
        o_s[:, :width] = dot_nt(n1_s[...], cat[2 * qk + width :, :])
        save(o_s, 4)
        for head in range(heads):
            e = dot_nt(a_low, head_only(b_low, head))
            kern = jnp.where(allowed, 1.0 + e + 0.5 * e * e, 0.0).astype(BF16)
            yx_s[head] = dot_nn(kern, cx_s[head])
        for j in range(nz - 1):

            @pl.when(j < at.s)
            def _(j=j):
                remote(ss.at[layer], sr.at[layer, j], st_send.at[layer, 0], st_recv.at[layer, j], core).wait_recv()

        hooks["states"]()
        sin_s[...] = jnp.zeros_like(sin_s)
        for head in range(heads):
            total = jnp.zeros((PSI_SENT, LANES), F32)
            for j in range(nz - 1):
                counts = (j < at.s) & (at.last_seg(j) == prior)
                total = total + jnp.where(counts, sr[layer, j, head].astype(F32), 0.0)
            sin_s[head, 0:PSI_SENT] = total.astype(BF16)
            one, two = lift_parts(a_low, tables, 1, head)
            psi = (one * two).astype(BF16)
            yx = yx_s[head] + jnp.where(applies, dot_nn(psi, sin_s[head]), 0.0)
            yx_s[head] = yx
            gate = o_s[:, head * HD : head * HD + LANES]
            y = yx / yx[:, HD : HD + 1]
            g_s[:, head * HD : head * HD + LANES] = y * (gate * jax.nn.sigmoid(gate))
        gb_s[...] = g_s[:, :width].astype(BF16)
        save(yx_s, 5)
        save(sin_s, 6)
        save(gb_s, 7)

        wait_weight(layer, 4)

        def mix_chunk(at_col, size):
            part_s[layer, 0, :, pl.ds(at_col, size)] = dot_nn(gb_s[...], w_out[:, pl.ds(at_col, size)]).astype(BF16)

        chunks(d, 256, mix_chunk)
        s1 = scatter_start(at, part_s.at[layer, 0], got_s, head_send.at[layer, 0], head_recv.at[layer, 0])
        hooks["rs1"]()
        hidden = x_s[at.mine].astype(F32) + scatter_sum(at, part_s.at[layer, 0], got_s, s1)
        h_s[...] = hidden
        n2_s[at.mine] = norm_rows(hidden, gain_ffn).astype(BF16)
        s2 = gather_start(at, n2_s, head_send.at[layer, 1], head_recv.at[layer, 1])
        save(h_s, 8)
        hooks["ag1"]()
        wait_recv(s2)
        hooks["n2"]()

        wait_weight(layer, 5)
        wait_weight(layer, 6)

        def up_chunk(at_row, size):
            cols = pl.ds(at_row, size)
            f = dot_nt(n2_s[...], w_gate[cols, :])
            v = dot_nt(n2_s[...], w_up[cols, :])
            f_s[:, cols] = f.astype(BF16)
            v_s[:, cols] = v.astype(BF16)
            t_s[:, cols] = (f * jax.nn.sigmoid(f) * v).astype(BF16)

        chunks(t_s.shape[1], 256, up_chunk)
        save(f_s, 9)
        save(v_s, 10)
        wait_weight(layer, 7)

        def down_chunk(at_col, size):
            part_s[layer, 1, :, pl.ds(at_col, size)] = dot_nn(t_s[...], w_down[:, pl.ds(at_col, size)]).astype(BF16)

        chunks(d, 256, down_chunk)
        s3 = scatter_start(at, part_s.at[layer, 1], got_s, head_send.at[layer, 2], head_recv.at[layer, 2])
        hooks["rs2"]()
        feed = scatter_sum(at, part_s.at[layer, 1], got_s, s3)
        xo_s[layer, at.mine] = jnp.where(my_valid, h_s[...] + feed, 0.0).astype(BF16)
        s4 = gather_start(at, xo_s.at[layer], head_send.at[layer, 3], head_recv.at[layer, 3])
        hooks["ag2"]()
        wait_recv(s4)
        for copy in keep:
            copy.wait()

        def finish():
            wait_send(s1 + s2 + s3 + s4)

            @pl.when(at.s + 1 < nz)
            def _():
                edge.wait_send()

            for k in range(1, nz):

                @pl.when(at.s + k < nz)
                def _(k=k):
                    state(k).wait_send()

        return finish

    def nothing():
        pass

    n2_copy = pltpu.make_async_copy(n2_s, gath_n2.at[at.s], io_sem.at[2])

    def ring_rest(ring):
        for k in range(3, nz - 1):
            ring.step(k)

    def n2_ready():
        n2_copy.start()

    x_copy.wait()
    finish_0 = layer_forward(
        0,
        x_s,
        dict(states=lambda: ring_g.step(1), rs1=nothing, ag1=nothing, n2=n2_ready, rs2=lambda: ring_g.step(2), ag2=nothing),
    )
    finish_0()
    n2_copy.wait()
    ring_rest(ring_g)
    ring_g.step(nz - 1)
    ring_n.step(0)

    def out_copy(layer):
        near = pltpu.make_async_copy(xo_s.at[layer], x_out.at[at.sec], io_sem.at[3])
        far = remote(xo_s.at[layer], x_out.at[at.sec], x_send.at[9], x_recv.at[9], core)
        return near, far

    def send_out(layer):
        near, far = out_copy(layer)

        @pl.when(at.sec == layer)
        def _():
            near.start()

        @pl.when(at.sec != layer)
        def _():
            far.start()

    send_out(0)
    n2_last = pltpu.make_async_copy(n2_s, n2_out, io_sem.at[4])
    finish_1 = layer_forward(
        1,
        xo_s.at[0],
        dict(states=lambda: ring_n.step(1), rs1=nothing, ag1=nothing, n2=n2_last.start, rs2=lambda: ring_n.step(2), ag2=nothing),
    )
    send_out(1)
    finish_1()
    ring_rest(ring_n)
    ring_n.step(nz - 1)
    n2_last.wait()
    ring_g.drain()
    ring_n.drain()
    near, far = out_copy(0)
    near.wait()
    far.wait_send()
    far.wait_recv()
    small_swap.wait_send()
    for here in range(2):

        @pl.when(at.sec == here)
        def _(here=here):
            for i in range(8):
                swap(here, i).wait_send()
                stash(1 - here, i).wait()


def bwd_kernel(dims, *refs):
    nz, nh, rows, heads = dims
    take = taker(refs)
    lens, inputs_grad, small_own, small_other, tables = take(5)
    own = take(8)
    other = take(8)
    saved = [take(SAVED), take(SAVED)]
    gath_g1, gath_n2_0, n2_1 = take(3)
    ig_o, gains_o, att_o = take(3)
    ffn_o = take(3)
    gath_n2_1, gath_g0 = take(2)
    a_mine, a_peer, a_land = take(3)
    wr_o = take(3)
    mats = take(5)
    keep_s = take(SAVED)
    (grad_s, part_s, got_s, dm_s, dh_s, dg_s, do_s, cx_s, dyx_s, ss, sr, st_s, da_s, db_s, dc_s, edge_s, dcat_s, ig_s) = take(18)
    gsum_s, gpeer_s, gtot_s, gz_s, gh_s = take(5)
    acc = take(3)
    wx_s = take(3)
    blk_n2, blk_g, n2t_s, gt_s = take(4)
    a_s, work_s = take(2)
    (w_sem, io_sem, keep_sem, e_send, e_recv, st_send, st_recv, head_send, head_recv, r_send, r_recv) = take(11)
    (wx_send, wx_recv, ap_send, ap_recv, l_send, l_recv, x_send, x_recv, gz_send, gz_recv, gh_send, gh_recv) = take(12)
    x_s, n1_s, qk_s, u_s, o_s, yx_s, sin_s, gb_s, h_s, f_s, v_s = keep_s
    df_s, dv_s = f_s, v_s
    at = Place(lens, nz, nh, rows)
    cat, w_out, w_gate, w_up, w_down = mats
    d = n1_s.shape[1]
    width, qk = heads * HD, heads * FEAT
    block = d // nz
    core = (1 - at.sec, at.s, at.h)
    slots = weight_slots(*mats, qk, width)

    def weight_start(layer, i):
        @pl.when(at.sec == layer)
        def _():
            pltpu.make_async_copy(own[i].at[0], slots[i], w_sem.at[i]).start()

        @pl.when(at.sec != layer)
        def _():
            pltpu.make_async_copy(other[i].at[0], slots[i], w_sem.at[i]).start()

    def weight_wait(i):
        pltpu.make_async_copy(own[i].at[0], slots[i], w_sem.at[i]).wait()

    def keep_copy(layer, i):
        return pltpu.make_async_copy(saved[layer][i], keep_s[i], keep_sem.at[i])

    ring_n = Ring(at, n2_1, gath_n2_1, r_send.at[0], r_recv.at[0])
    ring_g = Ring(at, ig_s.at[1], gath_g0, r_send.at[1], r_recv.at[1])
    line = [
        LineSum(at, a_mine.at[0], a_peer.at[0], a_land.at[0], work_s, io_sem.at[4], l_send.at[0], l_recv.at[0], ap_recv),
        LineSum(at, a_mine.at[1], a_peer.at[1], a_land.at[1], work_s, io_sem.at[4], l_send.at[1], l_recv.at[1], ap_recv),
    ]

    def piece(layer, i):
        which = order(at, i)
        if isinstance(i, int) and i == 0:
            n2_src = n2_1 if layer == 1 else gath_n2_0.at[at.s]
            g_src = inputs_grad.at[at.sec] if layer == 1 else ig_s.at[1]
        else:
            n2_src = (gath_n2_1 if layer == 1 else gath_n2_0).at[which]
            g_src = (gath_g1 if layer == 1 else gath_g0).at[which]
        loads = [pltpu.make_async_copy(n2_src, blk_n2, io_sem.at[0]), pltpu.make_async_copy(g_src, blk_g, io_sem.at[1])]
        for copy in loads:
            copy.start()
        for copy in loads:
            copy.wait()
        pos = which * rows + lax.broadcasted_iota(jnp.int32, (rows, 1), 0)
        blk_g[...] = jnp.where(pos < at.tot, blk_g[...].astype(F32), 0.0).astype(BF16)
        for part in range(nz):

            @pl.when(at.s == part)
            def _(part=part):
                n2t_s[...] = blk_n2[:, part * block : (part + 1) * block].T
                gt_s[...] = blk_g[:, part * block : (part + 1) * block].T

        def hidden(at_row, size):
            cols = pl.ds(at_row, size)
            f = dot_nt(blk_n2[...], w_gate[cols, :])
            v = dot_nt(blk_n2[...], w_up[cols, :])
            dt = dot_nt(blk_g[...], w_down[cols, :])
            sig = jax.nn.sigmoid(f)
            act = f * sig
            t = (act * v).astype(BF16)
            df = (dt * v * (sig + act * (1.0 - sig))).astype(BF16)
            dv = (dt * act).astype(BF16)
            parts = (dot_nn(n2t_s[...], df), dot_nn(n2t_s[...], dv), dot_nn(gt_s[...], t))
            for total, new in zip(acc, parts):
                if isinstance(i, int) and i == 0:
                    total[:, cols] = new
                else:
                    total[:, cols] += new

        chunks(w_gate.shape[0], 640, hidden)

    def ffn_swap(i):
        return remote(wx_s[i], wr_o[i], wx_send.at[i], wx_recv.at[i], core)

    def ffn_send(layer):
        @pl.when(at.sec != layer)
        def _():
            for i in range(3):
                wx_s[i][...] = acc[i][...].astype(BF16)
                ffn_swap(i).start()

    def ffn_take(layer):
        @pl.when(at.sec == layer)
        def _():
            copies = []
            if layer == 0:
                for i in range(3):
                    ffn_swap(i).wait_send()
            loads = [pltpu.make_async_copy(wr_o[i], wx_s[i], io_sem.at[9 + i]) for i in range(3)]
            for i in range(3):
                ffn_swap(i).wait_recv()
                loads[i].start()
            for i in range(3):
                loads[i].wait()
                acc[i][...] += wx_s[i][...].astype(F32)
                copy = pltpu.make_async_copy(acc[i], ffn_o[i], io_sem.at[5 + i])
                copy.start()
                copies.append(copy)
            for copy in copies:
                copy.wait()

    def ig_copy(layer):
        near = pltpu.make_async_copy(ig_s.at[layer], ig_o.at[at.sec], io_sem.at[3])
        far = remote(ig_s.at[layer], ig_o.at[at.sec], x_send.at[0], x_recv.at[0], core)
        return near, far

    def ig_send(layer):
        near, far = ig_copy(layer)

        @pl.when(at.sec == layer)
        def _():
            near.start()

        @pl.when(at.sec != layer)
        def _():
            far.start()

    allowed = at.allowed()
    applies, tail, mine_last = at.applies(), at.tail(), at.last_seg(at.s)
    valid = at.pos() < at.tot
    lane = lax.broadcasted_iota(jnp.int32, (rows, LANES), 1)

    def peer_chunk(layer, i):
        return remote(a_s.at[i], a_peer.at[layer, i], ap_send.at[i], ap_recv.at[i], core)

    def mine_chunk(layer, i):
        return pltpu.make_async_copy(a_s.at[i], a_mine.at[layer, i], ap_send.at[i])

    def mixer_grads(layer):
        for i in range(nz):
            cols = slice(i * block, (i + 1) * block)
            a_s[i, :, 0 : 2 * qk + 2 * width] = dot_tn(n1_s[:, cols], dcat_s[...]).astype(BF16)
            a_s[i, :, 2 * qk + 2 * width :] = dot_tn(dm_s[:, cols], gb_s[...]).astype(BF16)

            @pl.when(at.sec != layer)
            def _(i=i):
                peer_chunk(layer, i).start()

            @pl.when(at.sec == layer)
            def _(i=i):
                mine_chunk(layer, i).start()

    def mixer_sent(layer):
        for i in range(nz):

            @pl.when(at.sec != layer)
            def _(i=i):
                peer_chunk(layer, i).wait_send()

            @pl.when(at.sec == layer)
            def _(i=i):
                mine_chunk(layer, i).wait()

    def layer_backward(layer, hooks):
        small = jnp.where(at.sec == layer, small_own[...], small_other[...])
        gain_attn, gain_ffn, taps = small[0:1], small[1:2], small[2 : 2 + KW]
        hooks["begin"]()

        weight_wait(7)
        keep_copy(layer, 9).wait()
        keep_copy(layer, 10).wait()

        def down_chunk(at_row, size):
            cols = pl.ds(at_row, size)
            dt = dot_nt(grad_s[...], w_down[cols, :])
            f = f_s[:, cols].astype(F32)
            v = v_s[:, cols].astype(F32)
            sig = jax.nn.sigmoid(f)
            df_s[:, cols] = (dt * v * sig * (1.0 + f * (1.0 - sig))).astype(BF16)
            dv_s[:, cols] = (dt * f * sig).astype(BF16)

        chunks(df_s.shape[1], 256, down_chunk)
        weight_wait(5)
        weight_wait(6)

        def up_chunk(at_col, size):
            cols = pl.ds(at_col, size)
            part = dot_nn(df_s[...], w_gate[:, cols]) + dot_nn(dv_s[...], w_up[:, cols])
            part_s[0, :, cols] = part.astype(BF16)

        chunks(d, 256, up_chunk)
        s1 = scatter_start(at, part_s.at[0], got_s, head_send.at[layer, 0], head_recv.at[layer, 0])
        hooks["rs1"]()
        keep_copy(layer, 8).wait()
        dn2 = scatter_sum(at, part_s.at[0], got_s, s1)
        back, gain_grad = norm_rows_back(h_s[...], gain_ffn, dn2)
        gsum_s[layer, 1:2, :] = gain_grad
        dh = grad_s[at.mine].astype(F32) + back
        dh_s[...] = dh
        dm_s[at.mine] = dh.astype(BF16)
        s2 = gather_start(at, dm_s, head_send.at[layer, 1], head_recv.at[layer, 1])
        for i in range(8):
            keep_copy(layer, i).wait()
        for i in (4, 0, 1, 2, 3):
            weight_wait(i)
        convolve(at, u_s, taps, do_s, cx_s, heads)
        a_low, b_low = qk_s[:, 0:qk], qk_s[:, qk : 2 * qk]
        hooks["ag1"]()
        wait_recv(s2)

        def out_chunk(at_row, size):
            cols = pl.ds(at_row, size)
            dg_s[:, cols] = dot_nt(dm_s[...], w_out[cols, :])

        chunks(width, 256, out_chunk)
        for head in range(heads):
            cols = slice(head * HD, head * HD + LANES)
            gate, dg, yx = o_s[:, cols], dg_s[:, cols], yx_s[head]
            sig = jax.nn.sigmoid(gate)
            inverse = 1.0 / yx[:, HD : HD + 1]
            y = yx * inverse
            do_s[:, cols] = dg * y * sig * (1.0 + gate * (1.0 - sig))
            dy = jnp.where(lane < HD, dg * gate * sig, 0.0)
            dden = -jnp.sum(dy * y, axis=1, keepdims=True) * inverse
            dyx_s[head] = jnp.where(lane == HD, dden, dy * inverse).astype(BF16)
            one, two = lift_parts(a_low, tables, 1, head)
            psi = jnp.where(applies, one * two, 0.0).astype(BF16)
            ss[layer, head] = dot_tn(psi, dyx_s[head])[:PSI_SENT].astype(BF16)

        def state(k):
            return remote(
                ss.at[layer], sr.at[layer, at.s], st_send.at[layer, k - 1], st_recv.at[layer, at.s],
                (at.sec, lax.rem(at.s + nz - k, nz), at.h),
            )

        for k in range(1, nz):

            @pl.when(at.s - k >= 0)
            def _(k=k):
                state(k).start()

        da_s[...] = jnp.zeros_like(da_s)
        db_s[...] = jnp.zeros_like(db_s)
        for head in range(heads):
            a_own, b_own = head_only(a_low, head), head_only(b_low, head)
            e = dot_nt(a_low, b_own)
            kern = jnp.where(allowed, 1.0 + e + 0.5 * e * e, 0.0).astype(BF16)
            dkern = dot_nt(dyx_s[head], cx_s[head])
            de = jnp.where(allowed, dkern * (1.0 + e), 0.0).astype(BF16)
            one, two = lift_parts(a_low, tables, 1, head)
            dpsi = jnp.where(applies, dot_nt(dyx_s[head], sin_s[head]), 0.0)
            pcols = slice(head * PSI, (head + 1) * PSI)
            da_s[...] += (
                dot_nn(de, b_own)
                + dot_nt((dpsi * two).astype(BF16), tables[0, :, pcols])
                + dot_nt((dpsi * one).astype(BF16), tables[1, :, pcols])
            )
            db_s[...] += dot_tn(de, a_own)
            yx_s[head] = dot_tn(kern, dyx_s[head])
        for j in range(1, nz):

            @pl.when(j > at.s)
            def _(j=j):
                remote(ss.at[layer], sr.at[layer, j], st_send.at[layer, 0], st_recv.at[layer, j], core).wait_recv()

        hooks["states"]()
        st_s[...] = jnp.zeros_like(st_s)
        for head in range(heads):
            total = jnp.zeros((PSI_SENT, LANES), F32)
            for j in range(1, nz):
                counts = (j > at.s) & (at.prior_seg(j) == mine_last)
                total = total + jnp.where(counts, sr[layer, j, head].astype(F32), 0.0)
            st_s[head, 0:PSI_SENT] = total.astype(BF16)
            one, two = lift_parts(b_low, tables, 2, head)
            psi = (one * two).astype(BF16)
            dpsi = jnp.where(tail, dot_nt(cx_s[head], st_s[head]), 0.0)
            pcols = slice(head * PSI, (head + 1) * PSI)
            db_s[...] += dot_nt((dpsi * two).astype(BF16), tables[0, :, pcols]) + dot_nt(
                (dpsi * one).astype(BF16), tables[2, :, pcols]
            )
            dc = yx_s[head] + jnp.where(tail, dot_nn(psi, st_s[head]), 0.0)
            dc_s[0:rows, head * HD : head * HD + LANES] = dc
        edge = remote(
            dc_s.at[pl.ds(0, 8)], edge_s.at[layer], e_send.at[layer], e_recv.at[layer],
            (at.sec, lax.rem(at.s + nz - 1, nz), at.h),
        )

        @pl.when(at.s > 0)
        def _():
            edge.start()

        dcat_s[:, 0:qk] = (da_s[...] * 0.5).astype(BF16)
        dcat_s[:, qk : 2 * qk] = (db_s[...] * 0.5).astype(BF16)
        dcat_s[:, 2 * qk + width :] = do_s[:, :width].astype(BF16)
        gsum_s[layer, 2:8, :] = jnp.zeros((6, d), F32)
        for j in range(KW):
            product = dc_s[0:rows, :width] * u_s[8 - j : 8 - j + rows, :width]
            gsum_s[layer, 2 + j : 3 + j, :width] = jnp.sum(jnp.where(at.same(-j), product, 0.0), axis=0, keepdims=True)

        @pl.when(at.s + 1 < nz)
        def _():
            edge.wait_recv()

        dc_s[rows : rows + 8, :] = edge_s[layer]
        du = taps[0:1, :width] * dc_s[0:rows, :width]
        for j in range(1, KW):
            du = du + jnp.where(at.same(j), dc_s[j : j + rows, :width] * taps[j : j + 1, :width], 0.0)
        dcat_s[:, 2 * qk : 2 * qk + width] = du.astype(BF16)

        def proj_chunk(at_col, size):
            cols = pl.ds(at_col, size)
            part_s[1, :, cols] = dot_nn(dcat_s[...], cat[:, cols]).astype(BF16)

        chunks(d, 256, proj_chunk)
        s3 = scatter_start(at, part_s.at[1], got_s, head_send.at[layer, 2], head_recv.at[layer, 2])
        mixer_grads(layer)
        hooks["rs2"]()
        dn1 = scatter_sum(at, part_s.at[1], got_s, s3)
        back, gain_grad = norm_rows_back(x_s[...].astype(F32), gain_attn, dn1)
        gsum_s[layer, 0:1, :] = gain_grad
        ig_s[layer, at.mine] = (dh_s[...] + back).astype(BF16)
        s4 = gather_start(at, ig_s.at[layer], head_send.at[layer, 3], head_recv.at[layer, 3])
        hooks["ag2"]()
        wait_recv(s4)
        ig_send(layer)
        wait_send(s1 + s3)

        def finish():
            wait_send(s2 + s4)

            @pl.when(at.s > 0)
            def _():
                edge.wait_send()

            for k in range(1, nz):

                @pl.when(at.s - k >= 0)
                def _(k=k):
                    state(k).wait_send()

        return finish

    def rest(layer, ring):
        for k in range(3, min(nz, 4)):
            ring.step(k)
            piece(layer, k)

        def one(k, carry):
            ring.step(k)
            piece(layer, k)
            return carry

        if nz > 4:
            lax.fori_loop(4, nz, one, 0)

    def owner(layer, what):
        @pl.when(at.sec == layer)
        def _():
            what()

    g_copy = pltpu.make_async_copy(inputs_grad.at[at.sec], grad_s, io_sem.at[2])
    g_copy.start()
    for i in (7, 5, 6, 4, 0, 1, 2, 3):
        weight_start(1, i)
    for i in (9, 10, 8, 3, 2, 4, 5, 6, 7, 1, 0):
        keep_copy(1, i).start()
    at.barrier(True, True, True)
    ring_n.step(0)
    g_copy.wait()
    grad_s[...] = jnp.where(valid, grad_s[...].astype(F32), 0.0).astype(BF16)

    def b1_ag1():
        ring_n.step(1)
        piece(1, 1)

    def b1_ag2():
        for i in (4, 0, 1, 2, 3):
            weight_start(0, i)
        for i in (9, 10, 8, 3, 2, 4, 5, 6, 7, 1, 0):
            keep_copy(0, i).start()
        rest(1, ring_n)
        for i in (7, 5, 6):
            weight_start(0, i)
        ffn_send(1)

    def nothing():
        pass

    def b1_states():
        ring_n.step(2)

    def b1_rs2():
        piece(1, 2)

    finish_1 = layer_backward(
        1, dict(begin=nothing, rs1=lambda: piece(1, 0), ag1=b1_ag1, states=b1_states, rs2=b1_rs2, ag2=b1_ag2)
    )
    finish_1()
    grad_s[...] = jnp.where(valid, ig_s[1].astype(F32), 0.0).astype(BF16)

    def b0_begin():
        ring_g.step(0)
        mixer_sent(1)
        owner(1, lambda: line[1].slot(0))

    def b0_rs1():
        ffn_take(1)
        piece(0, 0)

    def b0_ag1():
        ring_g.step(1)
        piece(0, 1)

    def b0_states():
        ring_g.step(2)
        owner(1, lambda: line[1].slot(1))

    def b0_rs2():
        piece(0, 2)
        owner(1, lambda: line[1].slot(2))

    def b0_ag2():
        rest(0, ring_g)
        ffn_send(0)

    finish_0 = layer_backward(
        0, dict(begin=b0_begin, rs1=b0_rs1, ag1=b0_ag1, states=b0_states, rs2=b0_rs2, ag2=b0_ag2)
    )

    gain_swap = remote(gsum_s.at[1 - at.sec], gpeer_s, x_send.at[1], x_recv.at[1], core)
    gain_swap.start()

    def line_end(layer, begin):
        for i in range(begin, nz - 1):
            line[layer].slot(i)
        line[layer].last()
        copy = pltpu.make_async_copy(work_s.at[0], att_o, io_sem.at[8])
        copy.start()
        copy.wait()

    owner(1, lambda: line_end(1, 3))
    mixer_sent(0)
    gain_swap.wait_recv()
    gtot_s[0] = gsum_s[at.sec] + gpeer_s[...]

    def gain_seq(k):
        to = lax.rem(at.s + k, nz)
        return remote(gtot_s.at[0], gz_s.at[k - 1], gz_send.at[k - 1], gz_recv.at[k - 1], (at.sec, to, at.h))

    for k in range(1, nz):
        gain_seq(k).start()
    ffn_take(0)
    for k in range(1, nz):
        gain_seq(k).wait_recv()
    total = gtot_s[0]
    for k in range(1, nz):
        total = total + gz_s[k - 1]
    gtot_s[1] = total

    def gain_head(m):
        return remote(gtot_s.at[1], gh_s.at[m - 1], gh_send.at[m - 1], gh_recv.at[m - 1], (at.sec, at.s, at.h ^ m))

    for m in range(1, nh):
        gain_head(m).start()
    owner(0, lambda: line_end(0, 0))
    for m in range(1, nh):
        gain_head(m).wait_recv()
    total = gtot_s[1, 0:2]
    for m in range(1, nh):
        total = total + gh_s[m - 1, 0:2]
    gains_o[...] = gtot_s[1]
    gains_o[0:2, :] = total

    finish_0()
    ring_n.drain()
    ring_g.drain()
    gain_swap.wait_send()
    for k in range(1, nz):
        gain_seq(k).wait_send()
    for m in range(1, nh):
        gain_head(m).wait_send()
    owner(1, lambda: wait_send([ffn_swap(i) for i in range(3)]))
    near, far = ig_copy(0)
    near.wait()
    far.wait_send()
    far.wait_recv()


def shape(dims, kind=BF16):
    return jax.ShapeDtypeStruct(tuple(dims), kind)


ANY = pl.BlockSpec(memory_space=pl.ANY)
VM = pl.BlockSpec(memory_space=pltpu.VMEM)
SM = pl.BlockSpec(memory_space=pltpu.SMEM)
DMA = pltpu.SemaphoreType.DMA


def params(number):
    return pltpu.CompilerParams(collective_id=number, has_side_effects=True, vmem_limit_bytes=VMEM_LIMIT)


def shards(nz, nh, inputs, out_grad, lengths, norm_attn, norm_ffn, w_query, w_key, w_value, w_output_gate, conv_kernel, w_out, w_gate, w_up, w_down):
    micro, rows, d = inputs.shape
    heads = w_query.shape[2] // FEAT
    width, qk, ff = w_value.shape[2], w_query.shape[2], w_gate.shape[2]
    part, block = rows // nh, d // nz
    dims = (nz, nh, rows, heads)
    wide = -(-((heads - 1) * HD + LANES) // LANES) * LANES
    total = 2 * qk + 3 * width
    tables = jnp.asarray(lift_tables(heads), BF16)
    turned = [jnp.swapaxes(w, 1, 2) for w in (w_query, w_key, w_value, w_output_gate)]
    own = (*turned, w_out, jnp.swapaxes(w_gate, 1, 2), jnp.swapaxes(w_up, 1, 2), w_down)
    small_own = jnp.concatenate(
        [norm_attn, norm_ffn, jnp.pad(conv_kernel[0], ((0, 0), (0, d - width))), jnp.zeros((3, d), F32)]
    )

    def vm(dims, kind=BF16):
        return pltpu.VMEM(tuple(dims), kind)

    mats = [vm((2 * qk + 2 * width, d)), vm((width, d)), vm((ff, d)), vm((ff, d)), vm((ff, d))]
    act = vm((rows, d))
    kept = [
        ((part, d), BF16),
        ((rows, d), BF16),
        ((rows, 2 * qk), BF16),
        ((rows + 8, wide), F32),
        ((rows, wide), F32),
        ((heads, rows, LANES), F32),
        ((heads, PSI, LANES), BF16),
        ((rows, width), BF16),
        ((part, d), F32),
        ((rows, ff), BF16),
        ((rows, ff), BF16),
    ]
    keep_shapes = [shape(*k) for k in kept]
    gathered = shape((nz, rows, d))
    outs = (
        [shape((8, d), F32)]
        + [shape(w.shape) for w in own]
        + keep_shapes * 2
        + [shape((micro, rows, d)), gathered, gathered, shape((rows, d))]
    )
    scratch = (
        mats
        + mats
        + [
            act,
            act,
            act,
            vm((rows, 2 * qk)),
            vm((rows + 8, wide), F32),
            vm((2, 8, wide), F32),
            vm((rows, wide), F32),
            vm((rows, wide), F32),
            vm((heads, rows, LANES)),
            vm((heads, rows, LANES), F32),
            vm((2, heads, PSI_SENT, LANES)),
            vm((2, nz, heads, PSI_SENT, LANES)),
            vm((heads, PSI, LANES)),
            vm((rows, wide), F32),
            vm((rows, width)),
            vm((2, 2, rows, d)),
            vm((nh - 1, part, d)),
            vm((rows, ff)),
            vm((rows, ff)),
            vm((rows, ff)),
            vm((2, rows, d)),
            vm((part, d), F32),
            vm((8, d), F32),
            DMA((16,)),
            DMA((5,)),
            DMA((SAVED,)),
            DMA((10,)),
            DMA((10,)),
            DMA((2,)),
            DMA((2,)),
            DMA((2, nz)),
            DMA((2, nz)),
            DMA((2, 4, nh - 1)),
            DMA((2, 4, nh - 1)),
            DMA((2, 2, nz - 1)),
            DMA((2, 2, nz - 1)),
        ]
    )
    first = pl.pallas_call(
        functools.partial(fwd_kernel, dims),
        out_shape=outs,
        in_specs=[SM, ANY, ANY, VM, VM] + [ANY] * 8,
        out_specs=[ANY] * len(outs),
        scratch_shapes=scratch,
        compiler_params=params(0),
    )(lengths, inputs, out_grad, small_own, tables, *own)
    small_other, other = first[0], first[1:9]
    saved = first[9 : 9 + 2 * SAVED]
    section_out, gath_g1, gath_n2_0, n2_1 = first[9 + 2 * SAVED :]

    outs = (
        [shape((micro, rows, d)), shape((8, d), F32), shape((block, total))]
        + [shape((block, ff), F32)] * 3
        + [gathered, gathered]
        + [shape((2, nz, block, total)), shape((2, nz, block, total)), shape((2, 2, nz, block, total))]
        + [shape((block, ff))] * 3
    )
    out_specs = [ANY, VM] + [ANY] * (len(outs) - 2)
    scratch = (
        mats
        + [vm(*k) for k in kept]
        + [
            act,
            vm((2, rows, d)),
            vm((nh - 1, part, d)),
            act,
            vm((part, d), F32),
            vm((rows, wide), F32),
            vm((rows, wide), F32),
            vm((heads, rows, LANES)),
            vm((heads, rows, LANES)),
            vm((2, heads, PSI_SENT, LANES)),
            vm((2, nz, heads, PSI_SENT, LANES)),
            vm((heads, PSI, LANES)),
            vm((rows, qk), F32),
            vm((rows, qk), F32),
            vm((rows + 8, wide), F32),
            vm((2, 8, wide), F32),
            vm((rows, 2 * qk + 2 * width)),
            vm((2, rows, d)),
            vm((2, 8, d), F32),
            vm((8, d), F32),
            vm((2, 8, d), F32),
            vm((nz - 1, 8, d), F32),
            vm((nh - 1, 8, d), F32),
        ]
        + [vm((block, ff), F32)] * 3
        + [vm((block, ff))] * 3
        + [act, act, vm((block, rows)), vm((block, rows)), vm((nz, block, total)), vm((3, block, total))]
        + [
            DMA((8,)),
            DMA((12,)),
            DMA((SAVED,)),
            DMA((2,)),
            DMA((2,)),
            DMA((2, nz)),
            DMA((2, nz)),
            DMA((2, 4, nh - 1)),
            DMA((2, 4, nh - 1)),
            DMA((2, 2, nz - 1)),
            DMA((2, 2, nz - 1)),
            DMA((3,)),
            DMA((3,)),
            DMA((nz,)),
            DMA((nz,)),
            DMA((2, 2, nz)),
            DMA((2, 2, nz)),
            DMA((2,)),
            DMA((2,)),
            DMA((nz - 1,)),
            DMA((nz - 1,)),
            DMA((nh - 1,)),
            DMA((nh - 1,)),
        ]
    )
    second = pl.pallas_call(
        functools.partial(bwd_kernel, dims),
        out_shape=outs,
        in_specs=[SM, ANY, VM, VM, VM] + [ANY] * (16 + 2 * SAVED + 3),
        out_specs=out_specs,
        scratch_shapes=scratch,
        compiler_params=params(1),
    )(lengths, out_grad, small_own, small_other, tables, *own, *other, *saved, gath_g1, gath_n2_0, n2_1)
    input_grad, gains, att, g_gate, g_up, g_down = second[:6]
    att = att.astype(F32)
    return (
        section_out[None],
        input_grad[None],
        gains[0:1],
        gains[1:2],
        att[None, :, 0:qk],
        att[None, :, qk : 2 * qk],
        att[None, :, 2 * qk : 2 * qk + width],
        att[None, :, 2 * qk + width : 2 * qk + 2 * width],
        gains[None, 2 : 2 + KW, :width],
        att[:, 2 * qk + 2 * width :].T[None],
        g_gate[None],
        g_up[None],
        g_down.T[None],
    )


def solution(mesh):
    return jax.shard_map(
        functools.partial(shards, mesh.shape["seq"], mesh.shape["head"]),
        mesh=mesh,
        in_specs=(
            P(None, "seq", None),
            P(None, "seq", None),
            P(),
            P("section", None),
            P("section", None),
            P("section", None, "head"),
            P("section", None, "head"),
            P("section", None, "head"),
            P("section", None, "head"),
            P("section", None, "head"),
            P("section", "head", None),
            P("section", None, "head"),
            P("section", None, "head"),
            P("section", "head", None),
        ),
        out_specs=(
            P("section", None, "seq", None),
            P("section", None, "seq", None),
            P("section", None),
            P("section", None),
            P("section", "seq", "head"),
            P("section", "seq", "head"),
            P("section", "seq", "head"),
            P("section", "seq", "head"),
            P("section", None, "head"),
            P("section", "head", "seq"),
            P("section", "seq", "head"),
            P("section", "seq", "head"),
            P("section", "head", "seq"),
        ),
        check_vma=False,
    )
```

time: 1900 us -> 493 us (0.26)
  waiting for transfers between devices: 771 us -> 0 us
  Pallas kernels: 0 us -> 463 us
  blocking collectives: 358 us -> 0 us
  matrix products: 288 us -> 0 us
  local copies, waits for them, and re-layouts: 217 us -> 20.6 us
  other arithmetic: 162 us -> 3.07 us
  between operations: 43 us -> 0.92 us
  starting transfers between devices: 40.3 us -> 0 us
    psum x11 -> x0, waiting for transfers between devices: 528 us -> none  [the longest x3 181 us: layer_grads(): lax.psum(partial_two.astype(jnp.bfloat16), 'head').astype(jnp.float32)]
    pallas_call x0 -> x2, Pallas kernels: none -> 463 us  [the longest x1 293 us: shards(): pl.pallas_call(functools.partial(bwd_kernel, dims), out_shape=outs, in_sp...]
    all_gather x18 -> x0, blocking collectives: 327 us -> none  [the longest x12 218 us: carried_in(): lax.all_gather(a.astype(kind), axis)]
    dot_general x153 -> x0, matrix products: 288 us -> none  [the longest x42 95 us: project(): return jnp.dot(left_arr, right_arr, preferred_element_type=jnp.float32)]
    unnamed x27 -> x0, waiting for transfers between devices: 243 us -> none
    unnamed x842 -> x20, local copies, waits for them, and re-layouts: 202 us -> 16.2 us
    select_n x41 -> x0, other arithmetic: 62.6 us -> none  [the longest x24 42.4 us: hop(): return jax.tree.map(lambda a, b: jnp.where(reached, a, b), new, before)]
    ppermute x13 -> x0, starting transfers between devices: 37.8 us -> none  [from_behind(): lax.ppermute(value, axis, [(source, source + steps) for source in range(i...]
  transfers between devices with their start and end apart: 32 -> 0, of which waited for: 14 -> 0; matrix products, arithmetic and copies ran while one was open for 19% -> 0% of each run, Pallas kernels for 0% -> 0%
where the time goes in v2:
time: 493 us; the launch traced here: 487 us
  Pallas kernels  463 us (94%)
  local copies, waits for them, and re-layouts  20.6 us (4%)
    pallas_call x1, Pallas kernels, shards(): pl.pallas_call(functools.partial(bwd_kernel, dims), out_shape=outs, in_sp...  293 us
    pallas_call x1, Pallas kernels, shards(): pl.pallas_call(functools.partial(fwd_kernel, dims), out_shape=outs, in_sp...  170 us
    unnamed x20, local copies, waits for them, and re-layouts  16.2 us

profile of v2, /device:TPU:0, one launch (start us, length us, event | category | flops | bytes accessed | tf_op | source)
XLA Modules:
  0.0 487.4 jit_solution(17324823000755819981)
XLA Ops:
  0.7 0.1 pad.8.clone
  0.7 0.7 copy.34
  1.4 1.4 fusion.refs_3_.refs_2_
  2.8 169.8 %shard_map.246 = (f32[8,1792]{1,0:T(8,128)}, bf16[1,64,1792]{2,1,0:T(8,128)(2,1)}, bf16[1,64,1792]{2,1,0:T(8,128)(2,1)}, bf16[1,448,1792]{2,1,0:T(8,128)(2,1)}, ...) custom-call(s32[2,2]{1,0:T(2,128)} %refs_0_.3, ...), custom_call_target="tpu_custom_call" | custom-call | tf_op jit(solution)/shard_map/pallas_call | solution.py:1243
  172.7 293.0 %shard_map.247 = (bf16[2,256,1792]{2,1,0:T(8,128)(2,1)}, f32[8,1792]{1,0:T(8,128)}, bf16[448,1472]{1,0:T(8,128)(2,1)}, f32[448,1216]{1,0:T(8,128)}, f32[448,1216...) custom-call(s32[2,2]{1,0:T(2,128)} %refs_0_.3, ...), custom_call_target="tpu_custom_call" | custom-call | tf_op jit(solution)/shard_map/pallas_call | solution.py:1320
  465.7 0.7 slice_bitcast_fusion.5
  466.4 1.5 fusion.2
  467.9 0.6 copy.30
  468.5 1.7 convert_element_type.5
  470.2 0.1 slice_bitcast_fusion.3
  470.3 0.8 copy.29
  471.1 1.9 slice_bitcast_fusion
  473.0 0.0 copy-start.3
  473.0 2.6 copy.31
  475.6 0.8 copy.28
  476.3 0.0 copy-done.3
  476.3 0.0 copy-start.4
  476.3 1.2 copy.40
  477.6 0.9 copy-done.4
  478.5 0.0 copy-start.2
  478.5 1.2 copy.41
  479.7 1.1 copy-done.2
  480.8 0.0 copy-start.1
  480.8 1.4 copy.42
  482.2 1.1 copy-done.1
  483.3 0.0 copy-start
  483.3 1.4 copy.43
  484.7 1.1 copy-done
  485.8 1.4 copy.44
  (1 shorter events, 0.0 us)
Async XLA Ops:
  473.0 3.3 copy-start.3
  476.3 2.2 copy-start.4
  478.5 2.3 copy-start.2
  480.8 2.5 copy-start.1
  483.3 2.5 copy-start

commit v3 on v2

--- a/solution.py
+++ b/solution.py
@@ -127,12 +127,21 @@
     )
 
 
-def scatter_start(at, buf, got, send, recv):
+def half_cols(buf, half):
+    size = buf.shape[-1] // 2
+    return pl.ds(half * size, size)
+
+
+def scatter_start(at, buf, got, send, recv, half):
     sent = []
+    cols = half_cols(buf, half)
     for m in sorted(range(1, at.nh), reverse=True):
         peer = at.h ^ m
         rows = pl.ds(pl.multiple_of(peer * at.part, at.part), at.part)
-        copy = remote(buf.at[rows], got.at[m - 1], send.at[m - 1], recv.at[m - 1], (at.sec, at.s, peer))
+        sem = half * (at.nh - 1) + m - 1
+        copy = remote(
+            buf.at[rows, cols], got.at[m - 1, :, cols], send.at[sem], recv.at[sem], (at.sec, at.s, peer)
+        )
         copy.start()
         sent.append(copy)
     return sent
@@ -216,45 +225,97 @@
 
 
 class Ring:
-    def __init__(self, at, src, dst, send, recv):
+    def __init__(self, at, src, dst, send, recv, pair_send, pair_recv):
         self.at, self.src, self.dst, self.send, self.recv = at, src, dst, send, recv
-
-    def _copy(self, way, k, block, first):
+        self.pair_send, self.pair_recv = pair_send, pair_recv
+
+    def _view(self, c):
         at = self.at
-        to = lax.rem(at.s + (1 if way == 0 else at.nz - 1), at.nz)
-        src = self.src if first else self.dst.at[block]
-        return remote(src, self.dst.at[block], self.send.at[way, k], self.recv.at[way, k], (at.sec, to, at.h))
+        rows, cols = at.rows // 2, self.dst.shape[-1] // 2
+        bit = lax.rem(at.h // (1 << c), 2)
+        return pl.ds(pl.multiple_of(bit * rows, rows), rows), pl.ds(c * cols, cols)
+
+    def _ways(self, k):
+        at = self.at
+        right = (at.s - k, at.s - k >= 0, at.s + 1 < at.nz, lax.rem(at.s + 1, at.nz))
+        left = (at.s + k, at.s + k < at.nz, at.s > 0, lax.rem(at.s + at.nz - 1, at.nz))
+        return right, left
+
+    def _copies(self, way, k, block, to, first):
+        at = self.at
+        for c in range(2):
+            rows, cols = self._view(c)
+            src = self.src.at[rows, cols] if first else self.dst.at[block, rows, cols]
+            yield remote(
+                src, self.dst.at[block, rows, cols], self.send.at[way, k, c], self.recv.at[way, k, c], (at.sec, to, at.h)
+            )
+
+    def _pairs(self, way, k, block):
+        at = self.at
+        for c in range(2):
+            rows, cols = self._view(c)
+            view = self.dst.at[block, rows, cols]
+            yield remote(view, view, self.pair_send.at[way, k, c], self.pair_recv.at[way, k, c], (at.sec, at.s, at.h ^ (1 << c)))
 
     def step(self, k):
         at = self.at
         first = isinstance(k, int) and k == 0
-        for way in range(2):
-            block = at.s - k if way == 0 else at.s + k
-            there = block >= 0 if way == 0 else block < at.nz
-            onward = at.s + 1 < at.nz if way == 0 else at.s > 0
+        for way, (block, there, onward, to) in enumerate(self._ways(k)):
             if not first:
 
                 @pl.when(there)
-                def _(way=way, block=block):
-                    self._copy(way, k - 1, block, False).wait_recv()
+                def _(way=way, block=block, to=to):
+                    wait_recv(self._copies(way, k - 1, block, to, False))
 
             if not isinstance(k, int) or k < at.nz - 1:
 
                 @pl.when(there & onward & (k < at.nz - 1))
-                def _(way=way, block=block):
-                    self._copy(way, k, block, first).start()
+                def _(way=way, block=block, to=to):
+                    for copy in self._copies(way, k, block, to, first):
+                        copy.start()
+
+    def pair(self, k):
+        for way, (block, there, _, _) in enumerate(self._ways(k + 1)):
+
+            @pl.when(there)
+            def _(way=way, block=block):
+                for copy in self._pairs(way, k, block):
+                    copy.start()
+
+    def ready(self, k):
+        for way, (block, there, _, _) in enumerate(self._ways(k + 1)):
+
+            @pl.when(there)
+            def _(way=way, block=block):
+                wait_recv(self._pairs(way, k, block))
 
     def drain(self):
-        at = self.at
-        for k in range(at.nz - 1):
-            for way in range(2):
-                block = at.s - k if way == 0 else at.s + k
-                there = block >= 0 if way == 0 else block < at.nz
-                onward = at.s + 1 < at.nz if way == 0 else at.s > 0
+        def one(k, carry):
+            for way, (_, there, onward, to) in enumerate(self._ways(k)):
 
                 @pl.when(there & onward)
-                def _(way=way, k=k):
-                    self._copy(way, k, at.s, True).wait_send()
+                def _(way=way, to=to):
+                    wait_send(self._copies(way, k, self.at.s, to, False))
+
+            for way, (_, there, _, _) in enumerate(self._ways(k + 1)):
+
+                @pl.when(there)
+                def _(way=way):
+                    wait_send(self._pairs(way, k, self.at.s))
+
+            return carry
+
+        lax.fori_loop(0, self.at.nz - 1, one, 0)
+
+
+def upward(begin, end, body):
+    if end > begin:
+
+        def one(k, carry):
+            body(k)
+            return carry
+
+        lax.fori_loop(begin, end, one, 0)
 
 
 class LineSum:
@@ -278,9 +339,9 @@
 
     def _own(self, slot, d):
         at = self.at
-        self._load(self.mine.at[d], slot)
         remote(self.mine.at[d], self.peer.at[d], self.peer_recv.at[d], self.peer_recv.at[d], (1 - at.sec, at.s, at.h)).wait_recv()
-        self._add(slot, self.peer.at[d])
+        self._load(self.peer.at[d], 2)
+        self.work[slot] = (self.mine[d].astype(F32) + self.work[2].astype(F32)).astype(BF16)
 
     def slot(self, i):
         at = self.at
@@ -361,7 +422,8 @@
     x_out, gath_g1, gath_n2, n2_out = take(4)
     mats = [take(5), take(5)]
     (x_s, n1_s, n2_s, qk_s, u_s, edge_s, o_s, c_s, cx_s, yx_s, ss, sr, sin_s, g_s, gb_s, part_s, got_s, f_s, v_s, t_s, xo_s, h_s, sm_s) = take(23)
-    w_sem, io_sem, save_sem, x_send, x_recv, e_send, e_recv, st_send, st_recv, head_send, head_recv, r_send, r_recv = take(13)
+    w_sem, io_sem, save_sem, x_send, x_recv, e_send, e_recv, st_send, st_recv, head_send, head_recv = take(11)
+    r_send, r_recv, p_send, p_recv = take(4)
     at = Place(lens, nz, nh, rows)
     d = x_s.shape[1]
     width, qk = heads * HD, heads * FEAT
@@ -397,8 +459,8 @@
             for i in (2, 0, 1, 3, 4, 5, 6, 7):
                 swap(here, i).start()
 
-    ring_g = Ring(at, out_grad.at[at.sec], gath_g1, r_send.at[0], r_recv.at[0])
-    ring_n = Ring(at, gath_n2.at[at.s], gath_n2, r_send.at[1], r_recv.at[1])
+    ring_g = Ring(at, out_grad.at[at.sec], gath_g1, r_send.at[0], r_recv.at[0], p_send.at[0], p_recv.at[0])
+    ring_n = Ring(at, gath_n2.at[at.s], gath_n2, r_send.at[1], r_recv.at[1], p_send.at[1], p_recv.at[1])
     ring_g.step(0)
     small_swap.wait_recv()
     small_copy = pltpu.make_async_copy(small_other, sm_s, io_sem.at[1])
@@ -431,6 +493,7 @@
             copy.start()
             keep.append(copy)
 
+        hooks["begin"]()
         n1_s[...] = norm_rows(x_s[...].astype(F32), gain_attn).astype(BF16)
         save(x_s.at[at.mine], 0)
         save(n1_s, 1)
@@ -512,11 +575,11 @@
 
         wait_weight(layer, 4)
 
-        def mix_chunk(at_col, size):
-            part_s[layer, 0, :, pl.ds(at_col, size)] = dot_nn(gb_s[...], w_out[:, pl.ds(at_col, size)]).astype(BF16)
-
-        chunks(d, 256, mix_chunk)
-        s1 = scatter_start(at, part_s.at[layer, 0], got_s, head_send.at[layer, 0], head_recv.at[layer, 0])
+        s1 = []
+        for half in range(2):
+            cols = half_cols(w_out, half)
+            part_s[layer, 0, :, cols] = dot_nn(gb_s[...], w_out[:, cols]).astype(BF16)
+            s1 += scatter_start(at, part_s.at[layer, 0], got_s, head_send.at[layer, 0], head_recv.at[layer, 0], half)
         hooks["rs1"]()
         hidden = x_s[at.mine].astype(F32) + scatter_sum(at, part_s.at[layer, 0], got_s, s1)
         h_s[...] = hidden
@@ -543,11 +606,11 @@
         save(v_s, 10)
         wait_weight(layer, 7)
 
-        def down_chunk(at_col, size):
-            part_s[layer, 1, :, pl.ds(at_col, size)] = dot_nn(t_s[...], w_down[:, pl.ds(at_col, size)]).astype(BF16)
-
-        chunks(d, 256, down_chunk)
-        s3 = scatter_start(at, part_s.at[layer, 1], got_s, head_send.at[layer, 2], head_recv.at[layer, 2])
+        s3 = []
+        for half in range(2):
+            cols = half_cols(w_down, half)
+            part_s[layer, 1, :, cols] = dot_nn(t_s[...], w_down[:, cols]).astype(BF16)
+            s3 += scatter_start(at, part_s.at[layer, 1], got_s, head_send.at[layer, 2], head_recv.at[layer, 2], half)
         hooks["rs2"]()
         feed = scatter_sum(at, part_s.at[layer, 1], got_s, s3)
         xo_s[layer, at.mine] = jnp.where(my_valid, h_s[...] + feed, 0.0).astype(BF16)
@@ -577,24 +640,35 @@
 
     n2_copy = pltpu.make_async_copy(n2_s, gath_n2.at[at.s], io_sem.at[2])
 
-    def ring_rest(ring):
-        for k in range(3, nz - 1):
-            ring.step(k)
-
     def n2_ready():
         n2_copy.start()
+        ring_g.step(2)
+
+    def f0_rs2():
+        n2_copy.wait()
+        ring_n.step(0)
+
+    def f1_begin():
+        upward(3, nz, ring_g.step)
+        upward(0, nz - 1, ring_g.pair)
+        ring_n.step(1)
+
+    def f1_states():
+        ring_n.pair(0)
+
+    def f1_rs1():
+        ring_n.step(2)
+
+    def f1_n2():
+        n2_last.start()
+        upward(3, nz, ring_n.step)
+        upward(1, nz - 1, ring_n.pair)
 
     x_copy.wait()
     finish_0 = layer_forward(
-        0,
-        x_s,
-        dict(states=lambda: ring_g.step(1), rs1=nothing, ag1=nothing, n2=n2_ready, rs2=lambda: ring_g.step(2), ag2=nothing),
+        0, x_s, dict(begin=nothing, states=nothing, rs1=lambda: ring_g.step(1), ag1=nothing, n2=n2_ready, rs2=f0_rs2, ag2=nothing)
     )
     finish_0()
-    n2_copy.wait()
-    ring_rest(ring_g)
-    ring_g.step(nz - 1)
-    ring_n.step(0)
 
     def out_copy(layer):
         near = pltpu.make_async_copy(xo_s.at[layer], x_out.at[at.sec], io_sem.at[3])
@@ -615,14 +689,12 @@
     send_out(0)
     n2_last = pltpu.make_async_copy(n2_s, n2_out, io_sem.at[4])
     finish_1 = layer_forward(
-        1,
-        xo_s.at[0],
-        dict(states=lambda: ring_n.step(1), rs1=nothing, ag1=nothing, n2=n2_last.start, rs2=lambda: ring_n.step(2), ag2=nothing),
+        1, xo_s.at[0], dict(begin=f1_begin, states=f1_states, rs1=f1_rs1, ag1=nothing, n2=f1_n2, rs2=nothing, ag2=nothing)
     )
     send_out(1)
     finish_1()
-    ring_rest(ring_n)
-    ring_n.step(nz - 1)
+    upward(0, nz - 1, ring_g.ready)
+    upward(0, nz - 1, ring_n.ready)
     n2_last.wait()
     ring_g.drain()
     ring_n.drain()
@@ -648,10 +720,11 @@
     other = take(8)
     saved = [take(SAVED), take(SAVED)]
     gath_g1, gath_n2_0, n2_1 = take(3)
-    ig_o, gains_o, att_o = take(3)
+    ig_o, gains_o = take(2)
+    att_o = take(2)
     ffn_o = take(3)
     gath_n2_1, gath_g0 = take(2)
-    a_mine, a_peer, a_land = take(3)
+    a_peer, a_land = take(2), take(2)
     wr_o = take(3)
     mats = take(5)
     keep_s = take(SAVED)
@@ -660,8 +733,8 @@
     acc = take(3)
     wx_s = take(3)
     blk_n2, blk_g, n2t_s, gt_s = take(4)
-    a_s, work_s = take(2)
-    (w_sem, io_sem, keep_sem, e_send, e_recv, st_send, st_recv, head_send, head_recv, r_send, r_recv) = take(11)
+    a_s, work_s = take(2), take(2)
+    (w_sem, io_sem, keep_sem, e_send, e_recv, st_send, st_recv, head_send, head_recv, r_send, r_recv, p_send, p_recv) = take(13)
     (wx_send, wx_recv, ap_send, ap_recv, l_send, l_recv, x_send, x_recv, gz_send, gz_recv, gh_send, gh_recv) = take(12)
     x_s, n1_s, qk_s, u_s, o_s, yx_s, sin_s, gb_s, h_s, f_s, v_s = keep_s
     df_s, dv_s = f_s, v_s
@@ -688,11 +761,17 @@
     def keep_copy(layer, i):
         return pltpu.make_async_copy(saved[layer][i], keep_s[i], keep_sem.at[i])
 
-    ring_n = Ring(at, n2_1, gath_n2_1, r_send.at[0], r_recv.at[0])
-    ring_g = Ring(at, ig_s.at[1], gath_g0, r_send.at[1], r_recv.at[1])
+    ring_n = Ring(at, n2_1, gath_n2_1, r_send.at[0], r_recv.at[0], p_send.at[0], p_recv.at[0])
+    ring_g = Ring(at, ig_s.at[1], gath_g0, r_send.at[1], r_recv.at[1], p_send.at[1], p_recv.at[1])
     line = [
-        LineSum(at, a_mine.at[0], a_peer.at[0], a_land.at[0], work_s, io_sem.at[4], l_send.at[0], l_recv.at[0], ap_recv),
-        LineSum(at, a_mine.at[1], a_peer.at[1], a_land.at[1], work_s, io_sem.at[4], l_send.at[1], l_recv.at[1], ap_recv),
+        [
+            LineSum(
+                at, a_s[g], a_peer[g].at[layer], a_land[g].at[layer], work_s[g], io_sem.at[4],
+                l_send.at[layer, g], l_recv.at[layer, g], ap_recv.at[layer, g],
+            )
+            for g in range(2)
+        ]
+        for layer in range(2)
     ]
 
     def piece(layer, i):
@@ -787,36 +866,32 @@
     valid = at.pos() < at.tot
     lane = lax.broadcasted_iota(jnp.int32, (rows, LANES), 1)
 
-    def peer_chunk(layer, i):
-        return remote(a_s.at[i], a_peer.at[layer, i], ap_send.at[i], ap_recv.at[i], core)
-
-    def mine_chunk(layer, i):
-        return pltpu.make_async_copy(a_s.at[i], a_mine.at[layer, i], ap_send.at[i])
-
-    def mixer_grads(layer):
+    def line_core(layer, g):
+        return 1 if layer == 1 or g == 1 else 0
+
+    def peer_chunk(layer, g, i):
+        return remote(a_s[g].at[i], a_peer[g].at[layer, i], ap_send.at[g, i], ap_recv.at[layer, g, i], core)
+
+    def mixer_grads(layer, g):
+        late = 2 * qk + width
         for i in range(nz):
             cols = slice(i * block, (i + 1) * block)
-            a_s[i, :, 0 : 2 * qk + 2 * width] = dot_tn(n1_s[:, cols], dcat_s[...]).astype(BF16)
-            a_s[i, :, 2 * qk + 2 * width :] = dot_tn(dm_s[:, cols], gb_s[...]).astype(BF16)
-
-            @pl.when(at.sec != layer)
+            if g == 0:
+                a_s[0][i, :, 0:width] = dot_tn(n1_s[:, cols], dcat_s[:, late:]).astype(BF16)
+                a_s[0][i, :, width:] = dot_tn(dm_s[:, cols], gb_s[...]).astype(BF16)
+            else:
+                a_s[1][i] = dot_tn(n1_s[:, cols], dcat_s[:, 0:late]).astype(BF16)
+
+            @pl.when(at.sec != line_core(layer, g))
             def _(i=i):
-                peer_chunk(layer, i).start()
-
-            @pl.when(at.sec == layer)
+                peer_chunk(layer, g, i).start()
+
+    def mixer_sent(layer, g):
+        for i in range(nz):
+
+            @pl.when(at.sec != line_core(layer, g))
             def _(i=i):
-                mine_chunk(layer, i).start()
-
-    def mixer_sent(layer):
-        for i in range(nz):
-
-            @pl.when(at.sec != layer)
-            def _(i=i):
-                peer_chunk(layer, i).wait_send()
-
-            @pl.when(at.sec == layer)
-            def _(i=i):
-                mine_chunk(layer, i).wait()
+                peer_chunk(layer, g, i).wait_send()
 
     def layer_backward(layer, hooks):
         small = jnp.where(at.sec == layer, small_own[...], small_other[...])
@@ -840,16 +915,15 @@
         weight_wait(5)
         weight_wait(6)
 
-        def up_chunk(at_col, size):
-            cols = pl.ds(at_col, size)
+        s1 = []
+        for half in range(2):
+            cols = half_cols(w_up, half)
             part = dot_nn(df_s[...], w_gate[:, cols]) + dot_nn(dv_s[...], w_up[:, cols])
-            part_s[0, :, cols] = part.astype(BF16)
-
-        chunks(d, 256, up_chunk)
-        s1 = scatter_start(at, part_s.at[0], got_s, head_send.at[layer, 0], head_recv.at[layer, 0])
+            part_s[:, cols] = part.astype(BF16)
+            s1 += scatter_start(at, part_s, got_s, head_send.at[layer, 0], head_recv.at[layer, 0], half)
         hooks["rs1"]()
         keep_copy(layer, 8).wait()
-        dn2 = scatter_sum(at, part_s.at[0], got_s, s1)
+        dn2 = scatter_sum(at, part_s, got_s, s1)
         back, gain_grad = norm_rows_back(h_s[...], gain_ffn, dn2)
         gsum_s[layer, 1:2, :] = gain_grad
         dh = grad_s[at.mine].astype(F32) + back
@@ -864,6 +938,7 @@
         a_low, b_low = qk_s[:, 0:qk], qk_s[:, qk : 2 * qk]
         hooks["ag1"]()
         wait_recv(s2)
+        hooks["dm"]()
 
         def out_chunk(at_row, size):
             cols = pl.ds(at_row, size)
@@ -883,6 +958,7 @@
             one, two = lift_parts(a_low, tables, 1, head)
             psi = jnp.where(applies, one * two, 0.0).astype(BF16)
             ss[layer, head] = dot_tn(psi, dyx_s[head])[:PSI_SENT].astype(BF16)
+        dcat_s[:, 2 * qk + width :] = do_s[:, :width].astype(BF16)
 
         def state(k):
             return remote(
@@ -914,6 +990,7 @@
             )
             db_s[...] += dot_tn(de, a_own)
             yx_s[head] = dot_tn(kern, dyx_s[head])
+        hooks["local"]()
         for j in range(1, nz):
 
             @pl.when(j > at.s)
@@ -948,7 +1025,6 @@
 
         dcat_s[:, 0:qk] = (da_s[...] * 0.5).astype(BF16)
         dcat_s[:, qk : 2 * qk] = (db_s[...] * 0.5).astype(BF16)
-        dcat_s[:, 2 * qk + width :] = do_s[:, :width].astype(BF16)
         gsum_s[layer, 2:8, :] = jnp.zeros((6, d), F32)
         for j in range(KW):
             product = dc_s[0:rows, :width] * u_s[8 - j : 8 - j + rows, :width]
@@ -964,15 +1040,14 @@
             du = du + jnp.where(at.same(j), dc_s[j : j + rows, :width] * taps[j : j + 1, :width], 0.0)
         dcat_s[:, 2 * qk : 2 * qk + width] = du.astype(BF16)
 
-        def proj_chunk(at_col, size):
-            cols = pl.ds(at_col, size)
-            part_s[1, :, cols] = dot_nn(dcat_s[...], cat[:, cols]).astype(BF16)
-
-        chunks(d, 256, proj_chunk)
-        s3 = scatter_start(at, part_s.at[1], got_s, head_send.at[layer, 2], head_recv.at[layer, 2])
-        mixer_grads(layer)
+        wait_send(s1)
+        s3 = []
+        for half in range(2):
+            cols = half_cols(cat, half)
+            part_s[:, cols] = dot_nn(dcat_s[...], cat[:, cols]).astype(BF16)
+            s3 += scatter_start(at, part_s, got_s, head_send.at[layer, 2], head_recv.at[layer, 2], half)
         hooks["rs2"]()
-        dn1 = scatter_sum(at, part_s.at[1], got_s, s3)
+        dn1 = scatter_sum(at, part_s, got_s, s3)
         back, gain_grad = norm_rows_back(x_s[...].astype(F32), gain_attn, dn1)
         gsum_s[layer, 0:1, :] = gain_grad
         ig_s[layer, at.mine] = (dh_s[...] + back).astype(BF16)
@@ -980,7 +1055,7 @@
         hooks["ag2"]()
         wait_recv(s4)
         ig_send(layer)
-        wait_send(s1 + s3)
+        wait_send(s3)
 
         def finish():
             wait_send(s2 + s4)
@@ -996,19 +1071,6 @@
                     state(k).wait_send()
 
         return finish
-
-    def rest(layer, ring):
-        for k in range(3, min(nz, 4)):
-            ring.step(k)
-            piece(layer, k)
-
-        def one(k, carry):
-            ring.step(k)
-            piece(layer, k)
-            return carry
-
-        if nz > 4:
-            lax.fori_loop(4, nz, one, 0)
 
     def owner(layer, what):
         @pl.when(at.sec == layer)
@@ -1026,77 +1088,128 @@
     g_copy.wait()
     grad_s[...] = jnp.where(valid, grad_s[...].astype(F32), 0.0).astype(BF16)
 
+    def slot(layer, g, i):
+        owner(line_core(layer, g), lambda: line[layer][g].slot(i))
+
+    def far_sum(g):
+        return remote(work_s[g].at[0], att_o[g], x_send.at[2], x_recv.at[2], core)
+
+    def line_last(layer, g):
+        def go():
+            upward(3, nz - 1, line[layer][g].slot)
+            line[layer][g].last()
+            if line_core(layer, g) == layer:
+                copy = pltpu.make_async_copy(work_s[g].at[0], att_o[g], io_sem.at[8])
+                copy.start()
+                copy.wait()
+            else:
+                far_sum(g).start()
+
+        owner(line_core(layer, g), go)
+
+    def pieces(layer, ring, begin, end):
+        def one(k):
+            ring.ready(k - 1)
+            piece(layer, k)
+
+        upward(begin, end, one)
+
+    def spread(ring):
+        upward(3, nz, ring.step)
+        upward(1, nz - 1, ring.pair)
+
+    def nothing():
+        pass
+
+    def b1_rs1():
+        ring_n.step(1)
+        ring_n.pair(0)
+        piece(1, 0)
+
     def b1_ag1():
-        ring_n.step(1)
-        piece(1, 1)
+        ring_n.step(2)
+        pieces(1, ring_n, 1, 2)
+
+    def b1_local():
+        mixer_grads(1, 0)
+
+    def b1_rs2():
+        mixer_grads(1, 1)
+        slot(1, 0, 0)
+        pieces(1, ring_n, 2, 3)
 
     def b1_ag2():
         for i in (4, 0, 1, 2, 3):
             weight_start(0, i)
         for i in (9, 10, 8, 3, 2, 4, 5, 6, 7, 1, 0):
             keep_copy(0, i).start()
-        rest(1, ring_n)
+        slot(1, 0, 1)
+        slot(1, 1, 0)
+        pieces(1, ring_n, 3, nz)
         for i in (7, 5, 6):
             weight_start(0, i)
         ffn_send(1)
 
-    def nothing():
-        pass
-
-    def b1_states():
-        ring_n.step(2)
-
-    def b1_rs2():
-        piece(1, 2)
-
     finish_1 = layer_backward(
-        1, dict(begin=nothing, rs1=lambda: piece(1, 0), ag1=b1_ag1, states=b1_states, rs2=b1_rs2, ag2=b1_ag2)
+        1,
+        dict(
+            begin=nothing, rs1=b1_rs1, ag1=b1_ag1, dm=lambda: spread(ring_n), local=b1_local,
+            states=nothing, rs2=b1_rs2, ag2=b1_ag2,
+        ),
     )
     finish_1()
     grad_s[...] = jnp.where(valid, ig_s[1].astype(F32), 0.0).astype(BF16)
 
     def b0_begin():
         ring_g.step(0)
-        mixer_sent(1)
-        owner(1, lambda: line[1].slot(0))
+        slot(1, 0, 2)
+        slot(1, 1, 1)
 
     def b0_rs1():
         ffn_take(1)
+        ring_g.step(1)
+        ring_g.pair(0)
         piece(0, 0)
 
     def b0_ag1():
-        ring_g.step(1)
-        piece(0, 1)
+        ring_g.step(2)
+        slot(1, 1, 2)
+        pieces(0, ring_g, 1, 2)
+
+    def b0_local():
+        line_last(1, 0)
+        mixer_sent(1, 0)
+        mixer_grads(0, 0)
 
     def b0_states():
-        ring_g.step(2)
-        owner(1, lambda: line[1].slot(1))
+        line_last(1, 1)
 
     def b0_rs2():
-        piece(0, 2)
-        owner(1, lambda: line[1].slot(2))
+        mixer_sent(1, 1)
+        mixer_grads(0, 1)
+        slot(0, 0, 0)
+        pieces(0, ring_g, 2, 3)
 
     def b0_ag2():
-        rest(0, ring_g)
+        slot(0, 0, 1)
+        slot(0, 1, 0)
+        pieces(0, ring_g, 3, nz)
         ffn_send(0)
 
     finish_0 = layer_backward(
-        0, dict(begin=b0_begin, rs1=b0_rs1, ag1=b0_ag1, states=b0_states, rs2=b0_rs2, ag2=b0_ag2)
+        0,
+        dict(
+            begin=b0_begin, rs1=b0_rs1, ag1=b0_ag1, dm=lambda: spread(ring_g), local=b0_local,
+            states=b0_states, rs2=b0_rs2, ag2=b0_ag2,
+        ),
     )
 
     gain_swap = remote(gsum_s.at[1 - at.sec], gpeer_s, x_send.at[1], x_recv.at[1], core)
     gain_swap.start()
 
-    def line_end(layer, begin):
-        for i in range(begin, nz - 1):
-            line[layer].slot(i)
-        line[layer].last()
-        copy = pltpu.make_async_copy(work_s.at[0], att_o, io_sem.at[8])
-        copy.start()
-        copy.wait()
-
-    owner(1, lambda: line_end(1, 3))
-    mixer_sent(0)
+    slot(0, 0, 2)
+    slot(0, 1, 1)
+    slot(0, 1, 2)
     gain_swap.wait_recv()
     gtot_s[0] = gsum_s[at.sec] + gpeer_s[...]
 
@@ -1106,7 +1219,8 @@
 
     for k in range(1, nz):
         gain_seq(k).start()
-    ffn_take(0)
+    line_last(0, 1)
+    line_last(0, 0)
     for k in range(1, nz):
         gain_seq(k).wait_recv()
     total = gtot_s[0]
@@ -1119,7 +1233,11 @@
 
     for m in range(1, nh):
         gain_head(m).start()
-    owner(0, lambda: line_end(0, 0))
+    ffn_take(0)
+    mixer_sent(0, 0)
+    mixer_sent(0, 1)
+    owner(0, lambda: far_sum(1).wait_recv())
+    owner(1, lambda: far_sum(1).wait_send())
     for m in range(1, nh):
         gain_head(m).wait_recv()
     total = gtot_s[1, 0:2]
@@ -1143,6 +1261,23 @@
     far.wait_recv()
 
 
+def final_kernel(qk, width, *refs):
+    take = taker(refs)
+    whole, (early, late), out, parts, (sems,) = take(5), take(2), take(5), take(5), take(1)
+    copies = [pltpu.make_async_copy(a, b, sems.at[i]) for i, (a, b) in enumerate(zip(whole, out))]
+    for copy in copies:
+        copy.start()
+    g_q, g_k, g_v, g_o, g_out = parts
+    turned = late[:, 0 : 2 * qk].astype(F32).T
+    g_q[...] = turned[0:qk]
+    g_k[...] = turned[qk : 2 * qk]
+    g_v[...] = late[:, 2 * qk :].astype(F32)
+    g_o[...] = early[:, 0:width].astype(F32)
+    g_out[...] = early[:, width:].astype(F32).T
+    for copy in copies:
+        copy.wait()
+
+
 def shape(dims, kind=BF16):
     return jax.ShapeDtypeStruct(tuple(dims), kind)
 
@@ -1164,7 +1299,7 @@
     part, block = rows // nh, d // nz
     dims = (nz, nh, rows, heads)
     wide = -(-((heads - 1) * HD + LANES) // LANES) * LANES
-    total = 2 * qk + 3 * width
+    groups = (2 * width, 2 * qk + width)
     tables = jnp.asarray(lift_tables(heads), BF16)
     turned = [jnp.swapaxes(w, 1, 2) for w in (w_query, w_key, w_value, w_output_gate)]
     own = (*turned, w_out, jnp.swapaxes(w_gate, 1, 2), jnp.swapaxes(w_up, 1, 2), w_down)
@@ -1234,10 +1369,12 @@
             DMA((2,)),
             DMA((2, nz)),
             DMA((2, nz)),
-            DMA((2, 4, nh - 1)),
-            DMA((2, 4, nh - 1)),
-            DMA((2, 2, nz - 1)),
-            DMA((2, 2, nz - 1)),
+            DMA((2, 4, 2 * (nh - 1))),
+            DMA((2, 4, 2 * (nh - 1))),
+            DMA((2, 2, nz - 1, 2)),
+            DMA((2, 2, nz - 1, 2)),
+            DMA((2, 2, nz - 1, 2)),
+            DMA((2, 2, nz - 1, 2)),
         ]
     )
     first = pl.pallas_call(
@@ -1253,10 +1390,12 @@
     section_out, gath_g1, gath_n2_0, n2_1 = first[9 + 2 * SAVED :]
 
     outs = (
-        [shape((micro, rows, d)), shape((8, d), F32), shape((block, total))]
+        [shape((micro, rows, d)), shape((8, d), F32)]
+        + [shape((block, g)) for g in groups]
         + [shape((block, ff), F32)] * 3
         + [gathered, gathered]
-        + [shape((2, nz, block, total)), shape((2, nz, block, total)), shape((2, 2, nz, block, total))]
+        + [shape((2, nz, block, g)) for g in groups]
+        + [shape((2, 2, nz, block, g)) for g in groups]
         + [shape((block, ff))] * 3
     )
     out_specs = [ANY, VM] + [ANY] * (len(outs) - 2)
@@ -1265,7 +1404,7 @@
         + [vm(*k) for k in kept]
         + [
             act,
-            vm((2, rows, d)),
+            act,
             vm((nh - 1, part, d)),
             act,
             vm((part, d), F32),
@@ -1290,7 +1429,9 @@
         ]
         + [vm((block, ff), F32)] * 3
         + [vm((block, ff))] * 3
-        + [act, act, vm((block, rows)), vm((block, rows)), vm((nz, block, total)), vm((3, block, total))]
+        + [act, act, vm((block, rows)), vm((block, rows))]
+        + [vm((nz, block, g)) for g in groups]
+        + [vm((3, block, g)) for g in groups]
         + [
             DMA((8,)),
             DMA((12,)),
@@ -1299,18 +1440,20 @@
             DMA((2,)),
             DMA((2, nz)),
             DMA((2, nz)),
-            DMA((2, 4, nh - 1)),
-            DMA((2, 4, nh - 1)),
-            DMA((2, 2, nz - 1)),
-            DMA((2, 2, nz - 1)),
+            DMA((2, 4, 2 * (nh - 1))),
+            DMA((2, 4, 2 * (nh - 1))),
+            DMA((2, 2, nz - 1, 2)),
+            DMA((2, 2, nz - 1, 2)),
+            DMA((2, 2, nz - 1, 2)),
+            DMA((2, 2, nz - 1, 2)),
             DMA((3,)),
             DMA((3,)),
-            DMA((nz,)),
-            DMA((nz,)),
+            DMA((2, nz)),
             DMA((2, 2, nz)),
-            DMA((2, 2, nz)),
-            DMA((2,)),
-            DMA((2,)),
+            DMA((2, 2, 2, nz)),
+            DMA((2, 2, 2, nz)),
+            DMA((3,)),
+            DMA((3,)),
             DMA((nz - 1,)),
             DMA((nz - 1,)),
             DMA((nh - 1,)),
@@ -1325,19 +1468,38 @@
         scratch_shapes=scratch,
         compiler_params=params(1),
     )(lengths, out_grad, small_own, small_other, tables, *own, *other, *saved, gath_g1, gath_n2_0, n2_1)
-    input_grad, gains, att, g_gate, g_up, g_down = second[:6]
-    att = att.astype(F32)
+    input_grad, gains, att_early, att_late, g_gate, g_up, g_down = second[:7]
+    finals = [
+        shape((micro, rows, d)),
+        shape((micro, rows, d)),
+        shape((block, ff), F32),
+        shape((block, ff), F32),
+        shape((block, ff), F32),
+        shape((qk, block), F32),
+        shape((qk, block), F32),
+        shape((block, width), F32),
+        shape((block, width), F32),
+        shape((width, block), F32),
+    ]
+    section_out, input_grad, g_gate, g_up, g_down, g_q, g_k, g_v, g_o, g_out = pl.pallas_call(
+        functools.partial(final_kernel, qk, width),
+        out_shape=finals,
+        in_specs=[ANY] * 5 + [VM] * 2,
+        out_specs=[ANY] * 5 + [VM] * 5,
+        scratch_shapes=[DMA((5,))],
+        compiler_params=pltpu.CompilerParams(vmem_limit_bytes=VMEM_LIMIT),
+    )(section_out, input_grad, g_gate, g_up, g_down, att_early, att_late)
     return (
         section_out[None],
         input_grad[None],
         gains[0:1],
         gains[1:2],
-        att[None, :, 0:qk],
-        att[None, :, qk : 2 * qk],
-        att[None, :, 2 * qk : 2 * qk + width],
-        att[None, :, 2 * qk + width : 2 * qk + 2 * width],
+        g_q.T[None],
+        g_k.T[None],
+        g_v[None],
+        g_o[None],
         gains[None, 2 : 2 + KW, :width],
-        att[:, 2 * qk + 2 * width :].T[None],
+        g_out[None],
         g_gate[None],
         g_up[None],
         g_down.T[None],

time: 493 us -> 712 us (1.44)
  Pallas kernels: 463 us -> 698 us
  local copies, waits for them, and re-layouts: 20.6 us -> 3.59 us
    pallas_call x0 -> x1, Pallas kernels: none -> 324 us  [shards(): pl.pallas_call(functools.partial(final_kernel, qk, width), out_shape=fina...]
    pallas_call x1, Pallas kernels: 293 us -> 229 us  [shards(): pl.pallas_call(functools.partial(bwd_kernel, dims), out_shape=outs, in_sp...]
    pallas_call x1, Pallas kernels: 170 us -> 145 us  [shards(): pl.pallas_call(functools.partial(fwd_kernel, dims), out_shape=outs, in_sp...]
    unnamed x20 -> x2, local copies, waits for them, and re-layouts: 16.2 us -> 1.29 us
where the time goes in v3:
time: 712 us; the launch traced here: 704 us
  Pallas kernels  698 us (98%)
    pallas_call x1, Pallas kernels, shards(): pl.pallas_call(functools.partial(final_kernel, qk, width), out_shape=fina...  324 us
    pallas_call x1, Pallas kernels, shards(): pl.pallas_call(functools.partial(bwd_kernel, dims), out_shape=outs, in_sp...  229 us
    pallas_call x1, Pallas kernels, shards(): pl.pallas_call(functools.partial(fwd_kernel, dims), out_shape=outs, in_sp...  145 us

profile of v3, /device:TPU:0, one launch (start us, length us, event | category | flops | bytes accessed | tf_op | source)
XLA Modules:
  0.0 704.2 jit_solution(15315284716999278626)
XLA Ops:
  0.7 0.1 pad.8.clone
  0.7 0.7 copy.31
  1.4 1.4 fusion.refs_3_.refs_2_
  2.8 145.2 %shard_map.246 = (f32[8,1792]{1,0:T(8,128)}, bf16[1,64,1792]{2,1,0:T(8,128)(2,1)}, bf16[1,64,1792]{2,1,0:T(8,128)(2,1)}, bf16[1,448,1792]{2,1,0:T(8,128)(2,1)}, ...) custom-call(s32[2,2]{1,0:T(2,128)} %refs_0_.3, ...), custom_call_target="tpu_custom_call" | custom-call | tf_op jit(solution)/shard_map/pallas_call | solution.py:1380
  148.1 229.4 %shard_map.247 = (bf16[2,256,1792]{2,1,0:T(8,128)(2,1)}, f32[8,1792]{1,0:T(8,128)}, bf16[448,896]{1,0:T(8,128)(2,1)}, bf16[448,576]{1,0:T(8,128)(2,1)}, f32[448,...) custom-call(s32[2,2]{1,0:T(2,128)} %refs_0_.3, ...), custom_call_target="tpu_custom_call" | custom-call | tf_op jit(solution)/shard_map/pallas_call | solution.py:1463
  377.5 0.7 slice_bitcast_fusion
  378.2 1.5 fusion.2
  379.7 0.6 copy.28
  380.3 323.7 %shard_map.248 = (bf16[2,256,1792]{2,1,0:T(8,128)(2,1)}, bf16[2,256,1792]{2,1,0:T(8,128)(2,1)}, f32[448,1216]{1,0:T(8,128)}, f32[448,1216]{1,0:T(8,128)}, f32[44...) custom-call(bf16[2,256,1792]{2,1,0:T(8,128)(2,1)} %get-tuple-element, ...), custom_call_target="tpu_custom_call" | custom-call | tf_op jit(solution)/shard_map/pallas_call | solution.py:1484
  (1 shorter events, 0.0 us)

commit v4 on v3

--- a/solution.py
+++ b/solution.py
@@ -289,15 +289,15 @@
             def _(way=way, block=block):
                 wait_recv(self._pairs(way, k, block))
 
-    def drain(self):
+    def drain(self, line=True, pairs=True):
         def one(k, carry):
-            for way, (_, there, onward, to) in enumerate(self._ways(k)):
+            for way, (_, there, onward, to) in enumerate(self._ways(k) if line else ()):
 
                 @pl.when(there & onward)
                 def _(way=way, to=to):
                     wait_send(self._copies(way, k, self.at.s, to, False))
 
-            for way, (_, there, _, _) in enumerate(self._ways(k + 1)):
+            for way, (_, there, _, _) in enumerate(self._ways(k + 1) if pairs else ()):
 
                 @pl.when(there)
                 def _(way=way):
@@ -461,7 +461,6 @@
 
     ring_g = Ring(at, out_grad.at[at.sec], gath_g1, r_send.at[0], r_recv.at[0], p_send.at[0], p_recv.at[0])
     ring_n = Ring(at, gath_n2.at[at.s], gath_n2, r_send.at[1], r_recv.at[1], p_send.at[1], p_recv.at[1])
-    ring_g.step(0)
     small_swap.wait_recv()
     small_copy = pltpu.make_async_copy(small_other, sm_s, io_sem.at[1])
     small_copy.start()
@@ -640,33 +639,23 @@
 
     n2_copy = pltpu.make_async_copy(n2_s, gath_n2.at[at.s], io_sem.at[2])
 
-    def n2_ready():
+    def f0_n2():
         n2_copy.start()
-        ring_g.step(2)
-
-    def f0_rs2():
+        ring_g.step(1)
+
+    def f1_begin():
         n2_copy.wait()
-        ring_n.step(0)
-
-    def f1_begin():
         upward(3, nz, ring_g.step)
         upward(0, nz - 1, ring_g.pair)
-        ring_n.step(1)
-
-    def f1_states():
-        ring_n.pair(0)
-
-    def f1_rs1():
-        ring_n.step(2)
+        ring_n.step(0)
 
     def f1_n2():
         n2_last.start()
-        upward(3, nz, ring_n.step)
-        upward(1, nz - 1, ring_n.pair)
+        ring_n.step(2)
 
     x_copy.wait()
     finish_0 = layer_forward(
-        0, x_s, dict(begin=nothing, states=nothing, rs1=lambda: ring_g.step(1), ag1=nothing, n2=n2_ready, rs2=f0_rs2, ag2=nothing)
+        0, x_s, dict(begin=nothing, states=nothing, rs1=lambda: ring_g.step(0), ag1=nothing, n2=f0_n2, rs2=nothing, ag2=lambda: ring_g.step(2))
     )
     finish_0()
 
@@ -689,15 +678,15 @@
     send_out(0)
     n2_last = pltpu.make_async_copy(n2_s, n2_out, io_sem.at[4])
     finish_1 = layer_forward(
-        1, xo_s.at[0], dict(begin=f1_begin, states=f1_states, rs1=f1_rs1, ag1=nothing, n2=f1_n2, rs2=nothing, ag2=nothing)
+        1, xo_s.at[0], dict(begin=f1_begin, states=nothing, rs1=lambda: ring_n.step(1), ag1=nothing, n2=f1_n2, rs2=nothing, ag2=nothing)
     )
     send_out(1)
     finish_1()
     upward(0, nz - 1, ring_g.ready)
-    upward(0, nz - 1, ring_n.ready)
+    upward(3, nz, ring_n.step)
     n2_last.wait()
     ring_g.drain()
-    ring_n.drain()
+    ring_n.drain(pairs=False)
     near, far = out_copy(0)
     near.wait()
     far.wait_send()
@@ -719,11 +708,11 @@
     own = take(8)
     other = take(8)
     saved = [take(SAVED), take(SAVED)]
-    gath_g1, gath_n2_0, n2_1 = take(3)
+    gath_g1, _, n2_1 = take(3)
     ig_o, gains_o = take(2)
     att_o = take(2)
     ffn_o = take(3)
-    gath_n2_1, gath_g0 = take(2)
+    gath_n2_1, gath_g0, gath_n2_0 = take(3)
     a_peer, a_land = take(2), take(2)
     wr_o = take(3)
     mats = take(5)
@@ -763,6 +752,7 @@
 
     ring_n = Ring(at, n2_1, gath_n2_1, r_send.at[0], r_recv.at[0], p_send.at[0], p_recv.at[0])
     ring_g = Ring(at, ig_s.at[1], gath_g0, r_send.at[1], r_recv.at[1], p_send.at[1], p_recv.at[1])
+    ring_0 = Ring(at, None, gath_n2_0, None, None, p_send.at[2], p_recv.at[2])
     line = [
         [
             LineSum(
@@ -818,6 +808,9 @@
     def ffn_swap(i):
         return remote(wx_s[i], wr_o[i], wx_send.at[i], wx_recv.at[i], core)
 
+    def ffn_own(i):
+        return pltpu.make_async_copy(acc[i], ffn_o[i], io_sem.at[5 + i])
+
     def ffn_send(layer):
         @pl.when(at.sec != layer)
         def _():
@@ -825,25 +818,16 @@
                 wx_s[i][...] = acc[i][...].astype(BF16)
                 ffn_swap(i).start()
 
-    def ffn_take(layer):
         @pl.when(at.sec == layer)
         def _():
-            copies = []
-            if layer == 0:
-                for i in range(3):
-                    ffn_swap(i).wait_send()
-            loads = [pltpu.make_async_copy(wr_o[i], wx_s[i], io_sem.at[9 + i]) for i in range(3)]
             for i in range(3):
-                ffn_swap(i).wait_recv()
-                loads[i].start()
+                ffn_own(i).start()
+
+    def ffn_done(layer):
+        @pl.when(at.sec == layer)
+        def _():
             for i in range(3):
-                loads[i].wait()
-                acc[i][...] += wx_s[i][...].astype(F32)
-                copy = pltpu.make_async_copy(acc[i], ffn_o[i], io_sem.at[5 + i])
-                copy.start()
-                copies.append(copy)
-            for copy in copies:
-                copy.wait()
+                ffn_own(i).wait()
 
     def ig_copy(layer):
         near = pltpu.make_async_copy(ig_s.at[layer], ig_o.at[at.sec], io_sem.at[3])
@@ -867,7 +851,7 @@
     lane = lax.broadcasted_iota(jnp.int32, (rows, LANES), 1)
 
     def line_core(layer, g):
-        return 1 if layer == 1 or g == 1 else 0
+        return 1 if layer == 0 and g == 1 else 0
 
     def peer_chunk(layer, g, i):
         return remote(a_s[g].at[i], a_peer[g].at[layer, i], ap_send.at[g, i], ap_recv.at[layer, g, i], core)
@@ -1092,7 +1076,7 @@
         owner(line_core(layer, g), lambda: line[layer][g].slot(i))
 
     def far_sum(g):
-        return remote(work_s[g].at[0], att_o[g], x_send.at[2], x_recv.at[2], core)
+        return remote(work_s[g].at[0], att_o[g], x_send.at[2 + g], x_recv.at[2 + g], core)
 
     def line_last(layer, g):
         def go():
@@ -1110,6 +1094,8 @@
     def pieces(layer, ring, begin, end):
         def one(k):
             ring.ready(k - 1)
+            if layer == 0:
+                ring_0.ready(k - 1)
             piece(layer, k)
 
         upward(begin, end, one)
@@ -1131,6 +1117,7 @@
         pieces(1, ring_n, 1, 2)
 
     def b1_local():
+        upward(0, nz - 1, ring_0.pair)
         mixer_grads(1, 0)
 
     def b1_rs2():
@@ -1144,7 +1131,6 @@
         for i in (9, 10, 8, 3, 2, 4, 5, 6, 7, 1, 0):
             keep_copy(0, i).start()
         slot(1, 0, 1)
-        slot(1, 1, 0)
         pieces(1, ring_n, 3, nz)
         for i in (7, 5, 6):
             weight_start(0, i)
@@ -1163,18 +1149,19 @@
     def b0_begin():
         ring_g.step(0)
         slot(1, 0, 2)
-        slot(1, 1, 1)
+        slot(1, 1, 0)
 
     def b0_rs1():
-        ffn_take(1)
+        ffn_done(1)
         ring_g.step(1)
         ring_g.pair(0)
         piece(0, 0)
+        slot(1, 1, 1)
 
     def b0_ag1():
         ring_g.step(2)
+        pieces(0, ring_g, 1, 2)
         slot(1, 1, 2)
-        pieces(0, ring_g, 1, 2)
 
     def b0_local():
         line_last(1, 0)
@@ -1187,6 +1174,7 @@
     def b0_rs2():
         mixer_sent(1, 1)
         mixer_grads(0, 1)
+        owner(0, lambda: far_sum(0).wait_send())
         slot(0, 0, 0)
         pieces(0, ring_g, 2, 3)
 
@@ -1233,11 +1221,11 @@
 
     for m in range(1, nh):
         gain_head(m).start()
-    ffn_take(0)
+    ffn_done(0)
     mixer_sent(0, 0)
     mixer_sent(0, 1)
-    owner(0, lambda: far_sum(1).wait_recv())
-    owner(1, lambda: far_sum(1).wait_send())
+    far_sum(1).wait()
+    owner(1, lambda: far_sum(0).wait_recv())
     for m in range(1, nh):
         gain_head(m).wait_recv()
     total = gtot_s[1, 0:2]
@@ -1249,12 +1237,14 @@
     finish_0()
     ring_n.drain()
     ring_g.drain()
+    ring_0.drain(line=False)
     gain_swap.wait_send()
     for k in range(1, nz):
         gain_seq(k).wait_send()
     for m in range(1, nh):
         gain_head(m).wait_send()
-    owner(1, lambda: wait_send([ffn_swap(i) for i in range(3)]))
+    for i in range(3):
+        ffn_swap(i).wait()
     near, far = ig_copy(0)
     near.wait()
     far.wait_send()
@@ -1263,9 +1253,10 @@
 
 def final_kernel(qk, width, *refs):
     take = taker(refs)
-    whole, (early, late), out, parts, (sems,) = take(5), take(2), take(5), take(5), take(1)
-    copies = [pltpu.make_async_copy(a, b, sems.at[i]) for i, (a, b) in enumerate(zip(whole, out))]
-    for copy in copies:
+    whole, far, (early, late), out, parts, held, held_far, (sems,) = take(5), take(3), take(2), take(5), take(5), take(5), take(3), take(1)
+    loads = [pltpu.make_async_copy(a, b, sems.at[i]) for i, (a, b) in enumerate(zip(whole + far, held + held_far))]
+    stores = [pltpu.make_async_copy(a, b, sems.at[8 + i]) for i, (a, b) in enumerate(zip(held, out))]
+    for copy in loads:
         copy.start()
     g_q, g_k, g_v, g_o, g_out = parts
     turned = late[:, 0 : 2 * qk].astype(F32).T
@@ -1274,7 +1265,13 @@
     g_v[...] = late[:, 2 * qk :].astype(F32)
     g_o[...] = early[:, 0:width].astype(F32)
     g_out[...] = early[:, width:].astype(F32).T
-    for copy in copies:
+    for i in range(5):
+        loads[i].wait()
+        if i >= 2:
+            loads[i + 3].wait()
+            held[i][...] += held_far[i - 2][...].astype(F32)
+        stores[i].start()
+    for copy in stores:
         copy.wait()
 
 
@@ -1393,7 +1390,7 @@
         [shape((micro, rows, d)), shape((8, d), F32)]
         + [shape((block, g)) for g in groups]
         + [shape((block, ff), F32)] * 3
-        + [gathered, gathered]
+        + [gathered, gathered, gathered]
         + [shape((2, nz, block, g)) for g in groups]
         + [shape((2, 2, nz, block, g)) for g in groups]
         + [shape((block, ff))] * 3
@@ -1444,16 +1441,16 @@
             DMA((2, 4, 2 * (nh - 1))),
             DMA((2, 2, nz - 1, 2)),
             DMA((2, 2, nz - 1, 2)),
-            DMA((2, 2, nz - 1, 2)),
-            DMA((2, 2, nz - 1, 2)),
+            DMA((3, 2, nz - 1, 2)),
+            DMA((3, 2, nz - 1, 2)),
             DMA((3,)),
             DMA((3,)),
             DMA((2, nz)),
             DMA((2, 2, nz)),
             DMA((2, 2, 2, nz)),
             DMA((2, 2, 2, nz)),
-            DMA((3,)),
-            DMA((3,)),
+            DMA((4,)),
+            DMA((4,)),
             DMA((nz - 1,)),
             DMA((nz - 1,)),
             DMA((nh - 1,)),
@@ -1466,9 +1463,11 @@
         in_specs=[SM, ANY, VM, VM, VM] + [ANY] * (16 + 2 * SAVED + 3),
         out_specs=out_specs,
         scratch_shapes=scratch,
+        input_output_aliases={5 + 16 + 2 * SAVED + 1: 9},
         compiler_params=params(1),
     )(lengths, out_grad, small_own, small_other, tables, *own, *other, *saved, gath_g1, gath_n2_0, n2_1)
     input_grad, gains, att_early, att_late, g_gate, g_up, g_down = second[:7]
+    far = second[-3:]
     finals = [
         shape((micro, rows, d)),
         shape((micro, rows, d)),
@@ -1484,11 +1483,11 @@
     section_out, input_grad, g_gate, g_up, g_down, g_q, g_k, g_v, g_o, g_out = pl.pallas_call(
         functools.partial(final_kernel, qk, width),
         out_shape=finals,
-        in_specs=[ANY] * 5 + [VM] * 2,
+        in_specs=[ANY] * 8 + [VM] * 2,
         out_specs=[ANY] * 5 + [VM] * 5,
-        scratch_shapes=[DMA((5,))],
+        scratch_shapes=[vm((micro, rows, d))] * 2 + [vm((block, ff), F32)] * 3 + [vm((block, ff))] * 3 + [DMA((13,))],
         compiler_params=pltpu.CompilerParams(vmem_limit_bytes=VMEM_LIMIT),
-    )(section_out, input_grad, g_gate, g_up, g_down, att_early, att_late)
+    )(section_out, input_grad, g_gate, g_up, g_down, *far, att_early, att_late)
     return (
         section_out[None],
         input_grad[None],

time: 712 us -> 405 us (0.57)
  Pallas kernels: 698 us -> 393 us
    pallas_call x1, Pallas kernels: 324 us -> 11.8 us  [shards(): pl.pallas_call(functools.partial(final_kernel, qk, width), out_shape=fina...]
    pallas_call x1, Pallas kernels: 229 us -> 239 us  [shards(): pl.pallas_call(functools.partial(bwd_kernel, dims), out_shape=outs, in_sp...]
where the time goes in v4:
time: 405 us; the launch traced here: 399 us
  Pallas kernels  393 us (97%)
    pallas_call x1, Pallas kernels, shards(): pl.pallas_call(functools.partial(bwd_kernel, dims), out_shape=outs, in_sp...  239 us
    pallas_call x1, Pallas kernels, shards(): pl.pallas_call(functools.partial(fwd_kernel, dims), out_shape=outs, in_sp...  142 us
    pallas_call x1, Pallas kernels, shards(): pl.pallas_call(functools.partial(final_kernel, qk, width), out_shape=fina...  11.8 us

profile of v4, /device:TPU:0, one launch (start us, length us, event | category | flops | bytes accessed | tf_op | source)
XLA Modules:
  0.0 398.8 jit_solution(2124933809702547948)
XLA Ops:
  0.7 0.1 pad.8.clone
  0.7 0.7 copy.32
  1.4 1.4 fusion.refs_3_.refs_2_
  2.8 142.1 %shard_map.246 = (f32[8,1792]{1,0:T(8,128)}, bf16[1,64,1792]{2,1,0:T(8,128)(2,1)}, bf16[1,64,1792]{2,1,0:T(8,128)(2,1)}, bf16[1,448,1792]{2,1,0:T(8,128)(2,1)}, ...) custom-call(s32[2,2]{1,0:T(2,128)} %refs_0_.3, ...), custom_call_target="tpu_custom_call" | custom-call | tf_op jit(solution)/shard_map/pallas_call | solution.py:1377
  144.9 239.1 %shard_map.247 = (bf16[2,256,1792]{2,1,0:T(8,128)(2,1)}, f32[8,1792]{1,0:T(8,128)}, bf16[448,896]{1,0:T(8,128)(2,1)}, bf16[448,576]{1,0:T(8,128)(2,1)}, f32[448,...) custom-call(s32[2,2]{1,0:T(2,128)} %refs_0_.3, ...), custom_call_target="tpu_custom_call", output_to_operand_aliasing={{9}: (44, {})} | custom-call | tf_op jit(solution)/shard_map/pallas_call | solution.py:1460
  384.0 11.8 %shard_map.248 = (bf16[2,256,1792]{2,1,0:T(8,128)(2,1)}, bf16[2,256,1792]{2,1,0:T(8,128)(2,1)}, f32[448,1216]{1,0:T(8,128)}, f32[448,1216]{1,0:T(8,128)}, f32[44...) custom-call(bf16[2,256,1792]{2,1,0:T(8,128)(2,1)} %get-tuple-element, ...), custom_call_target="tpu_custom_call" | custom-call | tf_op jit(solution)/shard_map/pallas_call | solution.py:1483
  395.8 0.7 slice_bitcast_fusion
  396.5 1.5 fusion.2
  398.0 0.6 copy.29
  (1 shorter events, 0.0 us)

commit v5 on v4

--- a/solution.py
+++ b/solution.py
@@ -18,7 +18,7 @@
 MESH = pl.DeviceIdType.MESH
 F32 = jnp.float32
 BF16 = jnp.bfloat16
-VMEM_LIMIT = 62 << 20
+VMEM_LIMIT = 63 << 20
 
 
 def dot_nn(a, b):
@@ -717,7 +717,7 @@
     wr_o = take(3)
     mats = take(5)
     keep_s = take(SAVED)
-    (grad_s, part_s, got_s, dm_s, dh_s, dg_s, do_s, cx_s, dyx_s, ss, sr, st_s, da_s, db_s, dc_s, edge_s, dcat_s, ig_s) = take(18)
+    (grad_s, t_s, part_s, got_s, dm_s, dh_s, dg_s, do_s, cx_s, dyx_s, ss, sr, st_s, da_s, db_s, dc_s, edge_s, dcat_s, ig_s) = take(19)
     gsum_s, gpeer_s, gtot_s, gz_s, gh_s = take(5)
     acc = take(3)
     wx_s = take(3)
@@ -764,14 +764,32 @@
         for layer in range(2)
     ]
 
+    def turn_blocks(n2_ref, g_ref):
+        for part in range(nz):
+
+            @pl.when(at.s == part)
+            def _(part=part):
+                n2t_s[...] = n2_ref[:, part * block : (part + 1) * block].T
+                gt_s[...] = g_ref[:, part * block : (part + 1) * block].T
+
+    def own_piece(layer):
+        copy = pltpu.make_async_copy(n2_1 if layer == 1 else gath_n2_0.at[at.s], blk_n2, io_sem.at[0])
+        copy.start()
+        copy.wait()
+        turn_blocks(blk_n2, grad_s)
+
+        def hidden(at_col, size):
+            cols = pl.ds(at_col, size)
+            acc[0][:, cols] = dot_nn(n2t_s[...], df_s[:, cols])
+            acc[1][:, cols] = dot_nn(n2t_s[...], dv_s[:, cols])
+            acc[2][:, cols] = dot_nn(gt_s[...], t_s[:, cols])
+
+        chunks(w_gate.shape[0], 640, hidden)
+
     def piece(layer, i):
         which = order(at, i)
-        if isinstance(i, int) and i == 0:
-            n2_src = n2_1 if layer == 1 else gath_n2_0.at[at.s]
-            g_src = inputs_grad.at[at.sec] if layer == 1 else ig_s.at[1]
-        else:
-            n2_src = (gath_n2_1 if layer == 1 else gath_n2_0).at[which]
-            g_src = (gath_g1 if layer == 1 else gath_g0).at[which]
+        n2_src = (gath_n2_1 if layer == 1 else gath_n2_0).at[which]
+        g_src = (gath_g1 if layer == 1 else gath_g0).at[which]
         loads = [pltpu.make_async_copy(n2_src, blk_n2, io_sem.at[0]), pltpu.make_async_copy(g_src, blk_g, io_sem.at[1])]
         for copy in loads:
             copy.start()
@@ -779,12 +797,7 @@
             copy.wait()
         pos = which * rows + lax.broadcasted_iota(jnp.int32, (rows, 1), 0)
         blk_g[...] = jnp.where(pos < at.tot, blk_g[...].astype(F32), 0.0).astype(BF16)
-        for part in range(nz):
-
-            @pl.when(at.s == part)
-            def _(part=part):
-                n2t_s[...] = blk_n2[:, part * block : (part + 1) * block].T
-                gt_s[...] = blk_g[:, part * block : (part + 1) * block].T
+        turn_blocks(blk_n2, blk_g)
 
         def hidden(at_row, size):
             cols = pl.ds(at_row, size)
@@ -796,12 +809,9 @@
             t = (act * v).astype(BF16)
             df = (dt * v * (sig + act * (1.0 - sig))).astype(BF16)
             dv = (dt * act).astype(BF16)
-            parts = (dot_nn(n2t_s[...], df), dot_nn(n2t_s[...], dv), dot_nn(gt_s[...], t))
-            for total, new in zip(acc, parts):
-                if isinstance(i, int) and i == 0:
-                    total[:, cols] = new
-                else:
-                    total[:, cols] += new
+            acc[0][:, cols] += dot_nn(n2t_s[...], df)
+            acc[1][:, cols] += dot_nn(n2t_s[...], dv)
+            acc[2][:, cols] += dot_nn(gt_s[...], t)
 
         chunks(w_gate.shape[0], 640, hidden)
 
@@ -851,7 +861,7 @@
     lane = lax.broadcasted_iota(jnp.int32, (rows, LANES), 1)
 
     def line_core(layer, g):
-        return 1 if layer == 0 and g == 1 else 0
+        return g
 
     def peer_chunk(layer, g, i):
         return remote(a_s[g].at[i], a_peer[g].at[layer, i], ap_send.at[g, i], ap_recv.at[layer, g, i], core)
@@ -892,8 +902,10 @@
             f = f_s[:, cols].astype(F32)
             v = v_s[:, cols].astype(F32)
             sig = jax.nn.sigmoid(f)
-            df_s[:, cols] = (dt * v * sig * (1.0 + f * (1.0 - sig))).astype(BF16)
-            dv_s[:, cols] = (dt * f * sig).astype(BF16)
+            act = f * sig
+            t_s[:, cols] = (act * v).astype(BF16)
+            df_s[:, cols] = (dt * v * (sig + act * (1.0 - sig))).astype(BF16)
+            dv_s[:, cols] = (dt * act).astype(BF16)
 
         chunks(df_s.shape[1], 256, down_chunk)
         weight_wait(5)
@@ -906,6 +918,8 @@
             part_s[:, cols] = part.astype(BF16)
             s1 += scatter_start(at, part_s, got_s, head_send.at[layer, 0], head_recv.at[layer, 0], half)
         hooks["rs1"]()
+        keep_copy(layer, 3).wait()
+        convolve(at, u_s, taps, do_s, cx_s, heads)
         keep_copy(layer, 8).wait()
         dn2 = scatter_sum(at, part_s, got_s, s1)
         back, gain_grad = norm_rows_back(h_s[...], gain_ffn, dn2)
@@ -914,11 +928,10 @@
         dh_s[...] = dh
         dm_s[at.mine] = dh.astype(BF16)
         s2 = gather_start(at, dm_s, head_send.at[layer, 1], head_recv.at[layer, 1])
-        for i in range(8):
+        for i in (0, 1, 2, 4, 5, 6, 7):
             keep_copy(layer, i).wait()
         for i in (4, 0, 1, 2, 3):
             weight_wait(i)
-        convolve(at, u_s, taps, do_s, cx_s, heads)
         a_low, b_low = qk_s[:, 0:qk], qk_s[:, qk : 2 * qk]
         hooks["ag1"]()
         wait_recv(s2)
@@ -1107,10 +1120,16 @@
     def nothing():
         pass
 
+    gain_swap = remote(gsum_s.at[1 - at.sec], gpeer_s, x_send.at[1], x_recv.at[1], core)
+
+    def gain_seq(k):
+        to = lax.rem(at.s + k, nz)
+        return remote(gtot_s.at[0], gz_s.at[k - 1], gz_send.at[k - 1], gz_recv.at[k - 1], (at.sec, to, at.h))
+
     def b1_rs1():
+        own_piece(1)
         ring_n.step(1)
         ring_n.pair(0)
-        piece(1, 0)
 
     def b1_ag1():
         ring_n.step(2)
@@ -1153,9 +1172,9 @@
 
     def b0_rs1():
         ffn_done(1)
+        own_piece(0)
         ring_g.step(1)
         ring_g.pair(0)
-        piece(0, 0)
         slot(1, 1, 1)
 
     def b0_ag1():
@@ -1177,12 +1196,19 @@
         owner(0, lambda: far_sum(0).wait_send())
         slot(0, 0, 0)
         pieces(0, ring_g, 2, 3)
-
-    def b0_ag2():
         slot(0, 0, 1)
         slot(0, 1, 0)
+
+    def b0_ag2():
+        gain_swap.start()
         pieces(0, ring_g, 3, nz)
         ffn_send(0)
+        slot(0, 0, 2)
+        slot(0, 1, 1)
+        gain_swap.wait_recv()
+        gtot_s[0] = gsum_s[at.sec] + gpeer_s[...]
+        for k in range(1, nz):
+            gain_seq(k).start()
 
     finish_0 = layer_backward(
         0,
@@ -1192,22 +1218,7 @@
         ),
     )
 
-    gain_swap = remote(gsum_s.at[1 - at.sec], gpeer_s, x_send.at[1], x_recv.at[1], core)
-    gain_swap.start()
-
-    slot(0, 0, 2)
-    slot(0, 1, 1)
     slot(0, 1, 2)
-    gain_swap.wait_recv()
-    gtot_s[0] = gsum_s[at.sec] + gpeer_s[...]
-
-    def gain_seq(k):
-        to = lax.rem(at.s + k, nz)
-        return remote(gtot_s.at[0], gz_s.at[k - 1], gz_send.at[k - 1], gz_recv.at[k - 1], (at.sec, to, at.h))
-
-    for k in range(1, nz):
-        gain_seq(k).start()
-    line_last(0, 1)
     line_last(0, 0)
     for k in range(1, nz):
         gain_seq(k).wait_recv()
@@ -1221,10 +1232,12 @@
 
     for m in range(1, nh):
         gain_head(m).start()
+    line_last(0, 1)
     ffn_done(0)
     mixer_sent(0, 0)
     mixer_sent(0, 1)
-    far_sum(1).wait()
+    owner(1, lambda: far_sum(1).wait_send())
+    owner(0, lambda: far_sum(1).wait_recv())
     owner(1, lambda: far_sum(0).wait_recv())
     for m in range(1, nh):
         gain_head(m).wait_recv()
@@ -1401,6 +1414,7 @@
         + [vm(*k) for k in kept]
         + [
             act,
+            vm((rows, ff)),
             act,
             vm((nh - 1, part, d)),
             act,

time: 405 us -> 397 us (0.980)
  Pallas kernels: 393 us -> 383 us
    pallas_call x1, Pallas kernels: 239 us -> 229 us  [shards(): pl.pallas_call(functools.partial(bwd_kernel, dims), out_shape=outs, in_sp...]
where the time goes in v5:
time: 397 us; the launch traced here: 389 us
  Pallas kernels  383 us (96%)
    pallas_call x1, Pallas kernels, shards(): pl.pallas_call(functools.partial(bwd_kernel, dims), out_shape=outs, in_sp...  229 us
    pallas_call x1, Pallas kernels, shards(): pl.pallas_call(functools.partial(fwd_kernel, dims), out_shape=outs, in_sp...  142 us
    pallas_call x1, Pallas kernels, shards(): pl.pallas_call(functools.partial(final_kernel, qk, width), out_shape=fina...  11.8 us

profile of v5, /device:TPU:0, one launch (start us, length us, event | category | flops | bytes accessed | tf_op | source)
XLA Modules:
  0.0 389.0 jit_solution(17909369059113892066)
XLA Ops:
  0.7 0.1 pad.8.clone
  0.7 0.7 copy.32
  1.4 1.4 fusion.refs_3_.refs_2_
  2.8 142.1 %shard_map.246 = (f32[8,1792]{1,0:T(8,128)}, bf16[1,64,1792]{2,1,0:T(8,128)(2,1)}, bf16[1,64,1792]{2,1,0:T(8,128)(2,1)}, bf16[1,448,1792]{2,1,0:T(8,128)(2,1)}, ...) custom-call(s32[2,2]{1,0:T(2,128)} %refs_0_.3, ...), custom_call_target="tpu_custom_call" | custom-call | tf_op jit(solution)/shard_map/pallas_call | solution.py:1390
  144.9 228.9 %shard_map.247 = (bf16[2,256,1792]{2,1,0:T(8,128)(2,1)}, f32[8,1792]{1,0:T(8,128)}, bf16[448,896]{1,0:T(8,128)(2,1)}, bf16[448,576]{1,0:T(8,128)(2,1)}, f32[448,...) custom-call(s32[2,2]{1,0:T(2,128)} %refs_0_.3, ...), custom_call_target="tpu_custom_call", output_to_operand_aliasing={{9}: (44, {})} | custom-call | tf_op jit(solution)/shard_map/pallas_call | solution.py:1474
  373.9 11.8 %shard_map.248 = (bf16[2,256,1792]{2,1,0:T(8,128)(2,1)}, bf16[2,256,1792]{2,1,0:T(8,128)(2,1)}, f32[448,1216]{1,0:T(8,128)}, f32[448,1216]{1,0:T(8,128)}, f32[44...) custom-call(bf16[2,256,1792]{2,1,0:T(8,128)(2,1)} %get-tuple-element, ...), custom_call_target="tpu_custom_call" | custom-call | tf_op jit(solution)/shard_map/pallas_call | solution.py:1497
  385.7 0.7 slice_bitcast_fusion
  386.4 1.5 fusion.2
  387.9 0.6 copy.29
  (1 shorter events, 0.0 us)

commit v6 on v5

--- a/solution.py
+++ b/solution.py
@@ -319,74 +319,59 @@
 
 
 class LineSum:
-    def __init__(self, at, mine, peer, land, work, io, send, recv, peer_recv):
-        self.at, self.mine, self.peer, self.land, self.work = at, mine, peer, land, work
+    def __init__(self, at, mine, peer, land, held, io, send, recv, peer_recv):
+        self.at, self.mine, self.peer, self.land, self.held = at, mine, peer, land, held
         self.io, self.send, self.recv, self.peer_recv = io, send, recv, peer_recv
 
     def _hop(self, way, d):
         at = self.at
         to = lax.rem(at.s + (1 if way == 0 else at.nz - 1), at.nz)
-        return remote(self.work.at[way], self.land.at[way, d], self.send.at[way, d], self.recv.at[way, d], (at.sec, to, at.h))
-
-    def _load(self, src, slot):
-        copy = pltpu.make_async_copy(src, self.work.at[slot], self.io)
+        return remote(self.mine.at[d], self.land.at[way, d], self.send.at[way, d], self.recv.at[way, d], (at.sec, to, at.h))
+
+    def _add(self, way, d):
+        self._hop(way, d).wait_recv()
+        held = self.held.at[:, pl.ds(0, self.mine.shape[-1])]
+        copy = pltpu.make_async_copy(self.land.at[way, d], held, self.io)
         copy.start()
         copy.wait()
-
-    def _add(self, slot, src):
-        self._load(src, 2)
-        self.work[slot] = (self.work[slot].astype(F32) + self.work[2].astype(F32)).astype(BF16)
-
-    def _own(self, slot, d):
-        at = self.at
-        remote(self.mine.at[d], self.peer.at[d], self.peer_recv.at[d], self.peer_recv.at[d], (1 - at.sec, at.s, at.h)).wait_recv()
-        self._load(self.peer.at[d], 2)
-        self.work[slot] = (self.mine[d].astype(F32) + self.work[2].astype(F32)).astype(BF16)
+        self.mine[d] += held[...]
 
     def slot(self, i):
         at = self.at
+        if isinstance(i, int) and i == 0:
+            for d in range(at.nz):
+                peer = self.peer.at[d, :, pl.ds(0, self.mine.shape[-1])]
+                remote(peer, peer, self.peer_recv.at[d], self.peer_recv.at[d], (1 - at.sec, at.s, at.h)).wait_recv()
+                self.mine[d] += peer[...]
         for way in range(2):
             begun = i - at.s if way == 0 else i - (at.nz - 1 - at.s)
             d = at.nz - 1 - begun if way == 0 else begun
             earlier = at.s > 0 if way == 0 else at.s < at.nz - 1
 
             @pl.when((begun >= 0) & (i < at.nz - 1))
-            def _(way=way, d=d, begun=begun, earlier=earlier):
-                @pl.when(begun > 0)
-                def _():
-                    self._hop(way, d + 1 if way == 0 else d - 1).wait_send()
-
-                self._own(way, d)
-
+            def _(way=way, d=d, earlier=earlier):
                 @pl.when(earlier)
                 def _():
-                    self._hop(way, d).wait_recv()
-                    self._add(way, self.land.at[way, d])
+                    self._add(way, d)
 
                 self._hop(way, d).start()
 
     def last(self):
         at = self.at
+        for d in range(at.nz):
+            for way, there in ((0, at.s < d), (1, at.s > d)):
+
+                @pl.when(there)
+                def _(way=way, d=d):
+                    self._hop(way, d).wait_send()
+
+        @pl.when(at.s > 0)
+        def _():
+            self._add(0, at.s)
 
         @pl.when(at.s < at.nz - 1)
         def _():
-            self._hop(0, at.s + 1).wait_send()
-
-        @pl.when(at.s > 0)
-        def _():
-            self._hop(1, at.s - 1).wait_send()
-
-        self._own(0, at.s)
-
-        @pl.when(at.s > 0)
-        def _():
-            self._hop(0, at.s).wait_recv()
-            self._add(0, self.land.at[0, at.s])
-
-        @pl.when(at.s < at.nz - 1)
-        def _():
-            self._hop(1, at.s).wait_recv()
-            self._add(0, self.land.at[1, at.s])
+            self._add(1, at.s)
 
 
 def taker(refs):
@@ -713,7 +698,7 @@
     att_o = take(2)
     ffn_o = take(3)
     gath_n2_1, gath_g0, gath_n2_0 = take(3)
-    a_peer, a_land = take(2), take(2)
+    a_land = take(2)
     wr_o = take(3)
     mats = take(5)
     keep_s = take(SAVED)
@@ -722,7 +707,8 @@
     acc = take(3)
     wx_s = take(3)
     blk_n2, blk_g, n2t_s, gt_s = take(4)
-    a_s, work_s = take(2), take(2)
+    a_s = take(2)
+    peer_s, held_s = take(2)
     (w_sem, io_sem, keep_sem, e_send, e_recv, st_send, st_recv, head_send, head_recv, r_send, r_recv, p_send, p_recv) = take(13)
     (wx_send, wx_recv, ap_send, ap_recv, l_send, l_recv, x_send, x_recv, gz_send, gz_recv, gh_send, gh_recv) = take(12)
     x_s, n1_s, qk_s, u_s, o_s, yx_s, sin_s, gb_s, h_s, f_s, v_s = keep_s
@@ -756,7 +742,7 @@
     line = [
         [
             LineSum(
-                at, a_s[g], a_peer[g].at[layer], a_land[g].at[layer], work_s[g], io_sem.at[4],
+                at, a_s[g], peer_s, a_land[g].at[layer], held_s, io_sem.at[4],
                 l_send.at[layer, g], l_recv.at[layer, g], ap_recv.at[layer, g],
             )
             for g in range(2)
@@ -786,7 +772,7 @@
 
         chunks(w_gate.shape[0], 640, hidden)
 
-    def piece(layer, i):
+    def piece(layer, i, between=None):
         which = order(at, i)
         n2_src = (gath_n2_1 if layer == 1 else gath_n2_0).at[which]
         g_src = (gath_g1 if layer == 1 else gath_g0).at[which]
@@ -813,7 +799,13 @@
             acc[1][:, cols] += dot_nn(n2t_s[...], dv)
             acc[2][:, cols] += dot_nn(gt_s[...], t)
 
-        chunks(w_gate.shape[0], 640, hidden)
+        ff = w_gate.shape[0]
+        if between is None:
+            chunks(ff, 640, hidden)
+        else:
+            hidden(0, 640)
+            between()
+            hidden(640, ff - 640)
 
     def ffn_swap(i):
         return remote(wx_s[i], wr_o[i], wx_send.at[i], wx_recv.at[i], core)
@@ -864,7 +856,8 @@
         return g
 
     def peer_chunk(layer, g, i):
-        return remote(a_s[g].at[i], a_peer[g].at[layer, i], ap_send.at[g, i], ap_recv.at[layer, g, i], core)
+        there = peer_s.at[i, :, pl.ds(0, a_s[g].shape[-1])]
+        return remote(a_s[g].at[i], there, ap_send.at[g, i], ap_recv.at[layer, g, i], core)
 
     def mixer_grads(layer, g):
         late = 2 * qk + width
@@ -874,7 +867,7 @@
                 a_s[0][i, :, 0:width] = dot_tn(n1_s[:, cols], dcat_s[:, late:]).astype(BF16)
                 a_s[0][i, :, width:] = dot_tn(dm_s[:, cols], gb_s[...]).astype(BF16)
             else:
-                a_s[1][i] = dot_tn(n1_s[:, cols], dcat_s[:, 0:late]).astype(BF16)
+                a_s[1][i, :, 0:late] = dot_tn(n1_s[:, cols], dcat_s[:, 0:late]).astype(BF16)
 
             @pl.when(at.sec != line_core(layer, g))
             def _(i=i):
@@ -1089,14 +1082,14 @@
         owner(line_core(layer, g), lambda: line[layer][g].slot(i))
 
     def far_sum(g):
-        return remote(work_s[g].at[0], att_o[g], x_send.at[2 + g], x_recv.at[2 + g], core)
+        return remote(a_s[g].at[at.s], att_o[g], x_send.at[2 + g], x_recv.at[2 + g], core)
 
     def line_last(layer, g):
         def go():
             upward(3, nz - 1, line[layer][g].slot)
             line[layer][g].last()
             if line_core(layer, g) == layer:
-                copy = pltpu.make_async_copy(work_s[g].at[0], att_o[g], io_sem.at[8])
+                copy = pltpu.make_async_copy(a_s[g].at[at.s], att_o[g], io_sem.at[8])
                 copy.start()
                 copy.wait()
             else:
@@ -1104,14 +1097,24 @@
 
         owner(line_core(layer, g), go)
 
-    def pieces(layer, ring, begin, end):
+    def pieces(layer, ring, begin, end, between=None):
         def one(k):
             ring.ready(k - 1)
             if layer == 0:
                 ring_0.ready(k - 1)
-            piece(layer, k)
-
-        upward(begin, end, one)
+            piece(layer, k, between)
+
+        if between is None:
+            upward(begin, end, one)
+        else:
+            one(begin)
+            upward(begin + 1, end, lambda k: late_piece(layer, ring, k))
+
+    def late_piece(layer, ring, k):
+        ring.ready(k - 1)
+        if layer == 0:
+            ring_0.ready(k - 1)
+        piece(layer, k)
 
     def spread(ring):
         upward(3, nz, ring.step)
@@ -1140,8 +1143,8 @@
         mixer_grads(1, 0)
 
     def b1_rs2():
+        slot(1, 0, 0)
         mixer_grads(1, 1)
-        slot(1, 0, 0)
         pieces(1, ring_n, 2, 3)
 
     def b1_ag2():
@@ -1181,9 +1184,10 @@
         ring_g.step(2)
         pieces(0, ring_g, 1, 2)
         slot(1, 1, 2)
+        line_last(1, 0)
 
     def b0_local():
-        line_last(1, 0)
+        owner(0, lambda: far_sum(0).wait_send())
         mixer_sent(1, 0)
         mixer_grads(0, 0)
 
@@ -1191,20 +1195,22 @@
         line_last(1, 1)
 
     def b0_rs2():
+        slot(0, 0, 0)
         mixer_sent(1, 1)
         mixer_grads(0, 1)
-        owner(0, lambda: far_sum(0).wait_send())
-        slot(0, 0, 0)
-        pieces(0, ring_g, 2, 3)
+        pieces(0, ring_g, 2, 3, lambda: slot(0, 1, 0))
         slot(0, 0, 1)
-        slot(0, 1, 0)
 
     def b0_ag2():
         gain_swap.start()
-        pieces(0, ring_g, 3, nz)
+
+        def between():
+            slot(0, 1, 1)
+            slot(0, 0, 2)
+
+        pieces(0, ring_g, 3, nz, between)
         ffn_send(0)
-        slot(0, 0, 2)
-        slot(0, 1, 1)
+        slot(0, 1, 2)
         gain_swap.wait_recv()
         gtot_s[0] = gsum_s[at.sec] + gpeer_s[...]
         for k in range(1, nz):
@@ -1218,7 +1224,6 @@
         ),
     )
 
-    slot(0, 1, 2)
     line_last(0, 0)
     for k in range(1, nz):
         gain_seq(k).wait_recv()
@@ -1266,16 +1271,20 @@
 
 def final_kernel(qk, width, *refs):
     take = taker(refs)
-    whole, far, (early, late), out, parts, held, held_far, (sems,) = take(5), take(3), take(2), take(5), take(5), take(5), take(3), take(1)
+    whole, far, (early, late, gains), out, parts = take(5), take(3), take(3), take(5), take(8)
+    held, held_far, (sems,) = take(5), take(3), take(1)
     loads = [pltpu.make_async_copy(a, b, sems.at[i]) for i, (a, b) in enumerate(zip(whole + far, held + held_far))]
     stores = [pltpu.make_async_copy(a, b, sems.at[8 + i]) for i, (a, b) in enumerate(zip(held, out))]
     for copy in loads:
         copy.start()
-    g_q, g_k, g_v, g_o, g_out = parts
+    g_q, g_k, g_v, g_o, g_out, g_attn, g_ffn, g_conv = parts
+    g_attn[...] = gains[0:1]
+    g_ffn[...] = gains[1:2]
+    g_conv[...] = gains[2 : 2 + KW, 0:width]
     turned = late[:, 0 : 2 * qk].astype(F32).T
     g_q[...] = turned[0:qk]
     g_k[...] = turned[qk : 2 * qk]
-    g_v[...] = late[:, 2 * qk :].astype(F32)
+    g_v[...] = late[:, 2 * qk : 2 * qk + width].astype(F32)
     g_o[...] = early[:, 0:width].astype(F32)
     g_out[...] = early[:, width:].astype(F32).T
     for i in range(5):
@@ -1309,7 +1318,7 @@
     part, block = rows // nh, d // nz
     dims = (nz, nh, rows, heads)
     wide = -(-((heads - 1) * HD + LANES) // LANES) * LANES
-    groups = (2 * width, 2 * qk + width)
+    groups = (2 * width, -(-(2 * qk + width) // LANES) * LANES)
     tables = jnp.asarray(lift_tables(heads), BF16)
     turned = [jnp.swapaxes(w, 1, 2) for w in (w_query, w_key, w_value, w_output_gate)]
     own = (*turned, w_out, jnp.swapaxes(w_gate, 1, 2), jnp.swapaxes(w_up, 1, 2), w_down)
@@ -1404,7 +1413,6 @@
         + [shape((block, g)) for g in groups]
         + [shape((block, ff), F32)] * 3
         + [gathered, gathered, gathered]
-        + [shape((2, nz, block, g)) for g in groups]
         + [shape((2, 2, nz, block, g)) for g in groups]
         + [shape((block, ff))] * 3
     )
@@ -1442,7 +1450,7 @@
         + [vm((block, ff))] * 3
         + [act, act, vm((block, rows)), vm((block, rows))]
         + [vm((nz, block, g)) for g in groups]
-        + [vm((3, block, g)) for g in groups]
+        + [vm((nz, block, max(groups))), vm((block, max(groups)))]
         + [
             DMA((8,)),
             DMA((12,)),
@@ -1493,25 +1501,28 @@
         shape((block, width), F32),
         shape((block, width), F32),
         shape((width, block), F32),
+        shape((1, d), F32),
+        shape((1, d), F32),
+        shape((KW, width), F32),
     ]
-    section_out, input_grad, g_gate, g_up, g_down, g_q, g_k, g_v, g_o, g_out = pl.pallas_call(
+    section_out, input_grad, g_gate, g_up, g_down, g_q, g_k, g_v, g_o, g_out, g_attn, g_ffn, g_conv = pl.pallas_call(
         functools.partial(final_kernel, qk, width),
         out_shape=finals,
-        in_specs=[ANY] * 8 + [VM] * 2,
-        out_specs=[ANY] * 5 + [VM] * 5,
+        in_specs=[ANY] * 8 + [VM] * 3,
+        out_specs=[ANY] * 5 + [VM] * 8,
         scratch_shapes=[vm((micro, rows, d))] * 2 + [vm((block, ff), F32)] * 3 + [vm((block, ff))] * 3 + [DMA((13,))],
         compiler_params=pltpu.CompilerParams(vmem_limit_bytes=VMEM_LIMIT),
-    )(section_out, input_grad, g_gate, g_up, g_down, *far, att_early, att_late)
+    )(section_out, input_grad, g_gate, g_up, g_down, *far, att_early, att_late, gains)
     return (
         section_out[None],
         input_grad[None],
-        gains[0:1],
-        gains[1:2],
+        g_attn,
+        g_ffn,
         g_q.T[None],
         g_k.T[None],
         g_v[None],
         g_o[None],
-        gains[None, 2 : 2 + KW, :width],
+        g_conv[None],
         g_out[None],
         g_gate[None],
         g_up[None],

time: 397 us -> 392 us (0.987)
  no operation moved by 1% of the time
where the time goes in v6:
time: 392 us; the launch traced here: 387 us
  Pallas kernels  382 us (97%)
    pallas_call x1, Pallas kernels, shards(): pl.pallas_call(functools.partial(bwd_kernel, dims), out_shape=outs, in_sp...  228 us
    pallas_call x1, Pallas kernels, shards(): pl.pallas_call(functools.partial(fwd_kernel, dims), out_shape=outs, in_sp...  142 us
    pallas_call x1, Pallas kernels, shards(): pl.pallas_call(functools.partial(final_kernel, qk, width), out_shape=fina...  11.8 us

profile of v6, /device:TPU:0, one launch (start us, length us, event | category | flops | bytes accessed | tf_op | source)
XLA Modules:
  0.0 386.7 jit_solution(15578124346794208887)
XLA Ops:
  0.7 0.1 pad.8.clone
  0.7 0.7 copy.32
  1.4 1.4 fusion.refs_3_.refs_2_
  2.8 142.1 %shard_map.246 = (f32[8,1792]{1,0:T(8,128)}, bf16[1,64,1792]{2,1,0:T(8,128)(2,1)}, bf16[1,64,1792]{2,1,0:T(8,128)(2,1)}, bf16[1,448,1792]{2,1,0:T(8,128)(2,1)}, ...) custom-call(s32[2,2]{1,0:T(2,128)} %refs_0_.3, ...), custom_call_target="tpu_custom_call" | custom-call | tf_op jit(solution)/shard_map/pallas_call | solution.py:1399
  144.9 228.2 %shard_map.247 = (bf16[2,256,1792]{2,1,0:T(8,128)(2,1)}, f32[8,1792]{1,0:T(8,128)}, bf16[448,896]{1,0:T(8,128)(2,1)}, bf16[448,640]{1,0:T(8,128)(2,1)}, f32[448,...) custom-call(s32[2,2]{1,0:T(2,128)} %refs_0_.3, ...), custom_call_target="tpu_custom_call", output_to_operand_aliasing={{9}: (44, {})} | custom-call | tf_op jit(solution)/shard_map/pallas_call | solution.py:1482
  373.1 11.8 %shard_map.248 = (bf16[2,256,1792]{2,1,0:T(8,128)(2,1)}, bf16[2,256,1792]{2,1,0:T(8,128)(2,1)}, f32[448,1216]{1,0:T(8,128)}, f32[448,1216]{1,0:T(8,128)}, f32[44...) custom-call(bf16[2,256,1792]{2,1,0:T(8,128)(2,1)} %get-tuple-element, ...), custom_call_target="tpu_custom_call" | custom-call | tf_op jit(solution)/shard_map/pallas_call | solution.py:1508
  384.9 1.3 copy.29
  (1 shorter events, 0.0 us)

commit v7 on v6

--- a/solution.py
+++ b/solution.py
@@ -758,10 +758,11 @@
                 n2t_s[...] = n2_ref[:, part * block : (part + 1) * block].T
                 gt_s[...] = g_ref[:, part * block : (part + 1) * block].T
 
+    def own_fetch(layer):
+        return pltpu.make_async_copy(n2_1 if layer == 1 else gath_n2_0.at[at.s], blk_n2, io_sem.at[0])
+
     def own_piece(layer):
-        copy = pltpu.make_async_copy(n2_1 if layer == 1 else gath_n2_0.at[at.s], blk_n2, io_sem.at[0])
-        copy.start()
-        copy.wait()
+        own_fetch(layer).wait()
         turn_blocks(blk_n2, grad_s)
 
         def hidden(at_col, size):
@@ -772,14 +773,22 @@
 
         chunks(w_gate.shape[0], 640, hidden)
 
-    def piece(layer, i, between=None):
+    def fetch(layer, i):
         which = order(at, i)
         n2_src = (gath_n2_1 if layer == 1 else gath_n2_0).at[which]
         g_src = (gath_g1 if layer == 1 else gath_g0).at[which]
-        loads = [pltpu.make_async_copy(n2_src, blk_n2, io_sem.at[0]), pltpu.make_async_copy(g_src, blk_g, io_sem.at[1])]
-        for copy in loads:
+        return pltpu.make_async_copy(n2_src, blk_n2, io_sem.at[0]), pltpu.make_async_copy(g_src, blk_g, io_sem.at[1])
+
+    def prefetch(layer, ring, k):
+        ring.ready(k - 1)
+        if layer == 0:
+            ring_0.ready(k - 1)
+        for copy in fetch(layer, k):
             copy.start()
-        for copy in loads:
+
+    def piece(layer, i, between=None):
+        which = order(at, i)
+        for copy in fetch(layer, i):
             copy.wait()
         pos = which * rows + lax.broadcasted_iota(jnp.int32, (rows, 1), 0)
         blk_g[...] = jnp.where(pos < at.tot, blk_g[...].astype(F32), 0.0).astype(BF16)
@@ -962,6 +971,7 @@
             def _(k=k):
                 state(k).start()
 
+        hooks["sent"]()
         da_s[...] = jnp.zeros_like(da_s)
         db_s[...] = jnp.zeros_like(db_s)
         for head in range(heads):
@@ -1073,6 +1083,7 @@
         weight_start(1, i)
     for i in (9, 10, 8, 3, 2, 4, 5, 6, 7, 1, 0):
         keep_copy(1, i).start()
+    own_fetch(1).start()
     at.barrier(True, True, True)
     ring_n.step(0)
     g_copy.wait()
@@ -1098,23 +1109,13 @@
         owner(line_core(layer, g), go)
 
     def pieces(layer, ring, begin, end, between=None):
+        piece(layer, begin, between)
+
         def one(k):
-            ring.ready(k - 1)
-            if layer == 0:
-                ring_0.ready(k - 1)
-            piece(layer, k, between)
-
-        if between is None:
-            upward(begin, end, one)
-        else:
-            one(begin)
-            upward(begin + 1, end, lambda k: late_piece(layer, ring, k))
-
-    def late_piece(layer, ring, k):
-        ring.ready(k - 1)
-        if layer == 0:
-            ring_0.ready(k - 1)
-        piece(layer, k)
+            prefetch(layer, ring, k)
+            piece(layer, k)
+
+        upward(begin + 1, end, one)
 
     def spread(ring):
         upward(3, nz, ring.step)
@@ -1136,33 +1137,36 @@
 
     def b1_ag1():
         ring_n.step(2)
+        prefetch(1, ring_n, 1)
         pieces(1, ring_n, 1, 2)
 
-    def b1_local():
+    def b1_sent():
         upward(0, nz - 1, ring_0.pair)
         mixer_grads(1, 0)
 
     def b1_rs2():
-        slot(1, 0, 0)
+        slot(1, 0, 1)
         mixer_grads(1, 1)
         pieces(1, ring_n, 2, 3)
+        prefetch(1, ring_n, 3)
+        slot(1, 0, 2)
 
     def b1_ag2():
         for i in (4, 0, 1, 2, 3):
             weight_start(0, i)
         for i in (9, 10, 8, 3, 2, 4, 5, 6, 7, 1, 0):
             keep_copy(0, i).start()
-        slot(1, 0, 1)
-        pieces(1, ring_n, 3, nz)
+        pieces(1, ring_n, 3, nz, lambda: slot(1, 1, 0))
         for i in (7, 5, 6):
             weight_start(0, i)
+        own_fetch(0).start()
         ffn_send(1)
 
     finish_1 = layer_backward(
         1,
         dict(
-            begin=nothing, rs1=b1_rs1, ag1=b1_ag1, dm=lambda: spread(ring_n), local=b1_local,
-            states=nothing, rs2=b1_rs2, ag2=b1_ag2,
+            begin=nothing, rs1=b1_rs1, ag1=b1_ag1, dm=lambda: spread(ring_n), sent=b1_sent, local=lambda: slot(1, 0, 0),
+            states=lambda: prefetch(1, ring_n, 2), rs2=b1_rs2, ag2=b1_ag2,
         ),
     )
     finish_1()
@@ -1170,47 +1174,41 @@
 
     def b0_begin():
         ring_g.step(0)
-        slot(1, 0, 2)
-        slot(1, 1, 0)
+        slot(1, 1, 1)
 
     def b0_rs1():
         ffn_done(1)
         own_piece(0)
         ring_g.step(1)
         ring_g.pair(0)
-        slot(1, 1, 1)
+        line_last(1, 0)
+        slot(1, 1, 2)
 
     def b0_ag1():
         ring_g.step(2)
+        prefetch(0, ring_g, 1)
         pieces(0, ring_g, 1, 2)
-        slot(1, 1, 2)
-        line_last(1, 0)
-
-    def b0_local():
+        line_last(1, 1)
+
+    def b0_sent():
         owner(0, lambda: far_sum(0).wait_send())
         mixer_sent(1, 0)
         mixer_grads(0, 0)
 
-    def b0_states():
-        line_last(1, 1)
-
     def b0_rs2():
-        slot(0, 0, 0)
+        slot(0, 0, 1)
         mixer_sent(1, 1)
         mixer_grads(0, 1)
         pieces(0, ring_g, 2, 3, lambda: slot(0, 1, 0))
-        slot(0, 0, 1)
+        prefetch(0, ring_g, 3)
+        slot(0, 0, 2)
 
     def b0_ag2():
         gain_swap.start()
-
-        def between():
-            slot(0, 1, 1)
-            slot(0, 0, 2)
-
-        pieces(0, ring_g, 3, nz, between)
+        pieces(0, ring_g, 3, nz, lambda: slot(0, 1, 1))
         ffn_send(0)
         slot(0, 1, 2)
+        line_last(0, 0)
         gain_swap.wait_recv()
         gtot_s[0] = gsum_s[at.sec] + gpeer_s[...]
         for k in range(1, nz):
@@ -1219,12 +1217,11 @@
     finish_0 = layer_backward(
         0,
         dict(
-            begin=b0_begin, rs1=b0_rs1, ag1=b0_ag1, dm=lambda: spread(ring_g), local=b0_local,
-            states=b0_states, rs2=b0_rs2, ag2=b0_ag2,
+            begin=b0_begin, rs1=b0_rs1, ag1=b0_ag1, dm=lambda: spread(ring_g), sent=b0_sent, local=lambda: slot(0, 0, 0),
+            states=lambda: prefetch(0, ring_g, 2), rs2=b0_rs2, ag2=b0_ag2,
         ),
     )
 
-    line_last(0, 0)
     for k in range(1, nz):
         gain_seq(k).wait_recv()
     total = gtot_s[0]

time: 392 us -> 377 us (0.962)
  Pallas kernels: 382 us -> 367 us
    pallas_call x1, Pallas kernels: 228 us -> 214 us  [shards(): pl.pallas_call(functools.partial(bwd_kernel, dims), out_shape=outs, in_sp...]
where the time goes in v7:
time: 377 us; the launch traced here: 372 us
  Pallas kernels  367 us (97%)
    pallas_call x1, Pallas kernels, shards(): pl.pallas_call(functools.partial(bwd_kernel, dims), out_shape=outs, in_sp...  214 us
    pallas_call x1, Pallas kernels, shards(): pl.pallas_call(functools.partial(fwd_kernel, dims), out_shape=outs, in_sp...  142 us
    pallas_call x1, Pallas kernels, shards(): pl.pallas_call(functools.partial(final_kernel, qk, width), out_shape=fina...  11.8 us

profile of v7, /device:TPU:0, one launch (start us, length us, event | category | flops | bytes accessed | tf_op | source)
XLA Modules:
  0.0 372.1 jit_solution(8960613307973288449)
XLA Ops:
  0.7 0.1 pad.8.clone
  0.7 0.7 copy.32
  1.4 1.4 fusion.refs_3_.refs_2_
  2.8 142.1 %shard_map.246 = (f32[8,1792]{1,0:T(8,128)}, bf16[1,64,1792]{2,1,0:T(8,128)(2,1)}, bf16[1,64,1792]{2,1,0:T(8,128)(2,1)}, bf16[1,448,1792]{2,1,0:T(8,128)(2,1)}, ...) custom-call(s32[2,2]{1,0:T(2,128)} %refs_0_.3, ...), custom_call_target="tpu_custom_call" | custom-call | tf_op jit(solution)/shard_map/pallas_call | solution.py:1396
  144.9 213.6 %shard_map.247 = (bf16[2,256,1792]{2,1,0:T(8,128)(2,1)}, f32[8,1792]{1,0:T(8,128)}, bf16[448,896]{1,0:T(8,128)(2,1)}, bf16[448,640]{1,0:T(8,128)(2,1)}, f32[448,...) custom-call(s32[2,2]{1,0:T(2,128)} %refs_0_.3, ...), custom_call_target="tpu_custom_call", output_to_operand_aliasing={{9}: (44, {})} | custom-call | tf_op jit(solution)/shard_map/pallas_call | solution.py:1479
  358.5 11.8 %shard_map.248 = (bf16[2,256,1792]{2,1,0:T(8,128)(2,1)}, bf16[2,256,1792]{2,1,0:T(8,128)(2,1)}, f32[448,1216]{1,0:T(8,128)}, f32[448,1216]{1,0:T(8,128)}, f32[44...) custom-call(bf16[2,256,1792]{2,1,0:T(8,128)(2,1)} %get-tuple-element, ...), custom_call_target="tpu_custom_call" | custom-call | tf_op jit(solution)/shard_map/pallas_call | solution.py:1505
  370.3 1.3 copy.29
  (1 shorter events, 0.0 us)

commit v8 on v7

--- a/solution.py
+++ b/solution.py
@@ -451,15 +451,19 @@
     small_copy.start()
     small_copy.wait()
 
+    def arrived(layer, i):
+        @pl.when(at.sec != layer)
+        def _():
+            swap(layer, i).wait_recv()
+            stash(layer, i).start()
+
     def wait_weight(layer, i):
         @pl.when(at.sec == layer)
         def _():
             local(layer, i).wait()
 
-        @pl.when(at.sec != layer)
-        def _():
-            swap(layer, i).wait_recv()
-            stash(layer, i).start()
+        if layer == 1:
+            arrived(layer, i)
 
     allowed = at.allowed()
     applies, tail, prior = at.applies(), at.tail(), at.prior_seg(at.s)
@@ -638,6 +642,8 @@
         n2_last.start()
         ring_n.step(2)
 
+    for i in (2, 0, 1, 3, 4, 5, 6, 7):
+        arrived(0, i)
     x_copy.wait()
     finish_0 = layer_forward(
         0, x_s, dict(begin=nothing, states=nothing, rs1=lambda: ring_g.step(0), ag1=nothing, n2=f0_n2, rs2=nothing, ag2=lambda: ring_g.step(2))
@@ -912,6 +918,7 @@
         chunks(df_s.shape[1], 256, down_chunk)
         weight_wait(5)
         weight_wait(6)
+        hooks["loads"]()
 
         s1 = []
         for half in range(2):
@@ -1079,13 +1086,13 @@
 
     g_copy = pltpu.make_async_copy(inputs_grad.at[at.sec], grad_s, io_sem.at[2])
     g_copy.start()
-    for i in (7, 5, 6, 4, 0, 1, 2, 3):
-        weight_start(1, i)
-    for i in (9, 10, 8, 3, 2, 4, 5, 6, 7, 1, 0):
+    weight_start(1, 7)
+    for i in (9, 10):
         keep_copy(1, i).start()
-    own_fetch(1).start()
     at.barrier(True, True, True)
     ring_n.step(0)
+    for i in (5, 6):
+        weight_start(1, i)
     g_copy.wait()
     grad_s[...] = jnp.where(valid, grad_s[...].astype(F32), 0.0).astype(BF16)
 
@@ -1130,6 +1137,13 @@
         to = lax.rem(at.s + k, nz)
         return remote(gtot_s.at[0], gz_s.at[k - 1], gz_send.at[k - 1], gz_recv.at[k - 1], (at.sec, to, at.h))
 
+    def b1_loads():
+        own_fetch(1).start()
+        for i in (8, 3, 2, 4, 5, 6, 7, 1, 0):
+            keep_copy(1, i).start()
+        for i in (4, 0, 1, 2, 3):
+            weight_start(1, i)
+
     def b1_rs1():
         own_piece(1)
         ring_n.step(1)
@@ -1157,15 +1171,16 @@
         for i in (9, 10, 8, 3, 2, 4, 5, 6, 7, 1, 0):
             keep_copy(0, i).start()
         pieces(1, ring_n, 3, nz, lambda: slot(1, 1, 0))
-        for i in (7, 5, 6):
+        weight_start(0, 7)
+        ffn_send(1)
+        for i in (5, 6):
             weight_start(0, i)
         own_fetch(0).start()
-        ffn_send(1)
 
     finish_1 = layer_backward(
         1,
         dict(
-            begin=nothing, rs1=b1_rs1, ag1=b1_ag1, dm=lambda: spread(ring_n), sent=b1_sent, local=lambda: slot(1, 0, 0),
+            begin=nothing, loads=b1_loads, rs1=b1_rs1, ag1=b1_ag1, dm=lambda: spread(ring_n), sent=b1_sent, local=lambda: slot(1, 0, 0),
             states=lambda: prefetch(1, ring_n, 2), rs2=b1_rs2, ag2=b1_ag2,
         ),
     )
@@ -1217,7 +1232,7 @@
     finish_0 = layer_backward(
         0,
         dict(
-            begin=b0_begin, rs1=b0_rs1, ag1=b0_ag1, dm=lambda: spread(ring_g), sent=b0_sent, local=lambda: slot(0, 0, 0),
+            begin=b0_begin, loads=nothing, rs1=b0_rs1, ag1=b0_ag1, dm=lambda: spread(ring_g), sent=b0_sent, local=lambda: slot(0, 0, 0),
             states=lambda: prefetch(0, ring_g, 2), rs2=b0_rs2, ag2=b0_ag2,
         ),
     )

time: 377 us -> 375 us (level)
    pallas_call x1, Pallas kernels: 142 us -> 122 us  [shards(): pl.pallas_call(functools.partial(fwd_kernel, dims), out_shape=outs, in_sp...]
    pallas_call x1, Pallas kernels: 214 us -> 231 us  [shards(): pl.pallas_call(functools.partial(bwd_kernel, dims), out_shape=outs, in_sp...]
where the time goes in v8:
time: 375 us; the launch traced here: 370 us
  Pallas kernels  365 us (97%)
    pallas_call x1, Pallas kernels, shards(): pl.pallas_call(functools.partial(bwd_kernel, dims), out_shape=outs, in_sp...  231 us
    pallas_call x1, Pallas kernels, shards(): pl.pallas_call(functools.partial(fwd_kernel, dims), out_shape=outs, in_sp...  122 us
    pallas_call x1, Pallas kernels, shards(): pl.pallas_call(functools.partial(final_kernel, qk, width), out_shape=fina...  11.8 us

profile of v8, /device:TPU:0, one launch (start us, length us, event | category | flops | bytes accessed | tf_op | source)
XLA Modules:
  0.0 369.7 jit_solution(813178466324718477)
XLA Ops:
  0.7 0.1 pad.8.clone
  0.7 0.7 copy.32
  1.4 1.4 fusion.refs_3_.refs_2_
  2.8 122.3 %shard_map.246 = (f32[8,1792]{1,0:T(8,128)}, bf16[1,64,1792]{2,1,0:T(8,128)(2,1)}, bf16[1,64,1792]{2,1,0:T(8,128)(2,1)}, bf16[1,448,1792]{2,1,0:T(8,128)(2,1)}, ...) custom-call(s32[2,2]{1,0:T(2,128)} %refs_0_.3, ...), custom_call_target="tpu_custom_call" | custom-call | tf_op jit(solution)/shard_map/pallas_call | solution.py:1411
  125.1 231.0 %shard_map.247 = (bf16[2,256,1792]{2,1,0:T(8,128)(2,1)}, f32[8,1792]{1,0:T(8,128)}, bf16[448,896]{1,0:T(8,128)(2,1)}, bf16[448,640]{1,0:T(8,128)(2,1)}, f32[448,...) custom-call(s32[2,2]{1,0:T(2,128)} %refs_0_.3, ...), custom_call_target="tpu_custom_call", output_to_operand_aliasing={{9}: (44, {})} | custom-call | tf_op jit(solution)/shard_map/pallas_call | solution.py:1494
  356.2 11.8 %shard_map.248 = (bf16[2,256,1792]{2,1,0:T(8,128)(2,1)}, bf16[2,256,1792]{2,1,0:T(8,128)(2,1)}, f32[448,1216]{1,0:T(8,128)}, f32[448,1216]{1,0:T(8,128)}, f32[44...) custom-call(bf16[2,256,1792]{2,1,0:T(8,128)(2,1)} %get-tuple-element, ...), custom_call_target="tpu_custom_call" | custom-call | tf_op jit(solution)/shard_map/pallas_call | solution.py:1520
  368.0 1.3 copy.29
  (1 shorter events, 0.0 us)
